TPU v7x, 32 devices: a whole 2x2x4 slice. The times are simulated.
32 devices in a mesh: row: 4 (over y, x), col: 8 (over z, core).
Axes of the slice: x: 2, y: 2, z: 4, core: 2. Of those that a mesh axis runs over, the one named last changes fastest.
Arguments:
- three_center: bfloat16 [4096, 6144], P(('row', 'col')), may hold values from -6 to 6
- density: bfloat16 [4096, 4096], P('row', 'col'), may hold values from -0.1875 to 0.1875
- block_mask: int32 [128, 48], P(('row', 'col')), may hold values 0 or 1
- density_mask: int32 [128, 128], P('row', 'col'), may hold values 0 or 1
- basis_count: int32 [128], replicated, may hold values from 8 to 32
- ri_count: int32 [48], replicated, may hold values from 16 to 128
Outputs:
- contracted: bfloat16 [4096, 6144], P('row', 'col')
All inputs are finite; a program needn't handle non-finite values. No bound on the sum of `block_mask` or of `density_mask` on one device may be relied on, other than what follows from the above.
Results may differ from a plain program's by a relative error of at most 0.001.
Values may be sent and summed in bfloat16 or wider, within the bound.
No kernel may reach another device: no remote copies, remote signals or barrier semaphores. Data moves between devices by JAX's collectives and lax.ppermute only.
A program may use at most 64 MiB of HBM per device.

v0:
```python
import jax
import jax.numpy as jnp
from jax import lax
from jax.experimental import pallas as pl
from jax.experimental.pallas import tpu as pltpu
from jax.sharding import PartitionSpec as P

BW = 32
RW = 128
CORES = 2
VMEM = 48 * 1024 * 1024
TILE = 256
BF16 = jnp.bfloat16
F32 = jnp.float32
SMEM_SPEC = pl.BlockSpec(memory_space=pltpu.SMEM)
VMEM_SPEC = pl.BlockSpec(memory_space=pltpu.VMEM)
ANY_SPEC = pl.BlockSpec(memory_space=pl.ANY)


def params(limit=VMEM):
    return pltpu.CompilerParams(vmem_limit_bytes=limit)


def cost(flops, bytes_accessed):
    return pl.CostEstimate(flops=flops, bytes_accessed=bytes_accessed, transcendentals=0)


def ones_where(cond):
    return jnp.where(cond, 1.0, 0.0).astype(BF16)


def iota(shape, axis):
    return lax.broadcasted_iota(jnp.int32, shape, axis)


def loop(n, unroll):
    def run(f):
        if unroll:
            for i in range(n):
                f(i)
        else:
            pl.loop(0, n)(f)

    return run


def span(i, size):
    return pl.ds(i * size if isinstance(i, int) else pl.multiple_of(i * size, size), size)


def place_row(count_ref, base, atoms, width):
    lane = iota((1, atoms * width), 1)

    def atom(a, carry):
        place, offset = carry
        count = count_ref[base + a]
        inside = (lane >= a * width) & (lane < a * width + count)
        return jnp.where(inside, lane - a * width + offset, place), offset + count

    return lax.fori_loop(0, atoms, atom, (jnp.full(lane.shape, -1, jnp.int32), jnp.int32(0)))[0]


def pack_rows(count_ref, base, atoms, width, size):
    place = place_row(count_ref, base, atoms, width)
    return ones_where(iota((size, atoms * width), 0) == place)


def pack_cols(count_ref, base, atoms, width, size, out, unroll):
    def atom(a, offset):
        count = count_ref[base + a]
        slot = iota((width, size), 0)
        gap = iota((width, size), 1) - slot
        out[span(a, width), :] = ones_where((gap == offset) & (slot < count))
        return offset + count

    if unroll:
        offset = jnp.int32(0)
        for a in range(atoms):
            offset = atom(a, offset)
    else:
        lax.fori_loop(0, atoms, atom, jnp.int32(0))


def first_fit(basis_count, ri_count, groups, levels):
    def body(count_ref, ri_ref, o_ref):
        level = jnp.int32(0)
        for axis, (ref, parts) in enumerate(zip((count_ref, count_ref, ri_ref), groups)):
            per = ref.shape[0] // parts
            most = jnp.int32(0)
            for g in range(parts):
                total = jnp.int32(0)
                for i in range(per):
                    total = total + ref[g * per + i]
                most = jnp.maximum(most, total)
            for n, sizes in enumerate(levels[:-1]):
                level = jnp.where(most > sizes[axis], jnp.maximum(level, n + 1), level)
        o_ref[0] = level

    return pl.pallas_call(
        body,
        out_shape=jax.ShapeDtypeStruct((1,), jnp.int32),
        in_specs=[SMEM_SPEC, SMEM_SPEC],
        out_specs=SMEM_SPEC,
        name="first_fit",
    )(basis_count, ri_count)


def pack_integrals(tc, block_mask, basis_count, ri_count, ncols, packed, unroll, arrived=None):
    rows, cols = tc.shape
    atoms = rows // BW
    wide = cols // ncols
    blocks = wide // RW
    chips = ncols // CORES
    first = arrived is None

    def body(count_ref, ri_ref, mask_ref, x_ref, *refs):
        outs = refs[:1] if first else refs[1 : 1 + chips]
        held, hot = refs[-2:] if first else refs[-3:-1]
        made = outs[0] if first else refs[-1]
        row, col = lax.axis_index("row"), lax.axis_index("col")
        base = (row * ncols + col) * atoms

        @loop(chips, unroll)
        def _(t):
            dest = col ^ (CORES * t + (1 if first else 0))

            @loop(blocks, unroll)
            def _(b):
                lanes = pl.ds(pl.multiple_of(dest * wide + b * RW, RW), RW)
                slot = iota((BW, RW), 0)
                for a in range(atoms):
                    limit = jnp.where(mask_ref[a, dest * blocks + b] > 0, count_ref[base + a], 0)
                    x = x_ref[pl.ds(a * BW, BW), lanes].astype(F32)
                    held[pl.ds(a * BW, BW), span(b, RW)] = jnp.where(slot < limit, x, 0.0).astype(BF16)

            pack_cols(ri_ref, dest * blocks, blocks, RW, packed, hot, unroll)
            made[t] = jnp.dot(held[...], hot[...], preferred_element_type=F32).astype(BF16)

        if not first:
            core = lax.rem(col, CORES)
            for t in range(chips):
                outs[t][pl.ds(pl.multiple_of(core * rows, rows), rows), :] = made[t]
                outs[t][pl.ds(pl.multiple_of((1 - core) * rows, rows), rows), :] = refs[0][t]

    shape = (chips, rows, packed)
    merged = jax.ShapeDtypeStruct((CORES * rows, packed), BF16)
    out_shape = [jax.ShapeDtypeStruct(shape, BF16)] if first else [merged] * chips
    out_specs = [VMEM_SPEC] * len(out_shape)
    return pl.pallas_call(
        body,
        out_shape=out_shape,
        in_specs=[SMEM_SPEC, SMEM_SPEC, SMEM_SPEC] + [VMEM_SPEC] * (1 if first else 2),
        out_specs=out_specs,
        scratch_shapes=[pltpu.VMEM((rows, wide), BF16), pltpu.VMEM((wide, packed), BF16)]
        + ([] if first else [pltpu.VMEM(shape, BF16)]),
        compiler_params=params(),
        cost_estimate=cost(rows * cols * packed, rows * cols + 3 * chips * rows * packed),
        name="pack_other_core" if first else "pack_own_core",
    )(basis_count, ri_count, block_mask, tc, *([] if first else [arrived]))


def pack_density(dens, mask, basis_count, lam_size, sum_size, unroll):
    rows, cols = dens.shape
    lam_atoms, sum_atoms = mask.shape
    steps = 1 if unroll else 4
    tile = rows // steps
    out_tile = lam_size // steps

    def body(count_ref, mask_ref, x_ref, o_ref, upper_ref, lower_ref, hot, keep, mid):
        row, col = lax.axis_index("row"), lax.axis_index("col")
        first = iota((sum_atoms, cols), 0) * BW
        lane = iota((sum_atoms, cols), 1)
        of_atom = ones_where((lane >= first) & (lane < first + BW))
        keep[...] = jnp.dot(ones_where(mask_ref[...] > 0), of_atom, preferred_element_type=F32).astype(BF16)
        pack_cols(count_ref, col * sum_atoms, sum_atoms, BW, sum_size, hot, unroll)

        @loop(steps, unroll)
        def _(i):
            at = span(i, tile)
            shape = (tile, lam_atoms)
            first = iota(shape, 1) * BW - i * tile
            atom = ones_where((iota(shape, 0) >= first) & (iota(shape, 0) < first + BW))
            kept = jnp.dot(atom, keep[...], preferred_element_type=F32)
            x = jnp.where(kept > 0.5, x_ref[at, :].astype(F32), 0.0).astype(BF16)
            mid[at, :] = jnp.dot(x, hot[...], preferred_element_type=F32).astype(BF16)

        place = place_row(count_ref, row * lam_atoms, lam_atoms, BW)

        @loop(steps, unroll)
        def _(i):
            at = span(i, out_tile)
            left = ones_where(iota((out_tile, rows), 0) + i * out_tile == place)
            o_ref[at, :] = jnp.dot(left, mid[...], preferred_element_type=F32).astype(BF16)

        upper_ref[...] = o_ref[pl.ds(0, TILE), :]
        lower_ref[...] = o_ref[pl.ds(TILE, lam_size - TILE), :]

    return pl.pallas_call(
        body,
        out_shape=[jax.ShapeDtypeStruct((n, sum_size), BF16) for n in (lam_size, TILE, lam_size - TILE)],
        in_specs=[SMEM_SPEC, VMEM_SPEC, VMEM_SPEC],
        out_specs=[VMEM_SPEC] * 3,
        scratch_shapes=[
            pltpu.VMEM((cols, sum_size), BF16),
            pltpu.VMEM((lam_atoms, cols), BF16),
            pltpu.VMEM((rows, sum_size), BF16),
        ],
        compiler_params=params(),
        cost_estimate=cost(2 * rows * sum_size * (cols + lam_size), 2 * rows * cols),
        name="pack_density",
    )(basis_count, mask, dens)


def pack_part(pieces, basis_count, first, ncols, size):
    rows, cols = pieces[0].shape
    per = len(pieces)
    depth = per * rows
    atoms = depth // BW

    def body(count_ref, *refs):
        blocks, o_ref, full = refs[:per], refs[per], refs[per + 1]
        row, chip = lax.axis_index("row"), lax.axis_index("col") // CORES
        for i in range(per):
            at = lax.rem(chip ^ (first + i), per) * rows
            full[pl.ds(pl.multiple_of(at, rows), rows), :] = blocks[i][...]
        part = (row * (ncols // CORES) + (chip ^ first)) * rows // depth
        hot = pack_rows(count_ref, part * atoms, atoms, BW, size)
        o_ref[...] = jnp.dot(hot, full[...], preferred_element_type=F32).astype(BF16)

    return pl.pallas_call(
        body,
        out_shape=jax.ShapeDtypeStruct((size, cols), BF16),
        in_specs=[SMEM_SPEC] + [VMEM_SPEC] * per,
        out_specs=VMEM_SPEC,
        scratch_shapes=[pltpu.VMEM((depth, cols), BF16)],
        compiler_params=params(),
        cost_estimate=cost((2 + 40 * first) * size * depth * cols, 2 * cols * (depth + size)),
        name="pack_part",
    )(basis_count, *pieces)


def exchange(x, axis, bit):
    peers = lax.axis_size(axis)
    return lax.ppermute(x, axis, [(i, i ^ bit) for i in range(peers)])


def after(x, *others):
    return lax.optimization_barrier((x, *others))[0]


def double(own, axis, bits):
    have = {0: own}
    for bit in bits:
        for far in sorted(have):
            have[far | bit] = exchange(have[far], axis, bit)
    return have


def add_parts(total, unroll, d_refs, sums, before=None):
    lam, cols = total.shape

    @loop(lam // TILE, unroll)
    def _(j):
        out = span(j, TILE)
        x = None if before is None else before[out, :]
        for chunks, part in zip(d_refs, sums):
            if len(chunks) == 1:
                d = chunks[0][out, :]
            elif isinstance(j, int):
                d = chunks[0][...] if j == 0 else chunks[1][span(j - 1, TILE), :]
            else:
                d = chunks[1][span(jnp.maximum(j - 1, 0), TILE), :].astype(F32)
                d = jnp.where(j == 0, chunks[0][...].astype(F32), d).astype(BF16)
            y = jnp.dot(d, part(), preferred_element_type=F32)
            x = y if x is None else x + y
        total[out, :] = x


def split_refs(dens, refs):
    lists, at = [], 0
    for chunks in dens.values():
        lists.append(refs[at : at + len(chunks)])
        at += len(chunks)
    return lists, refs[at:]


def flat(dens):
    return [chunk for chunks in dens.values() for chunk in chunks]


def ways_back(basis_count, ri_count, nrows, ncols, rows, wide, lam, cols, unroll):
    lam_atoms, blocks = rows // BW, wide // RW

    def body(count_ref, ri_ref, lam_hot, col_hot):
        row, col = lax.axis_index("row"), lax.axis_index("col")
        pack_cols(count_ref, row * lam_atoms, lam_atoms, BW, lam, lam_hot, unroll)
        place = place_row(ri_ref, col * blocks, blocks, RW)

        @loop(cols // RW, unroll)
        def _(i):
            col_hot[span(i, RW), :] = ones_where(iota((RW, wide), 0) + i * RW == place)

    return pl.pallas_call(
        body,
        out_shape=[jax.ShapeDtypeStruct((rows, lam), BF16), jax.ShapeDtypeStruct((cols, wide), BF16)],
        in_specs=[SMEM_SPEC, SMEM_SPEC],
        out_specs=[VMEM_SPEC] * 2,
        compiler_params=params(16 * 1024 * 1024),
        name="ways_back",
    )(basis_count, ri_count)


def contract_near(dens, integrals, ncols, unroll):
    lam, depth = dens[0][0].shape
    groups, nrows = len(integrals), len(integrals[0])
    sums = [integrals[g][far] for far in range(nrows) for g in range(groups)]
    cols = sums[0].shape[1]
    n, parts = len(dens), len(sums)

    def body(*refs):
        d_refs, refs = split_refs(dens, refs)
        s_refs, refs = refs[:parts], refs[parts:]
        total, s_rest, s_all, s_sem, r_sem = refs
        row, col = lax.axis_index("row"), lax.axis_index("col")
        for j, ref in enumerate(s_refs):
            part = (row ^ (j // groups)) * groups + (col // (ncols // groups) ^ (j % groups))
            pltpu.make_async_copy(ref, s_all.at[part], s_sem.at[part]).start()

        @pl.loop(0, parts)
        def _(i):
            pltpu.make_async_copy(s_all.at[i], s_all.at[i], s_sem.at[i]).wait()

        rest = [
            pltpu.make_async_copy(s_all.at[col ^ far], s_rest.at[far - n], r_sem.at[far - n])
            for far in range(n, parts)
        ]
        for copy in rest:
            copy.start()
        add_parts(total, unroll, d_refs, [lambda far=far: s_all[col ^ far] for far in range(n)])
        for copy in rest:
            copy.wait()

    need = 2 * (n * depth * lam + 2 * parts * depth * cols + 4 * lam * cols)
    return pl.pallas_call(
        body,
        out_shape=[
            jax.ShapeDtypeStruct((lam, cols), F32),
            jax.ShapeDtypeStruct((parts - n, depth, cols), BF16),
        ],
        in_specs=[VMEM_SPEC] * n + [ANY_SPEC] * parts,
        out_specs=[VMEM_SPEC] * 2,
        scratch_shapes=[
            pltpu.VMEM((parts, depth, cols), BF16),
            pltpu.SemaphoreType.DMA((parts,)),
            pltpu.SemaphoreType.DMA((parts - n,)),
        ],
        compiler_params=params(need + 4 * 1024 * 1024),
        cost_estimate=cost(2 * n * depth * lam * cols, 2 * n * depth * (lam + cols)),
        name="contract_near",
    )(*flat(dens), *sums)


def contract_far(dens, first, total, sums, unroll):
    (lam, cols), depth = total.shape, sums.shape[1]
    n = len(dens)

    def body(before, s_ref, *refs):
        d_refs, (o_ref,) = split_refs(dens, refs)
        add_parts(o_ref, unroll, d_refs, [lambda i=i: s_ref[first + i] for i in range(n)], before)

    need = 2 * (n * depth * lam + sums.size + 4 * lam * cols)
    return pl.pallas_call(
        body,
        out_shape=jax.ShapeDtypeStruct((lam, cols), F32),
        in_specs=[VMEM_SPEC] * (2 + len(flat(dens))),
        out_specs=VMEM_SPEC,
        compiler_params=params(need + 4 * 1024 * 1024),
        cost_estimate=cost(2 * n * depth * lam * cols, 2 * n * depth * (lam + cols)),
        name="contract_far",
    )(total, sums, *flat(dens))


def contract_last(dens, first, total, sums, lam_hot, col_hot, unroll):
    (rows, lam), (cols, wide) = lam_hot.shape, col_hot.shape
    depth = sums.shape[1]
    n = len(dens)
    half = lam // 2

    def body(before, s_ref, lam_hot, col_hot, *refs):
        d_refs, (o_ref, total, packed) = split_refs(dens, refs)
        add_parts(total, unroll, d_refs, [lambda i=i: s_ref[first + i] for i in range(n)], before)

        @loop(2, unroll)
        def _(j):
            x = total[span(j, half), :].astype(BF16)
            packed[span(j, half), :] = jnp.dot(x, col_hot[...], preferred_element_type=F32).astype(BF16)

        @loop(4, unroll)
        def _(j):
            out = span(j, rows // 4)
            o_ref[out, :] = jnp.dot(lam_hot[out, :], packed[...], preferred_element_type=F32).astype(BF16)

    need = 2 * (n * depth * lam + sums.size + 4 * lam * cols + rows * lam + cols * wide + (lam + rows) * wide)
    return pl.pallas_call(
        body,
        out_shape=jax.ShapeDtypeStruct((rows, wide), BF16),
        in_specs=[VMEM_SPEC] * (4 + len(flat(dens))),
        out_specs=VMEM_SPEC,
        scratch_shapes=[pltpu.VMEM((lam, cols), F32), pltpu.VMEM((lam, wide), BF16)],
        compiler_params=params(need + 4 * 1024 * 1024),
        cost_estimate=cost(2 * n * depth * lam * cols, 2 * n * depth * (lam + cols)),
        name="contract_last",
    )(total, sums, lam_hot, col_hot, *flat(dens))


def program(lam_size, sum_size, col_size, common):
    unroll = common

    def run(three_center, density, block_mask, density_mask, basis_count, ri_count):
        ncols = lax.axis_size("col")
        nrows = lax.axis_size("row")
        chips = ncols // CORES
        rows, depth = density.shape
        wide = three_center.shape[1] // ncols
        row_bits = [1 << b for b in range(nrows.bit_length() - 1)]
        chip_bits = [CORES << b for b in range(chips.bit_length() - 1)][::-1]
        far_bit, near_bits = chip_bits[0], chip_bits[1:]

        counts = (block_mask, basis_count, ri_count, ncols, col_size, unroll)
        other = exchange(pack_integrals(three_center, *counts)[0], "col", 1)
        own, upper, lower = pack_density(density, density_mask, basis_count, lam_size, sum_size, unroll)
        lines = [{0: upper, far_bit: exchange(upper, "col", far_bit)}, {0: lower}]
        near = {0: own, 1: exchange(own, "col", 1)}
        pieces = pack_integrals(three_center, *counts, after(other, own))
        early = lines[0][far_bit]
        got = [pieces[0]] + [exchange(pieces[t], "col", CORES * t) for t in range(1, chips)]
        per = depth // pieces[0].shape[0]
        lam_hot, col_hot = ways_back(
            basis_count, ri_count, nrows, ncols, rows, wide, lam_size, col_size, unroll
        )
        parts, groups, orders = [], [], []
        for g in range(chips // per):
            arrived = got[g * per : (g + 1) * per]
            if g == 0:
                arrived = [after(arrived[0], near[1], early)] + arrived[1:]
            elif g == 1:
                arrived = [after(arrived[0], lam_hot)] + arrived[1:]
            part = pack_part(arrived, basis_count, g * per, ncols, sum_size)
            if g == 0:
                near.update(double(after(own, part), "col", near_bits))
                steps = [near[far] for far in near if far > 1]
            else:
                part = after(part, *[groups[0][bit] for bit in row_bits])
            parts.append(part)
            orders.append(row_bits if g % 2 == 0 else row_bits[::-1])
            groups.append({0: part})
            for bit in orders[g]:
                groups[g][bit] = exchange(part, "row", bit)
        step = groups[-1][orders[-1][0]]
        across = exchange(after(early, parts[-1]), "col", 1)
        forward = double(after(early, across, *steps), "col", near_bits)
        lines[0].update({far_bit | far: block for far, block in forward.items() if far > 0})
        lines[1][far_bit] = exchange(after(lower, parts[-1]), "col", far_bit)
        for far in [far for far in near if far > 1]:
            near[far | 1] = exchange(after(near[far], across), "col", 1)
        for g, have in enumerate(groups):
            done = [0, orders[g][0]]
            for bit in orders[g][1:]:
                for far in done[1:]:
                    block = have[far] if g == len(groups) - 1 else after(have[far], *[groups[-1][bit] for bit in row_bits])
                    have[far | bit] = exchange(block, "row", bit)
                done += [far | bit for far in done]
        first = {far: [near[far]] for far in sorted(near)}
        total, sums = contract_near(first, groups, ncols, unroll)
        block = after(lines[1][far_bit], lines[0][ncols - CORES])
        for away, block in double(block, "col", near_bits).items():
            lines[1][far_bit | away] = block
        middle = {}
        for far in range(far_bit, ncols - CORES, CORES):
            middle[far] = [line[far] for line in lines]
            middle[far | 1] = [across if line[far] is early else exchange(line[far], "col", 1) for line in lines]
        total = contract_far(middle, 0, total, sums, unroll)
        ends = [line[ncols - CORES] for line in lines]
        last = {ncols - CORES: ends}
        last[ncols - 1] = [exchange(ends[0], "col", 1), exchange(after(ends[1], total), "col", 1)]
        return contract_last(last, len(middle), total, sums, lam_hot, col_hot, unroll)

    return run


def choose(here, yes, no):
    return lambda *args: lax.cond(here, yes, no, *args)


def shards(three_center, density, block_mask, density_mask, basis_count, ri_count):
    ncols = lax.axis_size("col")
    nrows = lax.axis_size("row")
    rows, depth = density.shape
    wide = three_center.shape[1] // ncols
    levels = (
        (rows * 3 // 4, depth * 3 // 4, wide * 5 // 6),
        (rows * 3 // 4, depth, wide * 5 // 6),
        (rows * 3 // 4, depth, wide),
        (rows, depth, wide),
    )
    level = first_fit(basis_count, ri_count, (nrows, ncols, ncols), levels)
    args = (three_center, density, block_mask, density_mask, basis_count, ri_count)
    run = program(*levels[-1], False)
    for n in reversed(range(len(levels) - 1)):
        run = choose(level[0] == n, program(*levels[n], n == 0), run)
    return run(*args)


def solution(mesh):
    in_specs = (
        P(("row", "col"), None),
        P("row", "col"),
        P(("row", "col"), None),
        P("row", "col"),
        P(),
        P(),
    )
    return jax.shard_map(
        shards, mesh=mesh, in_specs=in_specs, out_specs=P("row", "col"), check_vma=False
    )
```

profile of v0, /device:TPU:0, one launch (start us, length us, event | category | flops | bytes accessed | tf_op | source)
XLA Modules:
  0.0 113.8 jit_solution(12082883347458676330)
XLA Ops:
  0.0 1.3 %first_fit.1 = s32[1]{0:T(128)} custom-call(s32[128]{0:T(128)} %count_ref.1, s32[48]{0:T(128)} %ri_ref.1), custom_call_target="tpu_custom_call" | custom-call | tf_op jit(solution)/shard_map/first_fit/pallas_call | solution.py:99
  2.0 110.6 %conditional.3 = (bf16[1024,768]{1,0:T(8,128)(2,1)S(1)}) conditional(s32[]{:T(128)} %convert_element_type.9, (s32[]{:T(128)}, s32[128]{0:T(128)}, s32[32,16]{0,1:T(8,128)}, bf16[1024,512]{1,0:T(8,128)(2,1)}, s32[48]{0:T(128)}, /*index=5*/s32[4,48]{1,0:T(4,128)}, bf16[128,6144]{1,0:T(8,128)(2,1)}) %tuple.74, (s32[128]{0:T(128)}, s32[32,16]{0,1:T(8,128)}, ...), branch_computations={%region_0.0_spmd, %region_5.0_spmd} | conditional | flops 26172456960 | bytes 89402256 | solution.py:492
  2.2 3.0 %pack_other_core.7 = bf16[4,128,640]{2,1,0:T(8,128)(2,1)S(1)} custom-call(s32[128]{0:T(128)} %get-tuple-element.198.count_ref, s32[48]{0:T(128)} %get-tuple-element.202.ri_ref, s32[4,48]{1,0:T(4,128)} %get-tuple-element.203.mask_ref, bf16[128,6144]{1,0:T(8,128)(2,1)} %get-tuple-element.204.x_ref), custom_call_target="tpu_custom_call" | custom-call | flops 503316480 | bytes 1769472 | tf_op jit(solution)/shard_map/cond/branch_1_fun/pack_other_core/pallas_call | solution.py:149
  5.9 4.0 %pack_density.7 = (bf16[768,384]{1,0:T(8,128)(2,1)S(1)}, bf16[256,384]{1,0:T(8,128)(2,1)S(1)}, bf16[512,384]{1,0:T(8,128)(2,1)S(1)}) custom-call(s32[128]{0:T(128)S(1)} %copy-done.12, s32[32,16]{1,0:T(8,128)S(1)} %copy.10.mask_ref, bf16[1024,512]{1,0:T(8,128)(2,1)} %get-tuple-element.200.x_ref), custom_call_target="tpu_custom_call" | custom-call | flops 1006632960 | bytes 1048576 | tf_op jit(solution)/shard_map/cond/branch_1_fun/pack_density/pallas_call | solution.py:198
  10.2 2.2 %pack_own_core.7 = (bf16[256,640]{1,0:T(8,128)(2,1)S(1)}, bf16[256,640]{1,0:T(8,128)(2,1)S(1)}, bf16[256,640]{1,0:T(8,128)(2,1)S(1)}, bf16[256,640]{1,0:T(8,128)(2,1)S(1)}) custom-call(s32[128]{0:T(128)S(1)} %copy-done.12, s32[48]{0:T(128)S(1)} %copy-done.16, s32[4,48]{1,0:T(4,128)S(1)} %copy-done.8, bf16[128,6144]{1,0:T(8,128)(2,1)S(1)} %copy-done.3, ...), custom_call_target="tpu_custom_call" | custom-call | flops 503316480 | bytes 1769472 | tf_op jit(solution)/shard_map/cond/branch_1_fun/pack_own_core/pallas_call | solution.py:149
  12.4 3.0 %collective-permute-start.66 = (bf16[256,640]{1,0:T(8,128)(2,1)S(1)}, bf16[256,640]{1,0:T(8,128)(2,1)S(1)}, u32[]{:S(2)}, u32[]{:S(2)}) collective-permute-start(bf16[256,640]{1,0:T(8,128)(2,1)S(1)} %get-tuple-element.209), channel_id=1, source_target_pairs={{0,2},{1,3},{2,0},{3,1},{4,6},{5,7},{6,4},{7,5},{8,10},{9,11},{10,... | collective-permute-start | bytes 983048 | tf_op jit(solution)/shard_map/cond/branch_1_fun/ppermute | solution.py:244
  15.4 2.6 %collective-permute-start.68 = (bf16[256,640]{1,0:T(8,128)(2,1)S(1)}, bf16[256,640]{1,0:T(8,128)(2,1)S(1)}, u32[]{:S(2)}, u32[]{:S(2)}) collective-permute-start(bf16[256,640]{1,0:T(8,128)(2,1)S(1)} %get-tuple-element.211), channel_id=1, source_target_pairs={{0,4},{1,5},{2,6},{3,7},{4,0},{5,1},{6,2},{7,3},{8,12},{9,13},{10,... | collective-permute-start | bytes 983048 | tf_op jit(solution)/shard_map/cond/branch_1_fun/ppermute | solution.py:244
  18.0 1.9 %collective-permute-start.65 = (bf16[256,384]{1,0:T(8,128)(2,1)S(1)}, bf16[256,384]{1,0:T(8,128)(2,1)S(1)}, u32[]{:S(2)}, u32[]{:S(2)}) collective-permute-start(bf16[256,384]{1,0:T(8,128)(2,1)S(1)} %get-tuple-element.207), channel_id=1, source_target_pairs={{0,4},{1,5},{2,6},{3,7},{4,0},{5,1},{6,2},{7,3},{8,12},{9,13},{10,... | collective-permute-start | bytes 589832 | tf_op jit(solution)/shard_map/cond/branch_1_fun/ppermute | solution.py:244
  21.0 34.3 %collective-permute-done.65.refs_0_ = bf16[256,384]{1,0:T(8,128)(2,1)S(1)} collective-permute-done((bf16[256,384]{1,0:T(8,128)(2,1)S(1)}, bf16[256,384]{1,0:T(8,128)(2,1)S(1)}, u32[]{:S(2)}, u32[]{:S(2)}) %collective-permute-start.65) | collective-permute-done | bytes 196640 | tf_op jit(solution)/shard_map/cond/branch_1_fun/ppermute | solution.py:244
  56.5 1.6 %collective-permute-start.70 = (bf16[384,640]{1,0:T(8,128)(2,1)S(1)}, bf16[384,640]{1,0:T(8,128)(2,1)S(1)}, u32[]{:S(2)}, u32[]{:S(2)}) collective-permute-start(bf16[384,640]{1,0:T(8,128)(2,1)S(1)} %pack_part.14.refs_4_), channel_id=1, source_target_pairs={{0,8},{8,0},{16,24},{24,16},{1,9},{9,1},{17,25},{25,17},{2,10},{10... | collective-permute-start | bytes 1474568 | tf_op jit(solution)/shard_map/cond/branch_1_fun/ppermute | solution.py:244
  58.1 1.5 %collective-permute-start.71 = (bf16[384,640]{1,0:T(8,128)(2,1)S(1)}, bf16[384,640]{1,0:T(8,128)(2,1)S(1)}, u32[]{:S(2)}, u32[]{:S(2)}) collective-permute-start(bf16[384,640]{1,0:T(8,128)(2,1)S(1)} %pack_part.14.refs_4_), channel_id=1, source_target_pairs={{0,16},{8,24},{16,0},{24,8},{1,17},{9,25},{17,1},{25,9},{2,18},{10... | collective-permute-start | bytes 1474568 | tf_op jit(solution)/shard_map/cond/branch_1_fun/ppermute | solution.py:244
  60.8 7.9 %collective-permute-done.70.refs_6_ = bf16[384,640]{1,0:T(8,128)(2,1)S(1)} collective-permute-done((bf16[384,640]{1,0:T(8,128)(2,1)S(1)}, bf16[384,640]{1,0:T(8,128)(2,1)S(1)}, u32[]{:S(2)}, u32[]{:S(2)}) %collective-permute-start.70) | collective-permute-done | bytes 491552 | tf_op jit(solution)/shard_map/cond/branch_1_fun/ppermute | solution.py:244
  70.5 1.5 %collective-permute-start.75 = (bf16[384,640]{1,0:T(8,128)(2,1)S(1)}, bf16[384,640]{1,0:T(8,128)(2,1)S(1)}, u32[]{:S(2)}, u32[]{:S(2)}) collective-permute-start(bf16[384,640]{1,0:T(8,128)(2,1)S(1)} %pack_part.15.refs_5_), channel_id=1, source_target_pairs={{0,16},{8,24},{16,0},{24,8},{1,17},{9,25},{17,1},{25,9},{2,18},{10... | collective-permute-start | bytes 1474568 | tf_op jit(solution)/shard_map/cond/branch_1_fun/ppermute | solution.py:244
  72.0 1.3 %collective-permute-done.67.refs_2_ = bf16[768,384]{1,0:T(8,128)(2,1)S(1)} collective-permute-done((bf16[768,384]{1,0:T(8,128)(2,1)S(1)}, bf16[768,384]{1,0:T(8,128)(2,1)S(1)}, u32[]{:S(2)}, u32[]{:S(2)}) %collective-permute-start.67) | collective-permute-done | bytes 589856 | tf_op jit(solution)/shard_map/cond/branch_1_fun/ppermute | solution.py:244
  73.6 7.3 %collective-permute-done.74.refs_7_ = bf16[384,640]{1,0:T(8,128)(2,1)S(1)} collective-permute-done((bf16[384,640]{1,0:T(8,128)(2,1)S(1)}, bf16[384,640]{1,0:T(8,128)(2,1)S(1)}, u32[]{:S(2)}, u32[]{:S(2)}) %collective-permute-start.74) | collective-permute-done | bytes 491552 | tf_op jit(solution)/shard_map/cond/branch_1_fun/ppermute | solution.py:244
  81.9 1.5 %collective-permute-start.76 = (bf16[384,640]{1,0:T(8,128)(2,1)S(1)}, bf16[384,640]{1,0:T(8,128)(2,1)S(1)}, u32[]{:S(2)}, u32[]{:S(2)}) collective-permute-start(bf16[384,640]{1,0:T(8,128)(2,1)S(1)} %collective-permute-done.70.refs_6_), channel_id=1, source_target_pairs={{0,16},{8,24},{16,0},{24,8},{1,17},{9,25},{17,1},{25,9},{2,18},{10... | collective-permute-start | bytes 1474568 | tf_op jit(solution)/shard_map/cond/branch_1_fun/ppermute | solution.py:244
  83.4 1.5 %collective-permute-start.77 = (bf16[384,640]{1,0:T(8,128)(2,1)S(1)}, bf16[384,640]{1,0:T(8,128)(2,1)S(1)}, u32[]{:S(2)}, u32[]{:S(2)}) collective-permute-start(bf16[384,640]{1,0:T(8,128)(2,1)S(1)} %collective-permute-done.75.refs_9_), channel_id=1, source_target_pairs={{0,8},{8,0},{16,24},{24,16},{1,9},{9,1},{17,25},{25,17},{2,10},{10... | collective-permute-start | bytes 1474568 | tf_op jit(solution)/shard_map/cond/branch_1_fun/ppermute | solution.py:244
  84.9 7.9 %collective-permute-done.78.refs_1_ = bf16[512,384]{1,0:T(8,128)(2,1)S(1)} collective-permute-done((bf16[512,384]{1,0:T(8,128)(2,1)S(1)}, bf16[512,384]{1,0:T(8,128)(2,1)S(1)}, u32[]{:S(2)}, u32[]{:S(2)}) %collective-permute-start.78) | collective-permute-done | bytes 393248 | tf_op jit(solution)/shard_map/cond/branch_1_fun/ppermute | solution.py:244
  92.8 2.6 %collective-permute-done.79.refs_0_ = bf16[256,384]{1,0:T(8,128)(2,1)S(1)} collective-permute-done((bf16[256,384]{1,0:T(8,128)(2,1)S(1)}, bf16[256,384]{1,0:T(8,128)(2,1)S(1)}, u32[]{:S(2)}, u32[]{:S(2)}) %collective-permute-start.79) | collective-permute-done | bytes 196640 | tf_op jit(solution)/shard_map/cond/branch_1_fun/ppermute | solution.py:244
  95.4 6.4 %contract_near.7 = (f32[768,640]{1,0:T(8,128)S(1)}, bf16[4,384,640]{2,1,0:T(8,128)(2,1)S(1)}) custom-call(bf16[768,384]{1,0:T(8,128)(2,1)S(1)} %get-tuple-element.210.refs_0_, bf16[768,384]{1,0:T(8,128)(2,1)S(1)} %collective-permute-done.64.refs_1_, bf16[768,384]{1,0:T(8,128)(2,1)S(1)} %collective-permute-done.67.refs_2_, ...), custom_call_target="tpu_custom_call" | custom-call | flops 1509949440 | bytes 4325376 | tf_op jit(solution)/shard_map/cond/branch_1_fun/contract_near/pallas_call | solution.py:344
  101.8 1.3 %contract_far.7.before = f32[768,640]{1,0:T(8,128)S(1)} custom-call(f32[768,640]{1,0:T(8,128)S(1)} %get-tuple-element.219.before, bf16[4,384,640]{2,1,0:T(8,128)(2,1)S(1)} %get-tuple-element.220.s_ref, bf16[256,384]{1,0:T(8,128)(2,1)S(1)} %collective-permute-done.65.refs_0_, bf16[512,384]{1,0:T(8,128)(2,1)S(1)} %collective-permute-done.78.refs_1_, ...), custom_call_target="tpu_custom_call" | custom-call | flops 754974720 | bytes 2162688 | tf_op jit(solution)/shard_map/cond/branch_1_fun/contract_far/pallas_call | solution.py:372
  103.1 3.8 %collective-permute-done.81.refs_1_ = bf16[512,384]{1,0:T(8,128)(2,1)S(1)} collective-permute-done((bf16[512,384]{1,0:T(8,128)(2,1)S(1)}, bf16[512,384]{1,0:T(8,128)(2,1)S(1)}, u32[]{:S(2)}, u32[]{:S(2)}) %collective-permute-start.81) | collective-permute-done | bytes 393248 | tf_op jit(solution)/shard_map/cond/branch_1_fun/ppermute | solution.py:244
  107.4 1.5 %collective-permute-done.82.refs_2_ = bf16[256,384]{1,0:T(8,128)(2,1)S(1)} collective-permute-done((bf16[256,384]{1,0:T(8,128)(2,1)S(1)}, bf16[256,384]{1,0:T(8,128)(2,1)S(1)}, u32[]{:S(2)}, u32[]{:S(2)}) %collective-permute-start.82) | collective-permute-done | bytes 196640 | tf_op jit(solution)/shard_map/cond/branch_1_fun/ppermute | solution.py:244
  108.9 3.4 %contract_last.7 = bf16[1024,768]{1,0:T(8,128)(2,1)S(1)} custom-call(f32[768,640]{1,0:T(8,128)S(1)} %contract_far.7.before, bf16[4,384,640]{2,1,0:T(8,128)(2,1)S(1)} %get-tuple-element.220.s_ref, bf16[1024,768]{1,0:T(8,128)(2,1)S(1)} %get-tuple-element.212.lam_hot, bf16[640,768]{1,0:T(8,128)(2,1)S(1)} %get-tuple-element.225.col_hot, ...), custom_call_target="tpu_custom_call" | custom-call | flops 754974720 | bytes 2162688 | tf_op jit(solution)/shard_map/cond/branch_1_fun/contract_last/pallas_call | solution.py:404
  (42 shorter events, 9.0 us)
Async XLA Ops:
  5.3 4.9 %copy-start.3 = (bf16[128,6144]{1,0:T(8,128)(2,1)S(1)}, bf16[128,6144]{1,0:T(8,128)(2,1)}, u32[]{:S(2)}) copy-start(bf16[128,6144]{1,0:T(8,128)(2,1)} %get-tuple-element.204.x_ref) | copy-start | bytes 4718596 | tf_op jit(solution)/shard_map/cond
  5.3 4.9 %copy-start.8 = (s32[4,48]{1,0:T(4,128)S(1)}, s32[4,48]{1,0:T(4,128)}, u32[]{:S(2)}) copy-start(s32[4,48]{1,0:T(4,128)} %get-tuple-element.203.mask_ref) | copy-start | bytes 2308 | tf_op jit(solution)/shard_map/cond
  5.3 4.9 %copy-start.16 = (s32[48]{0:T(128)S(1)}, s32[48]{0:T(128)}, u32[]{:S(2)}) copy-start(s32[48]{0:T(128)} %get-tuple-element.202.ri_ref) | copy-start | bytes 580 | tf_op jit(solution)/shard_map/cond
  5.3 4.9 %collective-permute-start.63 = (bf16[4,128,640]{2,1,0:T(8,128)(2,1)S(1)}, bf16[4,128,640]{2,1,0:T(8,128)(2,1)S(1)}, u32[]{:S(2)}, u32[]{:S(2)}) collective-permute-start(bf16[4,128,640]{2,1,0:T(8,128)(2,1)S(1)} %pack_other_core.7), channel_id=1, source_target_pairs={{0,1},{1,0},{2,3},{3,2},{4,5},{5,4},{6,7},{7,6},{8,9},{9,8},{10,11... | collective-permute-start | bytes 1966088 | tf_op jit(solution)/shard_map/cond/branch_1_fun/ppermute | solution.py:244
  9.9 45.4 %collective-permute-start.64 = (bf16[768,384]{1,0:T(8,128)(2,1)S(1)}, bf16[768,384]{1,0:T(8,128)(2,1)S(1)}, u32[]{:S(2)}, u32[]{:S(2)}) collective-permute-start(bf16[768,384]{1,0:T(8,128)(2,1)S(1)} %get-tuple-element.210.refs_0_), channel_id=1, source_target_pairs={{0,1},{1,0},{2,3},{3,2},{4,5},{5,4},{6,7},{7,6},{8,9},{9,8},{10,11... | collective-permute-start | bytes 1769480 | tf_op jit(solution)/shard_map/cond/branch_1_fun/ppermute | solution.py:244
  12.4 42.9 %collective-permute-start.66 = (bf16[256,640]{1,0:T(8,128)(2,1)S(1)}, bf16[256,640]{1,0:T(8,128)(2,1)S(1)}, u32[]{:S(2)}, u32[]{:S(2)}) collective-permute-start(bf16[256,640]{1,0:T(8,128)(2,1)S(1)} %get-tuple-element.209), channel_id=1, source_target_pairs={{0,2},{1,3},{2,0},{3,1},{4,6},{5,7},{6,4},{7,5},{8,10},{9,11},{10,... | collective-permute-start | bytes 983048 | tf_op jit(solution)/shard_map/cond/branch_1_fun/ppermute | solution.py:244
  15.4 44.2 %collective-permute-start.68 = (bf16[256,640]{1,0:T(8,128)(2,1)S(1)}, bf16[256,640]{1,0:T(8,128)(2,1)S(1)}, u32[]{:S(2)}, u32[]{:S(2)}) collective-permute-start(bf16[256,640]{1,0:T(8,128)(2,1)S(1)} %get-tuple-element.211), channel_id=1, source_target_pairs={{0,4},{1,5},{2,6},{3,7},{4,0},{5,1},{6,2},{7,3},{8,12},{9,13},{10,... | collective-permute-start | bytes 983048 | tf_op jit(solution)/shard_map/cond/branch_1_fun/ppermute | solution.py:244
  18.0 41.6 %collective-permute-start.69 = (bf16[256,640]{1,0:T(8,128)(2,1)S(1)}, bf16[256,640]{1,0:T(8,128)(2,1)S(1)}, u32[]{:S(2)}, u32[]{:S(2)}) collective-permute-start(bf16[256,640]{1,0:T(8,128)(2,1)S(1)} %get-tuple-element.214), channel_id=1, source_target_pairs={{0,6},{1,7},{2,4},{3,5},{4,2},{5,3},{6,0},{7,1},{8,14},{9,15},{10,... | collective-permute-start | bytes 983048 | tf_op jit(solution)/shard_map/cond/branch_1_fun/ppermute | solution.py:244
  18.0 37.3 %collective-permute-start.65 = (bf16[256,384]{1,0:T(8,128)(2,1)S(1)}, bf16[256,384]{1,0:T(8,128)(2,1)S(1)}, u32[]{:S(2)}, u32[]{:S(2)}) collective-permute-start(bf16[256,384]{1,0:T(8,128)(2,1)S(1)} %get-tuple-element.207), channel_id=1, source_target_pairs={{0,4},{1,5},{2,6},{3,7},{4,0},{5,1},{6,2},{7,3},{8,12},{9,13},{10,... | collective-permute-start | bytes 589832 | tf_op jit(solution)/shard_map/cond/branch_1_fun/ppermute | solution.py:244
  56.5 12.2 %collective-permute-start.70 = (bf16[384,640]{1,0:T(8,128)(2,1)S(1)}, bf16[384,640]{1,0:T(8,128)(2,1)S(1)}, u32[]{:S(2)}, u32[]{:S(2)}) collective-permute-start(bf16[384,640]{1,0:T(8,128)(2,1)S(1)} %pack_part.14.refs_4_), channel_id=1, source_target_pairs={{0,8},{8,0},{16,24},{24,16},{1,9},{9,1},{17,25},{25,17},{2,10},{10... | collective-permute-start | bytes 1474568 | tf_op jit(solution)/shard_map/cond/branch_1_fun/ppermute | solution.py:244
  58.1 11.9 %collective-permute-start.71 = (bf16[384,640]{1,0:T(8,128)(2,1)S(1)}, bf16[384,640]{1,0:T(8,128)(2,1)S(1)}, u32[]{:S(2)}, u32[]{:S(2)}) collective-permute-start(bf16[384,640]{1,0:T(8,128)(2,1)S(1)} %pack_part.14.refs_4_), channel_id=1, source_target_pairs={{0,16},{8,24},{16,0},{24,8},{1,17},{9,25},{17,1},{25,9},{2,18},{10... | collective-permute-start | bytes 1474568 | tf_op jit(solution)/shard_map/cond/branch_1_fun/ppermute | solution.py:244
  59.6 13.7 %collective-permute-start.67 = (bf16[768,384]{1,0:T(8,128)(2,1)S(1)}, bf16[768,384]{1,0:T(8,128)(2,1)S(1)}, u32[]{:S(2)}, u32[]{:S(2)}) collective-permute-start(bf16[768,384]{1,0:T(8,128)(2,1)S(1)} %get-tuple-element.210.refs_0_), channel_id=1, source_target_pairs={{0,2},{1,3},{2,0},{3,1},{4,6},{5,7},{6,4},{7,5},{8,10},{9,11},{10,... | collective-permute-start | bytes 1769480 | tf_op jit(solution)/shard_map/cond/branch_1_fun/ppermute | solution.py:244
  70.0 10.9 %collective-permute-start.74 = (bf16[384,640]{1,0:T(8,128)(2,1)S(1)}, bf16[384,640]{1,0:T(8,128)(2,1)S(1)}, u32[]{:S(2)}, u32[]{:S(2)}) collective-permute-start(bf16[384,640]{1,0:T(8,128)(2,1)S(1)} %pack_part.15.refs_5_), channel_id=1, source_target_pairs={{0,8},{8,0},{16,24},{24,16},{1,9},{9,1},{17,25},{25,17},{2,10},{10... | collective-permute-start | bytes 1474568 | tf_op jit(solution)/shard_map/cond/branch_1_fun/ppermute | solution.py:244
  70.5 11.4 %collective-permute-start.75 = (bf16[384,640]{1,0:T(8,128)(2,1)S(1)}, bf16[384,640]{1,0:T(8,128)(2,1)S(1)}, u32[]{:S(2)}, u32[]{:S(2)}) collective-permute-start(bf16[384,640]{1,0:T(8,128)(2,1)S(1)} %pack_part.15.refs_5_), channel_id=1, source_target_pairs={{0,16},{8,24},{16,0},{24,8},{1,17},{9,25},{17,1},{25,9},{2,18},{10... | collective-permute-start | bytes 1474568 | tf_op jit(solution)/shard_map/cond/branch_1_fun/ppermute | solution.py:244
  72.0 1.4 %collective-permute-start.72 = (bf16[256,384]{1,0:T(8,128)(2,1)S(1)}, bf16[256,384]{1,0:T(8,128)(2,1)S(1)}, u32[]{:S(2)}, u32[]{:S(2)}) collective-permute-start(bf16[256,384]{1,0:T(8,128)(2,1)S(1)} %collective-permute-done.65.refs_0_), channel_id=1, source_target_pairs={{0,1},{1,0},{2,3},{3,2},{4,5},{5,4},{6,7},{7,6},{8,9},{9,8},{10,11... | collective-permute-start | bytes 589832 | tf_op jit(solution)/shard_map/cond/branch_1_fun/ppermute | solution.py:244
  72.0 20.8 %collective-permute-start.78 = (bf16[512,384]{1,0:T(8,128)(2,1)S(1)}, bf16[512,384]{1,0:T(8,128)(2,1)S(1)}, u32[]{:S(2)}, u32[]{:S(2)}) collective-permute-start(bf16[512,384]{1,0:T(8,128)(2,1)S(1)} %get-tuple-element.222), channel_id=1, source_target_pairs={{0,4},{1,5},{2,6},{3,7},{4,0},{5,1},{6,2},{7,3},{8,12},{9,13},{10,... | collective-permute-start | bytes 1179656 | tf_op jit(solution)/shard_map/cond/branch_1_fun/ppermute | solution.py:244
  73.5 21.9 %collective-permute-start.73 = (bf16[768,384]{1,0:T(8,128)(2,1)S(1)}, bf16[768,384]{1,0:T(8,128)(2,1)S(1)}, u32[]{:S(2)}, u32[]{:S(2)}) collective-permute-start(bf16[768,384]{1,0:T(8,128)(2,1)S(1)} %collective-permute-done.67.refs_2_), channel_id=1, source_target_pairs={{0,1},{1,0},{2,3},{3,2},{4,5},{5,4},{6,7},{7,6},{8,9},{9,8},{10,11... | collective-permute-start | bytes 1769480 | tf_op jit(solution)/shard_map/cond/branch_1_fun/ppermute | solution.py:244
  81.9 13.5 %collective-permute-start.76 = (bf16[384,640]{1,0:T(8,128)(2,1)S(1)}, bf16[384,640]{1,0:T(8,128)(2,1)S(1)}, u32[]{:S(2)}, u32[]{:S(2)}) collective-permute-start(bf16[384,640]{1,0:T(8,128)(2,1)S(1)} %collective-permute-done.70.refs_6_), channel_id=1, source_target_pairs={{0,16},{8,24},{16,0},{24,8},{1,17},{9,25},{17,1},{25,9},{2,18},{10... | collective-permute-start | bytes 1474568 | tf_op jit(solution)/shard_map/cond/branch_1_fun/ppermute | solution.py:244
  83.4 12.0 %collective-permute-start.77 = (bf16[384,640]{1,0:T(8,128)(2,1)S(1)}, bf16[384,640]{1,0:T(8,128)(2,1)S(1)}, u32[]{:S(2)}, u32[]{:S(2)}) collective-permute-start(bf16[384,640]{1,0:T(8,128)(2,1)S(1)} %collective-permute-done.75.refs_9_), channel_id=1, source_target_pairs={{0,8},{8,0},{16,24},{24,16},{1,9},{9,1},{17,25},{25,17},{2,10},{10... | collective-permute-start | bytes 1474568 | tf_op jit(solution)/shard_map/cond/branch_1_fun/ppermute | solution.py:244
  84.9 10.5 %collective-permute-start.79 = (bf16[256,384]{1,0:T(8,128)(2,1)S(1)}, bf16[256,384]{1,0:T(8,128)(2,1)S(1)}, u32[]{:S(2)}, u32[]{:S(2)}) collective-permute-start(bf16[256,384]{1,0:T(8,128)(2,1)S(1)} %collective-permute-done.65.refs_0_), channel_id=1, source_target_pairs={{0,2},{1,3},{2,0},{3,1},{4,6},{5,7},{6,4},{7,5},{8,10},{9,11},{10,... | collective-permute-start | bytes 589832 | tf_op jit(solution)/shard_map/cond/branch_1_fun/ppermute | solution.py:244
  95.4 6.5 %collective-permute-start.80 = (bf16[512,384]{1,0:T(8,128)(2,1)S(1)}, bf16[512,384]{1,0:T(8,128)(2,1)S(1)}, u32[]{:S(2)}, u32[]{:S(2)}) collective-permute-start(bf16[512,384]{1,0:T(8,128)(2,1)S(1)} %collective-permute-done.78.refs_1_), channel_id=1, source_target_pairs={{0,1},{1,0},{2,3},{3,2},{4,5},{5,4},{6,7},{7,6},{8,9},{9,8},{10,11... | collective-permute-start | bytes 1179656 | tf_op jit(solution)/shard_map/cond/branch_1_fun/ppermute | solution.py:244
  95.4 11.5 %collective-permute-start.81 = (bf16[512,384]{1,0:T(8,128)(2,1)S(1)}, bf16[512,384]{1,0:T(8,128)(2,1)S(1)}, u32[]{:S(2)}, u32[]{:S(2)}) collective-permute-start(bf16[512,384]{1,0:T(8,128)(2,1)S(1)} %collective-permute-done.78.refs_1_), channel_id=1, source_target_pairs={{0,2},{1,3},{2,0},{3,1},{4,6},{5,7},{6,4},{7,5},{8,10},{9,11},{10,... | collective-permute-start | bytes 1179656 | tf_op jit(solution)/shard_map/cond/branch_1_fun/ppermute | solution.py:244
  106.9 2.0 %collective-permute-start.83 = (bf16[512,384]{1,0:T(8,128)(2,1)S(1)}, bf16[512,384]{1,0:T(8,128)(2,1)S(1)}, u32[]{:S(2)}, u32[]{:S(2)}) collective-permute-start(bf16[512,384]{1,0:T(8,128)(2,1)S(1)} %collective-permute-done.81.refs_1_), channel_id=1, source_target_pairs={{0,1},{1,0},{2,3},{3,2},{4,5},{5,4},{6,7},{7,6},{8,9},{9,8},{10,11... | collective-permute-start | bytes 1179656 | tf_op jit(solution)/shard_map/cond/branch_1_fun/ppermute | solution.py:244
  106.9 2.0 %collective-permute-start.82 = (bf16[256,384]{1,0:T(8,128)(2,1)S(1)}, bf16[256,384]{1,0:T(8,128)(2,1)S(1)}, u32[]{:S(2)}, u32[]{:S(2)}) collective-permute-start(bf16[256,384]{1,0:T(8,128)(2,1)S(1)} %collective-permute-done.79.refs_0_), channel_id=1, source_target_pairs={{0,1},{1,0},{2,3},{3,2},{4,5},{5,4},{6,7},{7,6},{8,9},{9,8},{10,11... | collective-permute-start | bytes 589832 | tf_op jit(solution)/shard_map/cond/branch_1_fun/ppermute | solution.py:244
  (3 other events, 8.4 us)
where the time goes:
time: 114 us
  waiting for transfers between devices  68.9 us (60%)
  Pallas kernels  25.2 us (22%)
  starting transfers between devices  17 us (15%)
  local copies, waits for them, and re-layouts  1.24 us (1%)
    ppermute x21, waiting for transfers between devices, exchange(): return lax.ppermute(x, axis, [(i, i ^ bit) for i in range(peers)])  68.9 us
    ppermute x21, starting transfers between devices, exchange(): return lax.ppermute(x, axis, [(i, i ^ bit) for i in range(peers)])  17 us
    pallas_call x1, Pallas kernels, contract_near(): pl.pallas_call(body, out_shape=[jax.ShapeDtypeStruct((lam, cols), F32), j...  6.43 us
    pallas_call x2, Pallas kernels, pack_integrals(): pl.pallas_call(body, out_shape=out_shape, in_specs=[SMEM_SPEC, SMEM_SPEC,...  5.23 us
    pallas_call x1, Pallas kernels, pack_density(): pl.pallas_call(body, out_shape=[jax.ShapeDtypeStruct((n, sum_size), BF16)...  4.05 us
    pallas_call x1, Pallas kernels, contract_last(): pl.pallas_call(body, out_shape=jax.ShapeDtypeStruct((rows, wide), BF16),...  3.42 us
    pallas_call x2, Pallas kernels, pack_part(): pl.pallas_call(body, out_shape=jax.ShapeDtypeStruct((size, cols), BF16),...  2.41 us
  transfers between devices with their start and end apart: 21, of which 11 were waited for; matrix products, arithmetic and copies ran while one was open for 0% of the time, Pallas kernels for 15%

commit v1 on v0

--- a/solution.py
+++ b/solution.py
@@ -442,7 +442,7 @@
         for g in range(chips // per):
             arrived = got[g * per : (g + 1) * per]
             if g == 0:
-                arrived = [after(arrived[0], near[1], early)] + arrived[1:]
+                arrived = [after(arrived[0], near[1])] + arrived[1:]
             elif g == 1:
                 arrived = [after(arrived[0], lam_hot)] + arrived[1:]
             part = pack_part(arrived, basis_count, g * per, ncols, sum_size)

time: 114 us -> 97 us (0.85)
  waiting for transfers between devices: 68.9 us -> 41.6 us
  starting transfers between devices: 17 us -> 27.4 us
    ppermute x21, waiting for transfers between devices: 68.9 us -> 41.6 us  [exchange(): return lax.ppermute(x, axis, [(i, i ^ bit) for i in range(peers)])]
    ppermute x21, starting transfers between devices: 17 us -> 27.4 us  [exchange(): return lax.ppermute(x, axis, [(i, i ^ bit) for i in range(peers)])]
  transfers between devices with their start and end apart: 21 -> 21, of which waited for: 11 -> 8; matrix products, arithmetic and copies ran while one was open for 0% -> 0% of each run, Pallas kernels for 15% -> 18%
where the time goes in v1:
time: 97 us; the launch traced here: 96.8 us
  waiting for transfers between devices  41.6 us (43%)
  starting transfers between devices  27.4 us (28%)
  Pallas kernels  25.2 us (26%)
  local copies, waits for them, and re-layouts  1.24 us (1%)
    ppermute x21, waiting for transfers between devices, exchange(): return lax.ppermute(x, axis, [(i, i ^ bit) for i in range(peers)])  41.6 us
    ppermute x21, starting transfers between devices, exchange(): return lax.ppermute(x, axis, [(i, i ^ bit) for i in range(peers)])  27.4 us
    pallas_call x1, Pallas kernels, contract_near(): pl.pallas_call(body, out_shape=[jax.ShapeDtypeStruct((lam, cols), F32), j...  6.43 us
    pallas_call x2, Pallas kernels, pack_integrals(): pl.pallas_call(body, out_shape=out_shape, in_specs=[SMEM_SPEC, SMEM_SPEC,...  5.23 us
    pallas_call x1, Pallas kernels, pack_density(): pl.pallas_call(body, out_shape=[jax.ShapeDtypeStruct((n, sum_size), BF16)...  4.05 us
    pallas_call x1, Pallas kernels, contract_last(): pl.pallas_call(body, out_shape=jax.ShapeDtypeStruct((rows, wide), BF16),...  3.42 us
    pallas_call x2, Pallas kernels, pack_part(): pl.pallas_call(body, out_shape=jax.ShapeDtypeStruct((size, cols), BF16),...  2.41 us
  transfers between devices with their start and end apart: 21, of which 8 were waited for; matrix products, arithmetic and copies ran while one was open for 0% of the time, Pallas kernels for 18%

profile of v1, /device:TPU:0, one launch (start us, length us, event | category | flops | bytes accessed | tf_op | source)
XLA Modules:
  0.0 96.8 jit_solution(2310293083189627749)
XLA Ops:
  2.0 93.7 %conditional.3 = (bf16[1024,768]{1,0:T(8,128)(2,1)S(1)}) conditional(s32[]{:T(128)} %convert_element_type.9, (s32[]{:T(128)}, s32[128]{0:T(128)}, s32[32,16]{0,1:T(8,128)}, bf16[1024,512]{1,0:T(8,128)(2,1)}, s32[48]{0:T(128)}, /*index=5*/s32[4,48]{1,0:T(4,128)}, bf16[128,6144]{1,0:T(8,128)(2,1)}) %tuple.74, (s32[128]{0:T(128)}, s32[32,16]{0,1:T(8,128)}, ...), branch_computations={%region_0.0_spmd, %region_5.0_spmd} | conditional | flops 26172456960 | bytes 89402256 | solution.py:492
  2.2 3.0 %pack_other_core.7 = bf16[4,128,640]{2,1,0:T(8,128)(2,1)S(1)} custom-call(s32[128]{0:T(128)} %get-tuple-element.198.count_ref, s32[48]{0:T(128)} %get-tuple-element.202.ri_ref, s32[4,48]{1,0:T(4,128)} %get-tuple-element.203.mask_ref, bf16[128,6144]{1,0:T(8,128)(2,1)} %get-tuple-element.204.x_ref), custom_call_target="tpu_custom_call" | custom-call | flops 503316480 | bytes 1769472 | tf_op jit(solution)/shard_map/cond/branch_1_fun/pack_other_core/pallas_call | solution.py:149
  5.9 4.0 %pack_density.7 = (bf16[768,384]{1,0:T(8,128)(2,1)S(1)}, bf16[256,384]{1,0:T(8,128)(2,1)S(1)}, bf16[512,384]{1,0:T(8,128)(2,1)S(1)}) custom-call(s32[128]{0:T(128)S(1)} %copy-done.12, s32[32,16]{1,0:T(8,128)S(1)} %copy.10.mask_ref, bf16[1024,512]{1,0:T(8,128)(2,1)} %get-tuple-element.200.x_ref), custom_call_target="tpu_custom_call" | custom-call | flops 1006632960 | bytes 1048576 | tf_op jit(solution)/shard_map/cond/branch_1_fun/pack_density/pallas_call | solution.py:198
  10.2 2.2 %pack_own_core.7 = (bf16[256,640]{1,0:T(8,128)(2,1)S(1)}, bf16[256,640]{1,0:T(8,128)(2,1)S(1)}, bf16[256,640]{1,0:T(8,128)(2,1)S(1)}, bf16[256,640]{1,0:T(8,128)(2,1)S(1)}) custom-call(s32[128]{0:T(128)S(1)} %copy-done.12, s32[48]{0:T(128)S(1)} %copy-done.16, s32[4,48]{1,0:T(4,128)S(1)} %copy-done.8, bf16[128,6144]{1,0:T(8,128)(2,1)S(1)} %copy-done.3, ...), custom_call_target="tpu_custom_call" | custom-call | flops 503316480 | bytes 1769472 | tf_op jit(solution)/shard_map/cond/branch_1_fun/pack_own_core/pallas_call | solution.py:149
  12.4 3.0 %collective-permute-start.65 = (bf16[256,640]{1,0:T(8,128)(2,1)S(1)}, bf16[256,640]{1,0:T(8,128)(2,1)S(1)}, u32[]{:S(2)}, u32[]{:S(2)}) collective-permute-start(bf16[256,640]{1,0:T(8,128)(2,1)S(1)} %get-tuple-element.208), channel_id=1, source_target_pairs={{0,2},{1,3},{2,0},{3,1},{4,6},{5,7},{6,4},{7,5},{8,10},{9,11},{10,... | collective-permute-start | bytes 983048 | tf_op jit(solution)/shard_map/cond/branch_1_fun/ppermute | solution.py:244
  15.4 2.6 %collective-permute-start.68 = (bf16[256,640]{1,0:T(8,128)(2,1)S(1)}, bf16[256,640]{1,0:T(8,128)(2,1)S(1)}, u32[]{:S(2)}, u32[]{:S(2)}) collective-permute-start(bf16[256,640]{1,0:T(8,128)(2,1)S(1)} %get-tuple-element.211), channel_id=1, source_target_pairs={{0,4},{1,5},{2,6},{3,7},{4,0},{5,1},{6,2},{7,3},{8,12},{9,13},{10,... | collective-permute-start | bytes 983048 | tf_op jit(solution)/shard_map/cond/branch_1_fun/ppermute | solution.py:244
  18.0 1.9 %collective-permute-start.67 = (bf16[256,384]{1,0:T(8,128)(2,1)S(1)}, bf16[256,384]{1,0:T(8,128)(2,1)S(1)}, u32[]{:S(2)}, u32[]{:S(2)}) collective-permute-start(bf16[256,384]{1,0:T(8,128)(2,1)S(1)} %get-tuple-element.210), channel_id=1, source_target_pairs={{0,4},{1,5},{2,6},{3,7},{4,0},{5,1},{6,2},{7,3},{8,12},{9,13},{10,... | collective-permute-start | bytes 589832 | tf_op jit(solution)/shard_map/cond/branch_1_fun/ppermute | solution.py:244
  21.0 8.8 %collective-permute-done.65.refs_1_ = bf16[256,640]{1,0:T(8,128)(2,1)S(1)} collective-permute-done((bf16[256,640]{1,0:T(8,128)(2,1)S(1)}, bf16[256,640]{1,0:T(8,128)(2,1)S(1)}, u32[]{:S(2)}, u32[]{:S(2)}) %collective-permute-start.65) | collective-permute-done | bytes 327712 | tf_op jit(solution)/shard_map/cond/branch_1_fun/ppermute | solution.py:244
  31.0 1.7 %collective-permute-start.70 = (bf16[384,640]{1,0:T(8,128)(2,1)S(1)}, bf16[384,640]{1,0:T(8,128)(2,1)S(1)}, u32[]{:S(2)}, u32[]{:S(2)}) collective-permute-start(bf16[384,640]{1,0:T(8,128)(2,1)S(1)} %pack_part.14.refs_4_), channel_id=1, source_target_pairs={{0,8},{8,0},{16,24},{24,16},{1,9},{9,1},{17,25},{25,17},{2,10},{10... | collective-permute-start | bytes 1474568 | tf_op jit(solution)/shard_map/cond/branch_1_fun/ppermute | solution.py:244
  32.7 1.5 %collective-permute-start.71 = (bf16[384,640]{1,0:T(8,128)(2,1)S(1)}, bf16[384,640]{1,0:T(8,128)(2,1)S(1)}, u32[]{:S(2)}, u32[]{:S(2)}) collective-permute-start(bf16[384,640]{1,0:T(8,128)(2,1)S(1)} %pack_part.14.refs_4_), channel_id=1, source_target_pairs={{0,16},{8,24},{16,0},{24,8},{1,17},{9,25},{17,1},{25,9},{2,18},{10... | collective-permute-start | bytes 1474568 | tf_op jit(solution)/shard_map/cond/branch_1_fun/ppermute | solution.py:244
  34.3 10.9 %collective-permute-done.68.refs_0_ = bf16[256,640]{1,0:T(8,128)(2,1)S(1)} collective-permute-done((bf16[256,640]{1,0:T(8,128)(2,1)S(1)}, bf16[256,640]{1,0:T(8,128)(2,1)S(1)}, u32[]{:S(2)}, u32[]{:S(2)}) %collective-permute-start.68) | collective-permute-done | bytes 327712 | tf_op jit(solution)/shard_map/cond/branch_1_fun/ppermute | solution.py:244
  46.4 1.6 %collective-permute-start.74 = (bf16[384,640]{1,0:T(8,128)(2,1)S(1)}, bf16[384,640]{1,0:T(8,128)(2,1)S(1)}, u32[]{:S(2)}, u32[]{:S(2)}) collective-permute-start(bf16[384,640]{1,0:T(8,128)(2,1)S(1)} %pack_part.15.refs_5_), channel_id=1, source_target_pairs={{0,8},{8,0},{16,24},{24,16},{1,9},{9,1},{17,25},{25,17},{2,10},{10... | collective-permute-start | bytes 1474568 | tf_op jit(solution)/shard_map/cond/branch_1_fun/ppermute | solution.py:244
  48.0 1.5 %collective-permute-start.75 = (bf16[384,640]{1,0:T(8,128)(2,1)S(1)}, bf16[384,640]{1,0:T(8,128)(2,1)S(1)}, u32[]{:S(2)}, u32[]{:S(2)}) collective-permute-start(bf16[384,640]{1,0:T(8,128)(2,1)S(1)} %pack_part.15.refs_5_), channel_id=1, source_target_pairs={{0,16},{8,24},{16,0},{24,8},{1,17},{9,25},{17,1},{25,9},{2,18},{10... | collective-permute-start | bytes 1474568 | tf_op jit(solution)/shard_map/cond/branch_1_fun/ppermute | solution.py:244
  49.5 5.9 %collective-permute-done.67.refs_0_ = bf16[256,384]{1,0:T(8,128)(2,1)S(1)} collective-permute-done((bf16[256,384]{1,0:T(8,128)(2,1)S(1)}, bf16[256,384]{1,0:T(8,128)(2,1)S(1)}, u32[]{:S(2)}, u32[]{:S(2)}) %collective-permute-start.67) | collective-permute-done | bytes 196640 | tf_op jit(solution)/shard_map/cond/branch_1_fun/ppermute | solution.py:244
  55.5 2.6 %collective-permute-start.78 = (bf16[512,384]{1,0:T(8,128)(2,1)S(1)}, bf16[512,384]{1,0:T(8,128)(2,1)S(1)}, u32[]{:S(2)}, u32[]{:S(2)}) collective-permute-start(bf16[512,384]{1,0:T(8,128)(2,1)S(1)} %get-tuple-element.222), channel_id=1, source_target_pairs={{0,4},{1,5},{2,6},{3,7},{4,0},{5,1},{6,2},{7,3},{8,12},{9,13},{10,... | collective-permute-start | bytes 1179656 | tf_op jit(solution)/shard_map/cond/branch_1_fun/ppermute | solution.py:244
  59.3 1.6 %collective-permute-start.76 = (bf16[384,640]{1,0:T(8,128)(2,1)S(1)}, bf16[384,640]{1,0:T(8,128)(2,1)S(1)}, u32[]{:S(2)}, u32[]{:S(2)}) collective-permute-start(bf16[384,640]{1,0:T(8,128)(2,1)S(1)} %collective-permute-done.70.refs_6_), channel_id=1, source_target_pairs={{0,16},{8,24},{16,0},{24,8},{1,17},{9,25},{17,1},{25,9},{2,18},{10... | collective-permute-start | bytes 1474568 | tf_op jit(solution)/shard_map/cond/branch_1_fun/ppermute | solution.py:244
  60.9 1.5 %collective-permute-start.77 = (bf16[384,640]{1,0:T(8,128)(2,1)S(1)}, bf16[384,640]{1,0:T(8,128)(2,1)S(1)}, u32[]{:S(2)}, u32[]{:S(2)}) collective-permute-start(bf16[384,640]{1,0:T(8,128)(2,1)S(1)} %collective-permute-done.75.refs_9_), channel_id=1, source_target_pairs={{0,8},{8,0},{16,24},{24,16},{1,9},{9,1},{17,25},{25,17},{2,10},{10... | collective-permute-start | bytes 1474568 | tf_op jit(solution)/shard_map/cond/branch_1_fun/ppermute | solution.py:244
  62.4 6.6 %collective-permute-start.79 = (bf16[256,384]{1,0:T(8,128)(2,1)S(1)}, bf16[256,384]{1,0:T(8,128)(2,1)S(1)}, u32[]{:S(2)}, u32[]{:S(2)}) collective-permute-start(bf16[256,384]{1,0:T(8,128)(2,1)S(1)} %collective-permute-done.67.refs_0_), channel_id=1, source_target_pairs={{0,2},{1,3},{2,0},{3,1},{4,6},{5,7},{6,4},{7,5},{8,10},{9,11},{10,... | collective-permute-start | bytes 589832 | tf_op jit(solution)/shard_map/cond/branch_1_fun/ppermute | solution.py:244
  69.0 7.4 %collective-permute-done.78.refs_1_ = bf16[512,384]{1,0:T(8,128)(2,1)S(1)} collective-permute-done((bf16[512,384]{1,0:T(8,128)(2,1)S(1)}, bf16[512,384]{1,0:T(8,128)(2,1)S(1)}, u32[]{:S(2)}, u32[]{:S(2)}) %collective-permute-start.78) | collective-permute-done | bytes 393248 | tf_op jit(solution)/shard_map/cond/branch_1_fun/ppermute | solution.py:244
  76.4 2.0 %collective-permute-done.79.refs_0_ = bf16[256,384]{1,0:T(8,128)(2,1)S(1)} collective-permute-done((bf16[256,384]{1,0:T(8,128)(2,1)S(1)}, bf16[256,384]{1,0:T(8,128)(2,1)S(1)}, u32[]{:S(2)}, u32[]{:S(2)}) %collective-permute-start.79) | collective-permute-done | bytes 196640 | tf_op jit(solution)/shard_map/cond/branch_1_fun/ppermute | solution.py:244
  78.5 6.4 %contract_near.7 = (f32[768,640]{1,0:T(8,128)S(1)}, bf16[4,384,640]{2,1,0:T(8,128)(2,1)S(1)}) custom-call(bf16[768,384]{1,0:T(8,128)(2,1)S(1)} %get-tuple-element.209.refs_0_, bf16[768,384]{1,0:T(8,128)(2,1)S(1)} %collective-permute-done.64.refs_1_, bf16[768,384]{1,0:T(8,128)(2,1)S(1)} %collective-permute-done.66.refs_2_, ...), custom_call_target="tpu_custom_call" | custom-call | flops 1509949440 | bytes 4325376 | tf_op jit(solution)/shard_map/cond/branch_1_fun/contract_near/pallas_call | solution.py:344
  86.2 3.8 %collective-permute-done.81.refs_1_ = bf16[512,384]{1,0:T(8,128)(2,1)S(1)} collective-permute-done((bf16[512,384]{1,0:T(8,128)(2,1)S(1)}, bf16[512,384]{1,0:T(8,128)(2,1)S(1)}, u32[]{:S(2)}, u32[]{:S(2)}) %collective-permute-start.81) | collective-permute-done | bytes 393248 | tf_op jit(solution)/shard_map/cond/branch_1_fun/ppermute | solution.py:244
  90.5 1.5 %collective-permute-done.82.refs_2_ = bf16[256,384]{1,0:T(8,128)(2,1)S(1)} collective-permute-done((bf16[256,384]{1,0:T(8,128)(2,1)S(1)}, bf16[256,384]{1,0:T(8,128)(2,1)S(1)}, u32[]{:S(2)}, u32[]{:S(2)}) %collective-permute-start.82) | collective-permute-done | bytes 196640 | tf_op jit(solution)/shard_map/cond/branch_1_fun/ppermute | solution.py:244
  92.0 3.4 %contract_last.7 = bf16[1024,768]{1,0:T(8,128)(2,1)S(1)} custom-call(f32[768,640]{1,0:T(8,128)S(1)} %contract_far.7.before, bf16[4,384,640]{2,1,0:T(8,128)(2,1)S(1)} %get-tuple-element.220.s_ref, bf16[1024,768]{1,0:T(8,128)(2,1)S(1)} %get-tuple-element.212.lam_hot, bf16[640,768]{1,0:T(8,128)(2,1)S(1)} %get-tuple-element.225.col_hot, ...), custom_call_target="tpu_custom_call" | custom-call | flops 754974720 | bytes 2162688 | tf_op jit(solution)/shard_map/cond/branch_1_fun/contract_last/pallas_call | solution.py:404
  (42 shorter events, 9.9 us)
Async XLA Ops:
  5.3 4.9 %copy-start.3 = (bf16[128,6144]{1,0:T(8,128)(2,1)S(1)}, bf16[128,6144]{1,0:T(8,128)(2,1)}, u32[]{:S(2)}) copy-start(bf16[128,6144]{1,0:T(8,128)(2,1)} %get-tuple-element.204.x_ref) | copy-start | bytes 4718596 | tf_op jit(solution)/shard_map/cond
  5.3 4.9 %copy-start.8 = (s32[4,48]{1,0:T(4,128)S(1)}, s32[4,48]{1,0:T(4,128)}, u32[]{:S(2)}) copy-start(s32[4,48]{1,0:T(4,128)} %get-tuple-element.203.mask_ref) | copy-start | bytes 2308 | tf_op jit(solution)/shard_map/cond
  5.3 4.9 %copy-start.16 = (s32[48]{0:T(128)S(1)}, s32[48]{0:T(128)}, u32[]{:S(2)}) copy-start(s32[48]{0:T(128)} %get-tuple-element.202.ri_ref) | copy-start | bytes 580 | tf_op jit(solution)/shard_map/cond
  5.3 4.9 %collective-permute-start.63 = (bf16[4,128,640]{2,1,0:T(8,128)(2,1)S(1)}, bf16[4,128,640]{2,1,0:T(8,128)(2,1)S(1)}, u32[]{:S(2)}, u32[]{:S(2)}) collective-permute-start(bf16[4,128,640]{2,1,0:T(8,128)(2,1)S(1)} %pack_other_core.7), channel_id=1, source_target_pairs={{0,1},{1,0},{2,3},{3,2},{4,5},{5,4},{6,7},{7,6},{8,9},{9,8},{10,11... | collective-permute-start | bytes 1966088 | tf_op jit(solution)/shard_map/cond/branch_1_fun/ppermute | solution.py:244
  9.9 11.0 %collective-permute-start.64 = (bf16[768,384]{1,0:T(8,128)(2,1)S(1)}, bf16[768,384]{1,0:T(8,128)(2,1)S(1)}, u32[]{:S(2)}, u32[]{:S(2)}) collective-permute-start(bf16[768,384]{1,0:T(8,128)(2,1)S(1)} %get-tuple-element.209.refs_0_), channel_id=1, source_target_pairs={{0,1},{1,0},{2,3},{3,2},{4,5},{5,4},{6,7},{7,6},{8,9},{9,8},{10,11... | collective-permute-start | bytes 1769480 | tf_op jit(solution)/shard_map/cond/branch_1_fun/ppermute | solution.py:244
  12.4 17.4 %collective-permute-start.65 = (bf16[256,640]{1,0:T(8,128)(2,1)S(1)}, bf16[256,640]{1,0:T(8,128)(2,1)S(1)}, u32[]{:S(2)}, u32[]{:S(2)}) collective-permute-start(bf16[256,640]{1,0:T(8,128)(2,1)S(1)} %get-tuple-element.208), channel_id=1, source_target_pairs={{0,2},{1,3},{2,0},{3,1},{4,6},{5,7},{6,4},{7,5},{8,10},{9,11},{10,... | collective-permute-start | bytes 983048 | tf_op jit(solution)/shard_map/cond/branch_1_fun/ppermute | solution.py:244
  15.4 29.8 %collective-permute-start.68 = (bf16[256,640]{1,0:T(8,128)(2,1)S(1)}, bf16[256,640]{1,0:T(8,128)(2,1)S(1)}, u32[]{:S(2)}, u32[]{:S(2)}) collective-permute-start(bf16[256,640]{1,0:T(8,128)(2,1)S(1)} %get-tuple-element.211), channel_id=1, source_target_pairs={{0,4},{1,5},{2,6},{3,7},{4,0},{5,1},{6,2},{7,3},{8,12},{9,13},{10,... | collective-permute-start | bytes 983048 | tf_op jit(solution)/shard_map/cond/branch_1_fun/ppermute | solution.py:244
  18.0 27.2 %collective-permute-start.69 = (bf16[256,640]{1,0:T(8,128)(2,1)S(1)}, bf16[256,640]{1,0:T(8,128)(2,1)S(1)}, u32[]{:S(2)}, u32[]{:S(2)}) collective-permute-start(bf16[256,640]{1,0:T(8,128)(2,1)S(1)} %get-tuple-element.214), channel_id=1, source_target_pairs={{0,6},{1,7},{2,4},{3,5},{4,2},{5,3},{6,0},{7,1},{8,14},{9,15},{10,... | collective-permute-start | bytes 983048 | tf_op jit(solution)/shard_map/cond/branch_1_fun/ppermute | solution.py:244
  18.0 37.5 %collective-permute-start.67 = (bf16[256,384]{1,0:T(8,128)(2,1)S(1)}, bf16[256,384]{1,0:T(8,128)(2,1)S(1)}, u32[]{:S(2)}, u32[]{:S(2)}) collective-permute-start(bf16[256,384]{1,0:T(8,128)(2,1)S(1)} %get-tuple-element.210), channel_id=1, source_target_pairs={{0,4},{1,5},{2,6},{3,7},{4,0},{5,1},{6,2},{7,3},{8,12},{9,13},{10,... | collective-permute-start | bytes 589832 | tf_op jit(solution)/shard_map/cond/branch_1_fun/ppermute | solution.py:244
  31.0 15.4 %collective-permute-start.70 = (bf16[384,640]{1,0:T(8,128)(2,1)S(1)}, bf16[384,640]{1,0:T(8,128)(2,1)S(1)}, u32[]{:S(2)}, u32[]{:S(2)}) collective-permute-start(bf16[384,640]{1,0:T(8,128)(2,1)S(1)} %pack_part.14.refs_4_), channel_id=1, source_target_pairs={{0,8},{8,0},{16,24},{24,16},{1,9},{9,1},{17,25},{25,17},{2,10},{10... | collective-permute-start | bytes 1474568 | tf_op jit(solution)/shard_map/cond/branch_1_fun/ppermute | solution.py:244
  32.7 13.7 %collective-permute-start.71 = (bf16[384,640]{1,0:T(8,128)(2,1)S(1)}, bf16[384,640]{1,0:T(8,128)(2,1)S(1)}, u32[]{:S(2)}, u32[]{:S(2)}) collective-permute-start(bf16[384,640]{1,0:T(8,128)(2,1)S(1)} %pack_part.14.refs_4_), channel_id=1, source_target_pairs={{0,16},{8,24},{16,0},{24,8},{1,17},{9,25},{17,1},{25,9},{2,18},{10... | collective-permute-start | bytes 1474568 | tf_op jit(solution)/shard_map/cond/branch_1_fun/ppermute | solution.py:244
  45.2 14.1 %collective-permute-start.66 = (bf16[768,384]{1,0:T(8,128)(2,1)S(1)}, bf16[768,384]{1,0:T(8,128)(2,1)S(1)}, u32[]{:S(2)}, u32[]{:S(2)}) collective-permute-start(bf16[768,384]{1,0:T(8,128)(2,1)S(1)} %get-tuple-element.209.refs_0_), channel_id=1, source_target_pairs={{0,2},{1,3},{2,0},{3,1},{4,6},{5,7},{6,4},{7,5},{8,10},{9,11},{10,... | collective-permute-start | bytes 1769480 | tf_op jit(solution)/shard_map/cond/branch_1_fun/ppermute | solution.py:244
  46.4 12.9 %collective-permute-start.74 = (bf16[384,640]{1,0:T(8,128)(2,1)S(1)}, bf16[384,640]{1,0:T(8,128)(2,1)S(1)}, u32[]{:S(2)}, u32[]{:S(2)}) collective-permute-start(bf16[384,640]{1,0:T(8,128)(2,1)S(1)} %pack_part.15.refs_5_), channel_id=1, source_target_pairs={{0,8},{8,0},{16,24},{24,16},{1,9},{9,1},{17,25},{25,17},{2,10},{10... | collective-permute-start | bytes 1474568 | tf_op jit(solution)/shard_map/cond/branch_1_fun/ppermute | solution.py:244
  48.0 11.3 %collective-permute-start.75 = (bf16[384,640]{1,0:T(8,128)(2,1)S(1)}, bf16[384,640]{1,0:T(8,128)(2,1)S(1)}, u32[]{:S(2)}, u32[]{:S(2)}) collective-permute-start(bf16[384,640]{1,0:T(8,128)(2,1)S(1)} %pack_part.15.refs_5_), channel_id=1, source_target_pairs={{0,16},{8,24},{16,0},{24,8},{1,17},{9,25},{17,1},{25,9},{2,18},{10... | collective-permute-start | bytes 1474568 | tf_op jit(solution)/shard_map/cond/branch_1_fun/ppermute | solution.py:244
  55.5 3.8 %collective-permute-start.72 = (bf16[256,384]{1,0:T(8,128)(2,1)S(1)}, bf16[256,384]{1,0:T(8,128)(2,1)S(1)}, u32[]{:S(2)}, u32[]{:S(2)}) collective-permute-start(bf16[256,384]{1,0:T(8,128)(2,1)S(1)} %collective-permute-done.67.refs_0_), channel_id=1, source_target_pairs={{0,1},{1,0},{2,3},{3,2},{4,5},{5,4},{6,7},{7,6},{8,9},{9,8},{10,11... | collective-permute-start | bytes 589832 | tf_op jit(solution)/shard_map/cond/branch_1_fun/ppermute | solution.py:244
  55.5 21.0 %collective-permute-start.78 = (bf16[512,384]{1,0:T(8,128)(2,1)S(1)}, bf16[512,384]{1,0:T(8,128)(2,1)S(1)}, u32[]{:S(2)}, u32[]{:S(2)}) collective-permute-start(bf16[512,384]{1,0:T(8,128)(2,1)S(1)} %get-tuple-element.222), channel_id=1, source_target_pairs={{0,4},{1,5},{2,6},{3,7},{4,0},{5,1},{6,2},{7,3},{8,12},{9,13},{10,... | collective-permute-start | bytes 1179656 | tf_op jit(solution)/shard_map/cond/branch_1_fun/ppermute | solution.py:244
  59.3 19.1 %collective-permute-start.73 = (bf16[768,384]{1,0:T(8,128)(2,1)S(1)}, bf16[768,384]{1,0:T(8,128)(2,1)S(1)}, u32[]{:S(2)}, u32[]{:S(2)}) collective-permute-start(bf16[768,384]{1,0:T(8,128)(2,1)S(1)} %collective-permute-done.66.refs_2_), channel_id=1, source_target_pairs={{0,1},{1,0},{2,3},{3,2},{4,5},{5,4},{6,7},{7,6},{8,9},{9,8},{10,11... | collective-permute-start | bytes 1769480 | tf_op jit(solution)/shard_map/cond/branch_1_fun/ppermute | solution.py:244
  59.3 19.1 %collective-permute-start.76 = (bf16[384,640]{1,0:T(8,128)(2,1)S(1)}, bf16[384,640]{1,0:T(8,128)(2,1)S(1)}, u32[]{:S(2)}, u32[]{:S(2)}) collective-permute-start(bf16[384,640]{1,0:T(8,128)(2,1)S(1)} %collective-permute-done.70.refs_6_), channel_id=1, source_target_pairs={{0,16},{8,24},{16,0},{24,8},{1,17},{9,25},{17,1},{25,9},{2,18},{10... | collective-permute-start | bytes 1474568 | tf_op jit(solution)/shard_map/cond/branch_1_fun/ppermute | solution.py:244
  60.9 17.5 %collective-permute-start.77 = (bf16[384,640]{1,0:T(8,128)(2,1)S(1)}, bf16[384,640]{1,0:T(8,128)(2,1)S(1)}, u32[]{:S(2)}, u32[]{:S(2)}) collective-permute-start(bf16[384,640]{1,0:T(8,128)(2,1)S(1)} %collective-permute-done.75.refs_9_), channel_id=1, source_target_pairs={{0,8},{8,0},{16,24},{24,16},{1,9},{9,1},{17,25},{25,17},{2,10},{10... | collective-permute-start | bytes 1474568 | tf_op jit(solution)/shard_map/cond/branch_1_fun/ppermute | solution.py:244
  62.4 16.0 %collective-permute-start.79 = (bf16[256,384]{1,0:T(8,128)(2,1)S(1)}, bf16[256,384]{1,0:T(8,128)(2,1)S(1)}, u32[]{:S(2)}, u32[]{:S(2)}) collective-permute-start(bf16[256,384]{1,0:T(8,128)(2,1)S(1)} %collective-permute-done.67.refs_0_), channel_id=1, source_target_pairs={{0,2},{1,3},{2,0},{3,1},{4,6},{5,7},{6,4},{7,5},{8,10},{9,11},{10,... | collective-permute-start | bytes 589832 | tf_op jit(solution)/shard_map/cond/branch_1_fun/ppermute | solution.py:244
  78.4 6.5 %collective-permute-start.80 = (bf16[512,384]{1,0:T(8,128)(2,1)S(1)}, bf16[512,384]{1,0:T(8,128)(2,1)S(1)}, u32[]{:S(2)}, u32[]{:S(2)}) collective-permute-start(bf16[512,384]{1,0:T(8,128)(2,1)S(1)} %collective-permute-done.78.refs_1_), channel_id=1, source_target_pairs={{0,1},{1,0},{2,3},{3,2},{4,5},{5,4},{6,7},{7,6},{8,9},{9,8},{10,11... | collective-permute-start | bytes 1179656 | tf_op jit(solution)/shard_map/cond/branch_1_fun/ppermute | solution.py:244
  78.4 11.5 %collective-permute-start.81 = (bf16[512,384]{1,0:T(8,128)(2,1)S(1)}, bf16[512,384]{1,0:T(8,128)(2,1)S(1)}, u32[]{:S(2)}, u32[]{:S(2)}) collective-permute-start(bf16[512,384]{1,0:T(8,128)(2,1)S(1)} %collective-permute-done.78.refs_1_), channel_id=1, source_target_pairs={{0,2},{1,3},{2,0},{3,1},{4,6},{5,7},{6,4},{7,5},{8,10},{9,11},{10,... | collective-permute-start | bytes 1179656 | tf_op jit(solution)/shard_map/cond/branch_1_fun/ppermute | solution.py:244
  90.0 2.0 %collective-permute-start.83 = (bf16[512,384]{1,0:T(8,128)(2,1)S(1)}, bf16[512,384]{1,0:T(8,128)(2,1)S(1)}, u32[]{:S(2)}, u32[]{:S(2)}) collective-permute-start(bf16[512,384]{1,0:T(8,128)(2,1)S(1)} %collective-permute-done.81.refs_1_), channel_id=1, source_target_pairs={{0,1},{1,0},{2,3},{3,2},{4,5},{5,4},{6,7},{7,6},{8,9},{9,8},{10,11... | collective-permute-start | bytes 1179656 | tf_op jit(solution)/shard_map/cond/branch_1_fun/ppermute | solution.py:244
  90.0 2.0 %collective-permute-start.82 = (bf16[256,384]{1,0:T(8,128)(2,1)S(1)}, bf16[256,384]{1,0:T(8,128)(2,1)S(1)}, u32[]{:S(2)}, u32[]{:S(2)}) collective-permute-start(bf16[256,384]{1,0:T(8,128)(2,1)S(1)} %collective-permute-done.79.refs_0_), channel_id=1, source_target_pairs={{0,1},{1,0},{2,3},{3,2},{4,5},{5,4},{6,7},{7,6},{8,9},{9,8},{10,11... | collective-permute-start | bytes 589832 | tf_op jit(solution)/shard_map/cond/branch_1_fun/ppermute | solution.py:244
  (3 other events, 8.4 us)

commit v2 on v1

--- a/solution.py
+++ b/solution.py
@@ -48,7 +48,7 @@
     return pl.ds(i * size if isinstance(i, int) else pl.multiple_of(i * size, size), size)
 
 
-def place_row(count_ref, base, atoms, width):
+def place_row(count_ref, base, atoms, width, unroll):
     lane = iota((1, atoms * width), 1)
 
     def atom(a, carry):
@@ -57,20 +57,26 @@
         inside = (lane >= a * width) & (lane < a * width + count)
         return jnp.where(inside, lane - a * width + offset, place), offset + count
 
-    return lax.fori_loop(0, atoms, atom, (jnp.full(lane.shape, -1, jnp.int32), jnp.int32(0)))[0]
-
-
-def pack_rows(count_ref, base, atoms, width, size):
-    place = place_row(count_ref, base, atoms, width)
+    carry = (jnp.full(lane.shape, -1, jnp.int32), jnp.int32(0))
+    if not unroll:
+        return lax.fori_loop(0, atoms, atom, carry)[0]
+    for a in range(atoms):
+        carry = atom(a, carry)
+    return carry[0]
+
+
+def pack_rows(count_ref, base, atoms, width, size, unroll):
+    place = place_row(count_ref, base, atoms, width, unroll)
     return ones_where(iota((size, atoms * width), 0) == place)
 
 
 def pack_cols(count_ref, base, atoms, width, size, out, unroll):
     def atom(a, offset):
         count = count_ref[base + a]
-        slot = iota((width, size), 0)
-        gap = iota((width, size), 1) - slot
-        out[span(a, width), :] = ones_where((gap == offset) & (slot < count))
+        lanes = min(size, (a + 1) * width) if unroll and width % 128 == 0 else size
+        slot = iota((width, lanes), 0)
+        gap = iota((width, lanes), 1) - slot
+        out[span(a, width), pl.ds(0, lanes)] = ones_where((gap == offset) & (slot < count))
         return offset + count
 
     if unroll:
@@ -119,6 +125,7 @@
         made = outs[0] if first else refs[-1]
         row, col = lax.axis_index("row"), lax.axis_index("col")
         base = (row * ncols + col) * atoms
+        hot[...] = jnp.zeros_like(hot)
 
         @loop(chips, unroll)
         def _(t):
@@ -184,7 +191,7 @@
             x = jnp.where(kept > 0.5, x_ref[at, :].astype(F32), 0.0).astype(BF16)
             mid[at, :] = jnp.dot(x, hot[...], preferred_element_type=F32).astype(BF16)
 
-        place = place_row(count_ref, row * lam_atoms, lam_atoms, BW)
+        place = place_row(count_ref, row * lam_atoms, lam_atoms, BW, unroll)
 
         @loop(steps, unroll)
         def _(i):
@@ -211,7 +218,7 @@
     )(basis_count, mask, dens)
 
 
-def pack_part(pieces, basis_count, first, ncols, size):
+def pack_part(pieces, basis_count, first, ncols, size, unroll):
     rows, cols = pieces[0].shape
     per = len(pieces)
     depth = per * rows
@@ -224,7 +231,7 @@
             at = lax.rem(chip ^ (first + i), per) * rows
             full[pl.ds(pl.multiple_of(at, rows), rows), :] = blocks[i][...]
         part = (row * (ncols // CORES) + (chip ^ first)) * rows // depth
-        hot = pack_rows(count_ref, part * atoms, atoms, BW, size)
+        hot = pack_rows(count_ref, part * atoms, atoms, BW, size, unroll)
         o_ref[...] = jnp.dot(hot, full[...], preferred_element_type=F32).astype(BF16)
 
     return pl.pallas_call(
@@ -294,7 +301,7 @@
     def body(count_ref, ri_ref, lam_hot, col_hot):
         row, col = lax.axis_index("row"), lax.axis_index("col")
         pack_cols(count_ref, row * lam_atoms, lam_atoms, BW, lam, lam_hot, unroll)
-        place = place_row(ri_ref, col * blocks, blocks, RW)
+        place = place_row(ri_ref, col * blocks, blocks, RW, unroll)
 
         @loop(cols // RW, unroll)
         def _(i):
@@ -445,7 +452,7 @@
                 arrived = [after(arrived[0], near[1])] + arrived[1:]
             elif g == 1:
                 arrived = [after(arrived[0], lam_hot)] + arrived[1:]
-            part = pack_part(arrived, basis_count, g * per, ncols, sum_size)
+            part = pack_part(arrived, basis_count, g * per, ncols, sum_size, unroll)
             if g == 0:
                 near.update(double(after(own, part), "col", near_bits))
                 steps = [near[far] for far in near if far > 1]

time: 97 us -> 96.1 us (level)
  transfers between devices with their start and end apart: 21 -> 21, of which waited for: 8 -> 8; matrix products, arithmetic and copies ran while one was open for 0% -> 0% of each run, Pallas kernels for 18% -> 17%
where the time goes in v2:
time: 96.1 us; the launch traced here: 95.9 us
  waiting for transfers between devices  41.7 us (43%)
  starting transfers between devices  27.2 us (28%)
  Pallas kernels  24.4 us (25%)
  local copies, waits for them, and re-layouts  1.24 us (1%)
    ppermute x21, waiting for transfers between devices, exchange(): return lax.ppermute(x, axis, [(i, i ^ bit) for i in range(peers)])  41.7 us
    ppermute x21, starting transfers between devices, exchange(): return lax.ppermute(x, axis, [(i, i ^ bit) for i in range(peers)])  27.2 us
    pallas_call x1, Pallas kernels, contract_near(): pl.pallas_call(body, out_shape=[jax.ShapeDtypeStruct((lam, cols), F32), j...  6.69 us
    pallas_call x2, Pallas kernels, pack_integrals(): pl.pallas_call(body, out_shape=out_shape, in_specs=[SMEM_SPEC, SMEM_SPEC,...  4.97 us
    pallas_call x1, Pallas kernels, contract_last(): pl.pallas_call(body, out_shape=jax.ShapeDtypeStruct((rows, wide), BF16),...  3.42 us
    pallas_call x1, Pallas kernels, pack_density(): pl.pallas_call(body, out_shape=[jax.ShapeDtypeStruct((n, sum_size), BF16)...  3.39 us
    pallas_call x2, Pallas kernels, pack_part(): pl.pallas_call(body, out_shape=jax.ShapeDtypeStruct((size, cols), BF16),...  2.24 us
  transfers between devices with their start and end apart: 21, of which 8 were waited for; matrix products, arithmetic and copies ran while one was open for 0% of the time, Pallas kernels for 17%

profile of v2, /device:TPU:0, one launch (start us, length us, event | category | flops | bytes accessed | tf_op | source)
XLA Modules:
  0.0 95.9 jit_solution(4557573181688317825)
XLA Ops:
  2.0 92.8 %conditional.3 = (bf16[1024,768]{1,0:T(8,128)(2,1)S(1)}) conditional(s32[]{:T(128)} %convert_element_type.9, (s32[]{:T(128)}, s32[128]{0:T(128)}, s32[32,16]{0,1:T(8,128)}, bf16[1024,512]{1,0:T(8,128)(2,1)}, s32[48]{0:T(128)}, /*index=5*/s32[4,48]{1,0:T(4,128)}, bf16[128,6144]{1,0:T(8,128)(2,1)}) %tuple.74, (s32[128]{0:T(128)}, s32[32,16]{0,1:T(8,128)}, ...), branch_computations={%region_0.0_spmd, %region_5.0_spmd} | conditional | flops 26172456960 | bytes 89402256 | solution.py:499
  2.2 2.9 %pack_other_core.7 = bf16[4,128,640]{2,1,0:T(8,128)(2,1)S(1)} custom-call(s32[128]{0:T(128)} %get-tuple-element.198.count_ref, s32[48]{0:T(128)} %get-tuple-element.202.ri_ref, s32[4,48]{1,0:T(4,128)} %get-tuple-element.203.mask_ref, bf16[128,6144]{1,0:T(8,128)(2,1)} %get-tuple-element.204.x_ref), custom_call_target="tpu_custom_call" | custom-call | flops 503316480 | bytes 1769472 | tf_op jit(solution)/shard_map/cond/branch_1_fun/pack_other_core/pallas_call | solution.py:156
  5.8 3.4 %pack_density.7 = (bf16[768,384]{1,0:T(8,128)(2,1)S(1)}, bf16[256,384]{1,0:T(8,128)(2,1)S(1)}, bf16[512,384]{1,0:T(8,128)(2,1)S(1)}) custom-call(s32[128]{0:T(128)S(1)} %copy-done.12, s32[32,16]{1,0:T(8,128)S(1)} %copy.10.mask_ref, bf16[1024,512]{1,0:T(8,128)(2,1)} %get-tuple-element.200.x_ref), custom_call_target="tpu_custom_call" | custom-call | flops 1006632960 | bytes 1048576 | tf_op jit(solution)/shard_map/cond/branch_1_fun/pack_density/pallas_call | solution.py:205
  9.4 2.1 %pack_own_core.7 = (bf16[256,640]{1,0:T(8,128)(2,1)S(1)}, bf16[256,640]{1,0:T(8,128)(2,1)S(1)}, bf16[256,640]{1,0:T(8,128)(2,1)S(1)}, bf16[256,640]{1,0:T(8,128)(2,1)S(1)}) custom-call(s32[128]{0:T(128)S(1)} %copy-done.12, s32[48]{0:T(128)S(1)} %copy-done.16, s32[4,48]{1,0:T(4,128)S(1)} %copy-done.8, bf16[128,6144]{1,0:T(8,128)(2,1)S(1)} %copy-done.3, ...), custom_call_target="tpu_custom_call" | custom-call | flops 503316480 | bytes 1769472 | tf_op jit(solution)/shard_map/cond/branch_1_fun/pack_own_core/pallas_call | solution.py:156
  11.5 3.0 %collective-permute-start.65 = (bf16[256,640]{1,0:T(8,128)(2,1)S(1)}, bf16[256,640]{1,0:T(8,128)(2,1)S(1)}, u32[]{:S(2)}, u32[]{:S(2)}) collective-permute-start(bf16[256,640]{1,0:T(8,128)(2,1)S(1)} %get-tuple-element.208), channel_id=1, source_target_pairs={{0,2},{1,3},{2,0},{3,1},{4,6},{5,7},{6,4},{7,5},{8,10},{9,11},{10,... | collective-permute-start | bytes 983048 | tf_op jit(solution)/shard_map/cond/branch_1_fun/ppermute | solution.py:251
  14.5 2.6 %collective-permute-start.68 = (bf16[256,640]{1,0:T(8,128)(2,1)S(1)}, bf16[256,640]{1,0:T(8,128)(2,1)S(1)}, u32[]{:S(2)}, u32[]{:S(2)}) collective-permute-start(bf16[256,640]{1,0:T(8,128)(2,1)S(1)} %get-tuple-element.211), channel_id=1, source_target_pairs={{0,4},{1,5},{2,6},{3,7},{4,0},{5,1},{6,2},{7,3},{8,12},{9,13},{10,... | collective-permute-start | bytes 983048 | tf_op jit(solution)/shard_map/cond/branch_1_fun/ppermute | solution.py:251
  17.1 1.9 %collective-permute-start.67 = (bf16[256,384]{1,0:T(8,128)(2,1)S(1)}, bf16[256,384]{1,0:T(8,128)(2,1)S(1)}, u32[]{:S(2)}, u32[]{:S(2)}) collective-permute-start(bf16[256,384]{1,0:T(8,128)(2,1)S(1)} %get-tuple-element.210), channel_id=1, source_target_pairs={{0,4},{1,5},{2,6},{3,7},{4,0},{5,1},{6,2},{7,3},{8,12},{9,13},{10,... | collective-permute-start | bytes 589832 | tf_op jit(solution)/shard_map/cond/branch_1_fun/ppermute | solution.py:251
  20.0 8.9 %collective-permute-done.65.refs_1_ = bf16[256,640]{1,0:T(8,128)(2,1)S(1)} collective-permute-done((bf16[256,640]{1,0:T(8,128)(2,1)S(1)}, bf16[256,640]{1,0:T(8,128)(2,1)S(1)}, u32[]{:S(2)}, u32[]{:S(2)}) %collective-permute-start.65) | collective-permute-done | bytes 327712 | tf_op jit(solution)/shard_map/cond/branch_1_fun/ppermute | solution.py:251
  30.0 1.7 %collective-permute-start.70 = (bf16[384,640]{1,0:T(8,128)(2,1)S(1)}, bf16[384,640]{1,0:T(8,128)(2,1)S(1)}, u32[]{:S(2)}, u32[]{:S(2)}) collective-permute-start(bf16[384,640]{1,0:T(8,128)(2,1)S(1)} %pack_part.14.refs_4_), channel_id=1, source_target_pairs={{0,8},{8,0},{16,24},{24,16},{1,9},{9,1},{17,25},{25,17},{2,10},{10... | collective-permute-start | bytes 1474568 | tf_op jit(solution)/shard_map/cond/branch_1_fun/ppermute | solution.py:251
  31.7 1.5 %collective-permute-start.71 = (bf16[384,640]{1,0:T(8,128)(2,1)S(1)}, bf16[384,640]{1,0:T(8,128)(2,1)S(1)}, u32[]{:S(2)}, u32[]{:S(2)}) collective-permute-start(bf16[384,640]{1,0:T(8,128)(2,1)S(1)} %pack_part.14.refs_4_), channel_id=1, source_target_pairs={{0,16},{8,24},{16,0},{24,8},{1,17},{9,25},{17,1},{25,9},{2,18},{10... | collective-permute-start | bytes 1474568 | tf_op jit(solution)/shard_map/cond/branch_1_fun/ppermute | solution.py:251
  33.3 11.0 %collective-permute-done.68.refs_0_ = bf16[256,640]{1,0:T(8,128)(2,1)S(1)} collective-permute-done((bf16[256,640]{1,0:T(8,128)(2,1)S(1)}, bf16[256,640]{1,0:T(8,128)(2,1)S(1)}, u32[]{:S(2)}, u32[]{:S(2)}) %collective-permute-start.68) | collective-permute-done | bytes 327712 | tf_op jit(solution)/shard_map/cond/branch_1_fun/ppermute | solution.py:251
  45.4 1.6 %collective-permute-start.74 = (bf16[384,640]{1,0:T(8,128)(2,1)S(1)}, bf16[384,640]{1,0:T(8,128)(2,1)S(1)}, u32[]{:S(2)}, u32[]{:S(2)}) collective-permute-start(bf16[384,640]{1,0:T(8,128)(2,1)S(1)} %pack_part.15.refs_5_), channel_id=1, source_target_pairs={{0,8},{8,0},{16,24},{24,16},{1,9},{9,1},{17,25},{25,17},{2,10},{10... | collective-permute-start | bytes 1474568 | tf_op jit(solution)/shard_map/cond/branch_1_fun/ppermute | solution.py:251
  47.0 1.5 %collective-permute-start.75 = (bf16[384,640]{1,0:T(8,128)(2,1)S(1)}, bf16[384,640]{1,0:T(8,128)(2,1)S(1)}, u32[]{:S(2)}, u32[]{:S(2)}) collective-permute-start(bf16[384,640]{1,0:T(8,128)(2,1)S(1)} %pack_part.15.refs_5_), channel_id=1, source_target_pairs={{0,16},{8,24},{16,0},{24,8},{1,17},{9,25},{17,1},{25,9},{2,18},{10... | collective-permute-start | bytes 1474568 | tf_op jit(solution)/shard_map/cond/branch_1_fun/ppermute | solution.py:251
  48.5 6.0 %collective-permute-done.67.refs_0_ = bf16[256,384]{1,0:T(8,128)(2,1)S(1)} collective-permute-done((bf16[256,384]{1,0:T(8,128)(2,1)S(1)}, bf16[256,384]{1,0:T(8,128)(2,1)S(1)}, u32[]{:S(2)}, u32[]{:S(2)}) %collective-permute-start.67) | collective-permute-done | bytes 196640 | tf_op jit(solution)/shard_map/cond/branch_1_fun/ppermute | solution.py:251
  54.5 2.5 %collective-permute-start.78 = (bf16[512,384]{1,0:T(8,128)(2,1)S(1)}, bf16[512,384]{1,0:T(8,128)(2,1)S(1)}, u32[]{:S(2)}, u32[]{:S(2)}) collective-permute-start(bf16[512,384]{1,0:T(8,128)(2,1)S(1)} %get-tuple-element.222), channel_id=1, source_target_pairs={{0,4},{1,5},{2,6},{3,7},{4,0},{5,1},{6,2},{7,3},{8,12},{9,13},{10,... | collective-permute-start | bytes 1179656 | tf_op jit(solution)/shard_map/cond/branch_1_fun/ppermute | solution.py:251
  58.4 1.6 %collective-permute-start.76 = (bf16[384,640]{1,0:T(8,128)(2,1)S(1)}, bf16[384,640]{1,0:T(8,128)(2,1)S(1)}, u32[]{:S(2)}, u32[]{:S(2)}) collective-permute-start(bf16[384,640]{1,0:T(8,128)(2,1)S(1)} %collective-permute-done.70.refs_6_), channel_id=1, source_target_pairs={{0,16},{8,24},{16,0},{24,8},{1,17},{9,25},{17,1},{25,9},{2,18},{10... | collective-permute-start | bytes 1474568 | tf_op jit(solution)/shard_map/cond/branch_1_fun/ppermute | solution.py:251
  60.0 1.5 %collective-permute-start.77 = (bf16[384,640]{1,0:T(8,128)(2,1)S(1)}, bf16[384,640]{1,0:T(8,128)(2,1)S(1)}, u32[]{:S(2)}, u32[]{:S(2)}) collective-permute-start(bf16[384,640]{1,0:T(8,128)(2,1)S(1)} %collective-permute-done.75.refs_9_), channel_id=1, source_target_pairs={{0,8},{8,0},{16,24},{24,16},{1,9},{9,1},{17,25},{25,17},{2,10},{10... | collective-permute-start | bytes 1474568 | tf_op jit(solution)/shard_map/cond/branch_1_fun/ppermute | solution.py:251
  61.5 6.5 %collective-permute-start.79 = (bf16[256,384]{1,0:T(8,128)(2,1)S(1)}, bf16[256,384]{1,0:T(8,128)(2,1)S(1)}, u32[]{:S(2)}, u32[]{:S(2)}) collective-permute-start(bf16[256,384]{1,0:T(8,128)(2,1)S(1)} %collective-permute-done.67.refs_0_), channel_id=1, source_target_pairs={{0,2},{1,3},{2,0},{3,1},{4,6},{5,7},{6,4},{7,5},{8,10},{9,11},{10,... | collective-permute-start | bytes 589832 | tf_op jit(solution)/shard_map/cond/branch_1_fun/ppermute | solution.py:251
  68.0 7.5 %collective-permute-done.78.refs_1_ = bf16[512,384]{1,0:T(8,128)(2,1)S(1)} collective-permute-done((bf16[512,384]{1,0:T(8,128)(2,1)S(1)}, bf16[512,384]{1,0:T(8,128)(2,1)S(1)}, u32[]{:S(2)}, u32[]{:S(2)}) %collective-permute-start.78) | collective-permute-done | bytes 393248 | tf_op jit(solution)/shard_map/cond/branch_1_fun/ppermute | solution.py:251
  75.5 2.0 %collective-permute-done.79.refs_0_ = bf16[256,384]{1,0:T(8,128)(2,1)S(1)} collective-permute-done((bf16[256,384]{1,0:T(8,128)(2,1)S(1)}, bf16[256,384]{1,0:T(8,128)(2,1)S(1)}, u32[]{:S(2)}, u32[]{:S(2)}) %collective-permute-start.79) | collective-permute-done | bytes 196640 | tf_op jit(solution)/shard_map/cond/branch_1_fun/ppermute | solution.py:251
  77.5 6.7 %contract_near.7 = (f32[768,640]{1,0:T(8,128)S(1)}, bf16[4,384,640]{2,1,0:T(8,128)(2,1)S(1)}) custom-call(bf16[768,384]{1,0:T(8,128)(2,1)S(1)} %get-tuple-element.209.refs_0_, bf16[768,384]{1,0:T(8,128)(2,1)S(1)} %collective-permute-done.64.refs_1_, bf16[768,384]{1,0:T(8,128)(2,1)S(1)} %collective-permute-done.66.refs_2_, ...), custom_call_target="tpu_custom_call" | custom-call | flops 1509949440 | bytes 4325376 | tf_op jit(solution)/shard_map/cond/branch_1_fun/contract_near/pallas_call | solution.py:351
  85.5 3.5 %collective-permute-done.81.refs_1_ = bf16[512,384]{1,0:T(8,128)(2,1)S(1)} collective-permute-done((bf16[512,384]{1,0:T(8,128)(2,1)S(1)}, bf16[512,384]{1,0:T(8,128)(2,1)S(1)}, u32[]{:S(2)}, u32[]{:S(2)}) %collective-permute-start.81) | collective-permute-done | bytes 393248 | tf_op jit(solution)/shard_map/cond/branch_1_fun/ppermute | solution.py:251
  89.6 1.5 %collective-permute-done.82.refs_2_ = bf16[256,384]{1,0:T(8,128)(2,1)S(1)} collective-permute-done((bf16[256,384]{1,0:T(8,128)(2,1)S(1)}, bf16[256,384]{1,0:T(8,128)(2,1)S(1)}, u32[]{:S(2)}, u32[]{:S(2)}) %collective-permute-start.82) | collective-permute-done | bytes 196640 | tf_op jit(solution)/shard_map/cond/branch_1_fun/ppermute | solution.py:251
  91.0 3.4 %contract_last.7 = bf16[1024,768]{1,0:T(8,128)(2,1)S(1)} custom-call(f32[768,640]{1,0:T(8,128)S(1)} %contract_far.7.before, bf16[4,384,640]{2,1,0:T(8,128)(2,1)S(1)} %get-tuple-element.220.s_ref, bf16[1024,768]{1,0:T(8,128)(2,1)S(1)} %get-tuple-element.212.lam_hot, bf16[640,768]{1,0:T(8,128)(2,1)S(1)} %get-tuple-element.225.col_hot, ...), custom_call_target="tpu_custom_call" | custom-call | flops 754974720 | bytes 2162688 | tf_op jit(solution)/shard_map/cond/branch_1_fun/contract_last/pallas_call | solution.py:411
  (42 shorter events, 9.8 us)
Async XLA Ops:
  5.1 4.3 %copy-start.3 = (bf16[128,6144]{1,0:T(8,128)(2,1)S(1)}, bf16[128,6144]{1,0:T(8,128)(2,1)}, u32[]{:S(2)}) copy-start(bf16[128,6144]{1,0:T(8,128)(2,1)} %get-tuple-element.204.x_ref) | copy-start | bytes 4718596 | tf_op jit(solution)/shard_map/cond
  5.1 4.3 %copy-start.8 = (s32[4,48]{1,0:T(4,128)S(1)}, s32[4,48]{1,0:T(4,128)}, u32[]{:S(2)}) copy-start(s32[4,48]{1,0:T(4,128)} %get-tuple-element.203.mask_ref) | copy-start | bytes 2308 | tf_op jit(solution)/shard_map/cond
  5.1 4.3 %copy-start.16 = (s32[48]{0:T(128)S(1)}, s32[48]{0:T(128)}, u32[]{:S(2)}) copy-start(s32[48]{0:T(128)} %get-tuple-element.202.ri_ref) | copy-start | bytes 580 | tf_op jit(solution)/shard_map/cond
  5.2 4.2 %collective-permute-start.63 = (bf16[4,128,640]{2,1,0:T(8,128)(2,1)S(1)}, bf16[4,128,640]{2,1,0:T(8,128)(2,1)S(1)}, u32[]{:S(2)}, u32[]{:S(2)}) collective-permute-start(bf16[4,128,640]{2,1,0:T(8,128)(2,1)S(1)} %pack_other_core.7), channel_id=1, source_target_pairs={{0,1},{1,0},{2,3},{3,2},{4,5},{5,4},{6,7},{7,6},{8,9},{9,8},{10,11... | collective-permute-start | bytes 1966088 | tf_op jit(solution)/shard_map/cond/branch_1_fun/ppermute | solution.py:251
  9.1 10.9 %collective-permute-start.64 = (bf16[768,384]{1,0:T(8,128)(2,1)S(1)}, bf16[768,384]{1,0:T(8,128)(2,1)S(1)}, u32[]{:S(2)}, u32[]{:S(2)}) collective-permute-start(bf16[768,384]{1,0:T(8,128)(2,1)S(1)} %get-tuple-element.209.refs_0_), channel_id=1, source_target_pairs={{0,1},{1,0},{2,3},{3,2},{4,5},{5,4},{6,7},{7,6},{8,9},{9,8},{10,11... | collective-permute-start | bytes 1769480 | tf_op jit(solution)/shard_map/cond/branch_1_fun/ppermute | solution.py:251
  11.5 17.4 %collective-permute-start.65 = (bf16[256,640]{1,0:T(8,128)(2,1)S(1)}, bf16[256,640]{1,0:T(8,128)(2,1)S(1)}, u32[]{:S(2)}, u32[]{:S(2)}) collective-permute-start(bf16[256,640]{1,0:T(8,128)(2,1)S(1)} %get-tuple-element.208), channel_id=1, source_target_pairs={{0,2},{1,3},{2,0},{3,1},{4,6},{5,7},{6,4},{7,5},{8,10},{9,11},{10,... | collective-permute-start | bytes 983048 | tf_op jit(solution)/shard_map/cond/branch_1_fun/ppermute | solution.py:251
  14.5 29.8 %collective-permute-start.68 = (bf16[256,640]{1,0:T(8,128)(2,1)S(1)}, bf16[256,640]{1,0:T(8,128)(2,1)S(1)}, u32[]{:S(2)}, u32[]{:S(2)}) collective-permute-start(bf16[256,640]{1,0:T(8,128)(2,1)S(1)} %get-tuple-element.211), channel_id=1, source_target_pairs={{0,4},{1,5},{2,6},{3,7},{4,0},{5,1},{6,2},{7,3},{8,12},{9,13},{10,... | collective-permute-start | bytes 983048 | tf_op jit(solution)/shard_map/cond/branch_1_fun/ppermute | solution.py:251
  17.1 27.2 %collective-permute-start.69 = (bf16[256,640]{1,0:T(8,128)(2,1)S(1)}, bf16[256,640]{1,0:T(8,128)(2,1)S(1)}, u32[]{:S(2)}, u32[]{:S(2)}) collective-permute-start(bf16[256,640]{1,0:T(8,128)(2,1)S(1)} %get-tuple-element.214), channel_id=1, source_target_pairs={{0,6},{1,7},{2,4},{3,5},{4,2},{5,3},{6,0},{7,1},{8,14},{9,15},{10,... | collective-permute-start | bytes 983048 | tf_op jit(solution)/shard_map/cond/branch_1_fun/ppermute | solution.py:251
  17.1 37.5 %collective-permute-start.67 = (bf16[256,384]{1,0:T(8,128)(2,1)S(1)}, bf16[256,384]{1,0:T(8,128)(2,1)S(1)}, u32[]{:S(2)}, u32[]{:S(2)}) collective-permute-start(bf16[256,384]{1,0:T(8,128)(2,1)S(1)} %get-tuple-element.210), channel_id=1, source_target_pairs={{0,4},{1,5},{2,6},{3,7},{4,0},{5,1},{6,2},{7,3},{8,12},{9,13},{10,... | collective-permute-start | bytes 589832 | tf_op jit(solution)/shard_map/cond/branch_1_fun/ppermute | solution.py:251
  30.0 15.4 %collective-permute-start.70 = (bf16[384,640]{1,0:T(8,128)(2,1)S(1)}, bf16[384,640]{1,0:T(8,128)(2,1)S(1)}, u32[]{:S(2)}, u32[]{:S(2)}) collective-permute-start(bf16[384,640]{1,0:T(8,128)(2,1)S(1)} %pack_part.14.refs_4_), channel_id=1, source_target_pairs={{0,8},{8,0},{16,24},{24,16},{1,9},{9,1},{17,25},{25,17},{2,10},{10... | collective-permute-start | bytes 1474568 | tf_op jit(solution)/shard_map/cond/branch_1_fun/ppermute | solution.py:251
  31.7 13.7 %collective-permute-start.71 = (bf16[384,640]{1,0:T(8,128)(2,1)S(1)}, bf16[384,640]{1,0:T(8,128)(2,1)S(1)}, u32[]{:S(2)}, u32[]{:S(2)}) collective-permute-start(bf16[384,640]{1,0:T(8,128)(2,1)S(1)} %pack_part.14.refs_4_), channel_id=1, source_target_pairs={{0,16},{8,24},{16,0},{24,8},{1,17},{9,25},{17,1},{25,9},{2,18},{10... | collective-permute-start | bytes 1474568 | tf_op jit(solution)/shard_map/cond/branch_1_fun/ppermute | solution.py:251
  44.3 14.1 %collective-permute-start.66 = (bf16[768,384]{1,0:T(8,128)(2,1)S(1)}, bf16[768,384]{1,0:T(8,128)(2,1)S(1)}, u32[]{:S(2)}, u32[]{:S(2)}) collective-permute-start(bf16[768,384]{1,0:T(8,128)(2,1)S(1)} %get-tuple-element.209.refs_0_), channel_id=1, source_target_pairs={{0,2},{1,3},{2,0},{3,1},{4,6},{5,7},{6,4},{7,5},{8,10},{9,11},{10,... | collective-permute-start | bytes 1769480 | tf_op jit(solution)/shard_map/cond/branch_1_fun/ppermute | solution.py:251
  45.4 13.0 %collective-permute-start.74 = (bf16[384,640]{1,0:T(8,128)(2,1)S(1)}, bf16[384,640]{1,0:T(8,128)(2,1)S(1)}, u32[]{:S(2)}, u32[]{:S(2)}) collective-permute-start(bf16[384,640]{1,0:T(8,128)(2,1)S(1)} %pack_part.15.refs_5_), channel_id=1, source_target_pairs={{0,8},{8,0},{16,24},{24,16},{1,9},{9,1},{17,25},{25,17},{2,10},{10... | collective-permute-start | bytes 1474568 | tf_op jit(solution)/shard_map/cond/branch_1_fun/ppermute | solution.py:251
  47.0 11.4 %collective-permute-start.75 = (bf16[384,640]{1,0:T(8,128)(2,1)S(1)}, bf16[384,640]{1,0:T(8,128)(2,1)S(1)}, u32[]{:S(2)}, u32[]{:S(2)}) collective-permute-start(bf16[384,640]{1,0:T(8,128)(2,1)S(1)} %pack_part.15.refs_5_), channel_id=1, source_target_pairs={{0,16},{8,24},{16,0},{24,8},{1,17},{9,25},{17,1},{25,9},{2,18},{10... | collective-permute-start | bytes 1474568 | tf_op jit(solution)/shard_map/cond/branch_1_fun/ppermute | solution.py:251
  54.5 3.8 %collective-permute-start.72 = (bf16[256,384]{1,0:T(8,128)(2,1)S(1)}, bf16[256,384]{1,0:T(8,128)(2,1)S(1)}, u32[]{:S(2)}, u32[]{:S(2)}) collective-permute-start(bf16[256,384]{1,0:T(8,128)(2,1)S(1)} %collective-permute-done.67.refs_0_), channel_id=1, source_target_pairs={{0,1},{1,0},{2,3},{3,2},{4,5},{5,4},{6,7},{7,6},{8,9},{9,8},{10,11... | collective-permute-start | bytes 589832 | tf_op jit(solution)/shard_map/cond/branch_1_fun/ppermute | solution.py:251
  54.5 21.0 %collective-permute-start.78 = (bf16[512,384]{1,0:T(8,128)(2,1)S(1)}, bf16[512,384]{1,0:T(8,128)(2,1)S(1)}, u32[]{:S(2)}, u32[]{:S(2)}) collective-permute-start(bf16[512,384]{1,0:T(8,128)(2,1)S(1)} %get-tuple-element.222), channel_id=1, source_target_pairs={{0,4},{1,5},{2,6},{3,7},{4,0},{5,1},{6,2},{7,3},{8,12},{9,13},{10,... | collective-permute-start | bytes 1179656 | tf_op jit(solution)/shard_map/cond/branch_1_fun/ppermute | solution.py:251
  58.4 19.1 %collective-permute-start.73 = (bf16[768,384]{1,0:T(8,128)(2,1)S(1)}, bf16[768,384]{1,0:T(8,128)(2,1)S(1)}, u32[]{:S(2)}, u32[]{:S(2)}) collective-permute-start(bf16[768,384]{1,0:T(8,128)(2,1)S(1)} %collective-permute-done.66.refs_2_), channel_id=1, source_target_pairs={{0,1},{1,0},{2,3},{3,2},{4,5},{5,4},{6,7},{7,6},{8,9},{9,8},{10,11... | collective-permute-start | bytes 1769480 | tf_op jit(solution)/shard_map/cond/branch_1_fun/ppermute | solution.py:251
  58.4 19.1 %collective-permute-start.76 = (bf16[384,640]{1,0:T(8,128)(2,1)S(1)}, bf16[384,640]{1,0:T(8,128)(2,1)S(1)}, u32[]{:S(2)}, u32[]{:S(2)}) collective-permute-start(bf16[384,640]{1,0:T(8,128)(2,1)S(1)} %collective-permute-done.70.refs_6_), channel_id=1, source_target_pairs={{0,16},{8,24},{16,0},{24,8},{1,17},{9,25},{17,1},{25,9},{2,18},{10... | collective-permute-start | bytes 1474568 | tf_op jit(solution)/shard_map/cond/branch_1_fun/ppermute | solution.py:251
  60.0 17.5 %collective-permute-start.77 = (bf16[384,640]{1,0:T(8,128)(2,1)S(1)}, bf16[384,640]{1,0:T(8,128)(2,1)S(1)}, u32[]{:S(2)}, u32[]{:S(2)}) collective-permute-start(bf16[384,640]{1,0:T(8,128)(2,1)S(1)} %collective-permute-done.75.refs_9_), channel_id=1, source_target_pairs={{0,8},{8,0},{16,24},{24,16},{1,9},{9,1},{17,25},{25,17},{2,10},{10... | collective-permute-start | bytes 1474568 | tf_op jit(solution)/shard_map/cond/branch_1_fun/ppermute | solution.py:251
  61.5 16.0 %collective-permute-start.79 = (bf16[256,384]{1,0:T(8,128)(2,1)S(1)}, bf16[256,384]{1,0:T(8,128)(2,1)S(1)}, u32[]{:S(2)}, u32[]{:S(2)}) collective-permute-start(bf16[256,384]{1,0:T(8,128)(2,1)S(1)} %collective-permute-done.67.refs_0_), channel_id=1, source_target_pairs={{0,2},{1,3},{2,0},{3,1},{4,6},{5,7},{6,4},{7,5},{8,10},{9,11},{10,... | collective-permute-start | bytes 589832 | tf_op jit(solution)/shard_map/cond/branch_1_fun/ppermute | solution.py:251
  77.5 6.7 %collective-permute-start.80 = (bf16[512,384]{1,0:T(8,128)(2,1)S(1)}, bf16[512,384]{1,0:T(8,128)(2,1)S(1)}, u32[]{:S(2)}, u32[]{:S(2)}) collective-permute-start(bf16[512,384]{1,0:T(8,128)(2,1)S(1)} %collective-permute-done.78.refs_1_), channel_id=1, source_target_pairs={{0,1},{1,0},{2,3},{3,2},{4,5},{5,4},{6,7},{7,6},{8,9},{9,8},{10,11... | collective-permute-start | bytes 1179656 | tf_op jit(solution)/shard_map/cond/branch_1_fun/ppermute | solution.py:251
  77.5 11.5 %collective-permute-start.81 = (bf16[512,384]{1,0:T(8,128)(2,1)S(1)}, bf16[512,384]{1,0:T(8,128)(2,1)S(1)}, u32[]{:S(2)}, u32[]{:S(2)}) collective-permute-start(bf16[512,384]{1,0:T(8,128)(2,1)S(1)} %collective-permute-done.78.refs_1_), channel_id=1, source_target_pairs={{0,2},{1,3},{2,0},{3,1},{4,6},{5,7},{6,4},{7,5},{8,10},{9,11},{10,... | collective-permute-start | bytes 1179656 | tf_op jit(solution)/shard_map/cond/branch_1_fun/ppermute | solution.py:251
  89.0 2.0 %collective-permute-start.83 = (bf16[512,384]{1,0:T(8,128)(2,1)S(1)}, bf16[512,384]{1,0:T(8,128)(2,1)S(1)}, u32[]{:S(2)}, u32[]{:S(2)}) collective-permute-start(bf16[512,384]{1,0:T(8,128)(2,1)S(1)} %collective-permute-done.81.refs_1_), channel_id=1, source_target_pairs={{0,1},{1,0},{2,3},{3,2},{4,5},{5,4},{6,7},{7,6},{8,9},{9,8},{10,11... | collective-permute-start | bytes 1179656 | tf_op jit(solution)/shard_map/cond/branch_1_fun/ppermute | solution.py:251
  89.0 2.0 %collective-permute-start.82 = (bf16[256,384]{1,0:T(8,128)(2,1)S(1)}, bf16[256,384]{1,0:T(8,128)(2,1)S(1)}, u32[]{:S(2)}, u32[]{:S(2)}) collective-permute-start(bf16[256,384]{1,0:T(8,128)(2,1)S(1)} %collective-permute-done.79.refs_0_), channel_id=1, source_target_pairs={{0,1},{1,0},{2,3},{3,2},{4,5},{5,4},{6,7},{7,6},{8,9},{9,8},{10,11... | collective-permute-start | bytes 589832 | tf_op jit(solution)/shard_map/cond/branch_1_fun/ppermute | solution.py:251
  (3 other events, 8.1 us)

commit v3 on v2

--- a/solution.py
+++ b/solution.py
@@ -87,10 +87,21 @@
         lax.fori_loop(0, atoms, atom, jnp.int32(0))
 
 
+class Sums:
+    def __init__(self, ref, atoms):
+        self.ref, self.atoms = ref, atoms
+
+    def __getitem__(self, i):
+        total = self.ref[i * self.atoms]
+        for a in range(1, self.atoms):
+            total = total + self.ref[i * self.atoms + a]
+        return total
+
+
 def first_fit(basis_count, ri_count, groups, levels):
     def body(count_ref, ri_ref, o_ref):
         level = jnp.int32(0)
-        for axis, (ref, parts) in enumerate(zip((count_ref, count_ref, ri_ref), groups)):
+        for axis, (ref, parts) in enumerate(zip((count_ref, count_ref, ri_ref, count_ref), groups)):
             per = ref.shape[0] // parts
             most = jnp.int32(0)
             for g in range(parts):
@@ -111,7 +122,7 @@
     )(basis_count, ri_count)
 
 
-def pack_integrals(tc, block_mask, basis_count, ri_count, ncols, packed, unroll, arrived=None):
+def pack_integrals(tc, block_mask, basis_count, ri_count, ncols, packed, unroll, chip_rows, arrived=None):
     rows, cols = tc.shape
     atoms = rows // BW
     wide = cols // ncols
@@ -121,8 +132,8 @@
 
     def body(count_ref, ri_ref, mask_ref, x_ref, *refs):
         outs = refs[:1] if first else refs[1 : 1 + chips]
-        held, hot = refs[-2:] if first else refs[-3:-1]
-        made = outs[0] if first else refs[-1]
+        held, hot = refs[-2:] if first else refs[-4:-2]
+        made, both = (outs[0], None) if first else refs[-2:]
         row, col = lax.axis_index("row"), lax.axis_index("col")
         base = (row * ncols + col) * atoms
         hot[...] = jnp.zeros_like(hot)
@@ -145,12 +156,18 @@
 
         if not first:
             core = lax.rem(col, CORES)
+            chip = (row * ncols + col - core) * atoms
             for t in range(chips):
-                outs[t][pl.ds(pl.multiple_of(core * rows, rows), rows), :] = made[t]
-                outs[t][pl.ds(pl.multiple_of((1 - core) * rows, rows), rows), :] = refs[0][t]
+                into = outs[t] if chip_rows == CORES * rows else both.at[t]
+                into[pl.ds(pl.multiple_of(core * rows, rows), rows), :] = made[t]
+                into[pl.ds(pl.multiple_of((1 - core) * rows, rows), rows), :] = refs[0][t]
+            if chip_rows < CORES * rows:
+                left = pack_rows(count_ref, chip, CORES * atoms, BW, chip_rows, unroll)
+                for t in range(chips):
+                    outs[t][...] = jnp.dot(left, both[t], preferred_element_type=F32).astype(BF16)
 
     shape = (chips, rows, packed)
-    merged = jax.ShapeDtypeStruct((CORES * rows, packed), BF16)
+    merged = jax.ShapeDtypeStruct((chip_rows, packed), BF16)
     out_shape = [jax.ShapeDtypeStruct(shape, BF16)] if first else [merged] * chips
     out_specs = [VMEM_SPEC] * len(out_shape)
     return pl.pallas_call(
@@ -159,7 +176,7 @@
         in_specs=[SMEM_SPEC, SMEM_SPEC, SMEM_SPEC] + [VMEM_SPEC] * (1 if first else 2),
         out_specs=out_specs,
         scratch_shapes=[pltpu.VMEM((rows, wide), BF16), pltpu.VMEM((wide, packed), BF16)]
-        + ([] if first else [pltpu.VMEM(shape, BF16)]),
+        + ([] if first else [pltpu.VMEM(shape, BF16), pltpu.VMEM((chips, CORES * rows, packed), BF16)]),
         compiler_params=params(),
         cost_estimate=cost(rows * cols * packed, rows * cols + 3 * chips * rows * packed),
         name="pack_other_core" if first else "pack_own_core",
@@ -218,11 +235,9 @@
     )(basis_count, mask, dens)
 
 
-def pack_part(pieces, basis_count, first, ncols, size, unroll):
+def pack_part(pieces, basis_count, first, ncols, chip_atoms, size, unroll):
     rows, cols = pieces[0].shape
     per = len(pieces)
-    depth = per * rows
-    atoms = depth // BW
 
     def body(count_ref, *refs):
         blocks, o_ref, full = refs[:per], refs[per], refs[per + 1]
@@ -230,8 +245,11 @@
         for i in range(per):
             at = lax.rem(chip ^ (first + i), per) * rows
             full[pl.ds(pl.multiple_of(at, rows), rows), :] = blocks[i][...]
-        part = (row * (ncols // CORES) + (chip ^ first)) * rows // depth
-        hot = pack_rows(count_ref, part * atoms, atoms, BW, size, unroll)
+        chips = (row * (ncols // CORES) + (chip ^ first)) // per * per
+        if rows == chip_atoms * BW:
+            hot = pack_rows(count_ref, chips * chip_atoms, per * chip_atoms, BW, size, unroll)
+        else:
+            hot = pack_rows(Sums(count_ref, chip_atoms), chips, per, rows, size, unroll)
         o_ref[...] = jnp.dot(hot, full[...], preferred_element_type=F32).astype(BF16)
 
     return pl.pallas_call(
@@ -239,9 +257,9 @@
         out_shape=jax.ShapeDtypeStruct((size, cols), BF16),
         in_specs=[SMEM_SPEC] + [VMEM_SPEC] * per,
         out_specs=VMEM_SPEC,
-        scratch_shapes=[pltpu.VMEM((depth, cols), BF16)],
+        scratch_shapes=[pltpu.VMEM((per * rows, cols), BF16)],
         compiler_params=params(),
-        cost_estimate=cost((2 + 40 * first) * size * depth * cols, 2 * cols * (depth + size)),
+        cost_estimate=cost((2 + 40 * first) * size * per * rows * cols, 2 * cols * (per * rows + size)),
         name="pack_part",
     )(basis_count, *pieces)
 
@@ -420,7 +438,7 @@
     )(total, sums, lam_hot, col_hot, *flat(dens))
 
 
-def program(lam_size, sum_size, col_size, common):
+def program(lam_size, sum_size, col_size, chip_size, common):
     unroll = common
 
     def run(three_center, density, block_mask, density_mask, basis_count, ri_count):
@@ -433,7 +451,7 @@
         chip_bits = [CORES << b for b in range(chips.bit_length() - 1)][::-1]
         far_bit, near_bits = chip_bits[0], chip_bits[1:]
 
-        counts = (block_mask, basis_count, ri_count, ncols, col_size, unroll)
+        counts = (block_mask, basis_count, ri_count, ncols, col_size, unroll, chip_size)
         other = exchange(pack_integrals(three_center, *counts)[0], "col", 1)
         own, upper, lower = pack_density(density, density_mask, basis_count, lam_size, sum_size, unroll)
         lines = [{0: upper, far_bit: exchange(upper, "col", far_bit)}, {0: lower}]
@@ -441,7 +459,8 @@
         pieces = pack_integrals(three_center, *counts, after(other, own))
         early = lines[0][far_bit]
         got = [pieces[0]] + [exchange(pieces[t], "col", CORES * t) for t in range(1, chips)]
-        per = depth // pieces[0].shape[0]
+        chip_rows = CORES * three_center.shape[0]
+        per = depth // chip_rows
         lam_hot, col_hot = ways_back(
             basis_count, ri_count, nrows, ncols, rows, wide, lam_size, col_size, unroll
         )
@@ -452,7 +471,7 @@
                 arrived = [after(arrived[0], near[1])] + arrived[1:]
             elif g == 1:
                 arrived = [after(arrived[0], lam_hot)] + arrived[1:]
-            part = pack_part(arrived, basis_count, g * per, ncols, sum_size, unroll)
+            part = pack_part(arrived, basis_count, g * per, ncols, chip_rows // BW, sum_size, unroll)
             if g == 0:
                 near.update(double(after(own, part), "col", near_bits))
                 steps = [near[far] for far in near if far > 1]
@@ -504,13 +523,14 @@
     nrows = lax.axis_size("row")
     rows, depth = density.shape
     wide = three_center.shape[1] // ncols
+    chip = CORES * three_center.shape[0]
     levels = (
-        (rows * 3 // 4, depth * 3 // 4, wide * 5 // 6),
-        (rows * 3 // 4, depth, wide * 5 // 6),
-        (rows * 3 // 4, depth, wide),
-        (rows, depth, wide),
+        (rows * 3 // 4, depth * 3 // 4, wide * 5 // 6, chip * 7 // 8),
+        (rows * 3 // 4, depth, wide * 5 // 6, chip),
+        (rows * 3 // 4, depth, wide, chip),
+        (rows, depth, wide, chip),
     )
-    level = first_fit(basis_count, ri_count, (nrows, ncols, ncols), levels)
+    level = first_fit(basis_count, ri_count, (nrows, ncols, ncols, nrows * ncols // CORES), levels)
     args = (three_center, density, block_mask, density_mask, basis_count, ri_count)
     run = program(*levels[-1], False)
     for n in reversed(range(len(levels) - 1)):

time: 96.1 us -> 93.1 us (0.969)
  starting transfers between devices: 27.2 us -> 25.2 us
  waiting for transfers between devices: 41.7 us -> 40.2 us
    ppermute x21, starting transfers between devices: 27.2 us -> 25.2 us  [exchange(): return lax.ppermute(x, axis, [(i, i ^ bit) for i in range(peers)])]
    ppermute x21, waiting for transfers between devices: 41.7 us -> 40.2 us  [exchange(): return lax.ppermute(x, axis, [(i, i ^ bit) for i in range(peers)])]
  transfers between devices with their start and end apart: 21 -> 21, of which waited for: 8 -> 8; matrix products, arithmetic and copies ran while one was open for 0% -> 0% of each run, Pallas kernels for 17% -> 18%
where the time goes in v3:
time: 93.1 us; the launch traced here: 93 us
  waiting for transfers between devices  40.2 us (43%)
  starting transfers between devices  25.2 us (27%)
  Pallas kernels  24.9 us (27%)
  local copies, waits for them, and re-layouts  1.24 us (1%)
    ppermute x21, waiting for transfers between devices, exchange(): return lax.ppermute(x, axis, [(i, i ^ bit) for i in range(peers)])  40.2 us
    ppermute x21, starting transfers between devices, exchange(): return lax.ppermute(x, axis, [(i, i ^ bit) for i in range(peers)])  25.2 us
    pallas_call x1, Pallas kernels, contract_near(): pl.pallas_call(body, out_shape=[jax.ShapeDtypeStruct((lam, cols), F32), j...  6.69 us
    pallas_call x2, Pallas kernels, pack_integrals(): pl.pallas_call(body, out_shape=out_shape, in_specs=[SMEM_SPEC, SMEM_SPEC,...  5.44 us
    pallas_call x1, Pallas kernels, contract_last(): pl.pallas_call(body, out_shape=jax.ShapeDtypeStruct((rows, wide), BF16),...  3.42 us
    pallas_call x1, Pallas kernels, pack_density(): pl.pallas_call(body, out_shape=[jax.ShapeDtypeStruct((n, sum_size), BF16)...  3.39 us
    pallas_call x2, Pallas kernels, pack_part(): pl.pallas_call(body, out_shape=jax.ShapeDtypeStruct((size, cols), BF16),...  2.23 us
  transfers between devices with their start and end apart: 21, of which 8 were waited for; matrix products, arithmetic and copies ran while one was open for 0% of the time, Pallas kernels for 18%

profile of v3, /device:TPU:0, one launch (start us, length us, event | category | flops | bytes accessed | tf_op | source)
XLA Modules:
  0.0 93.0 jit_solution(7308545546982112673)
XLA Ops:
  2.0 89.8 %conditional.3 = (bf16[1024,768]{1,0:T(8,128)(2,1)S(1)}) conditional(s32[]{:T(128)} %convert_element_type.9, (s32[]{:T(128)}, s32[128]{0:T(128)}, s32[32,16]{0,1:T(8,128)}, bf16[1024,512]{1,0:T(8,128)(2,1)}, s32[48]{0:T(128)}, /*index=5*/s32[4,48]{1,0:T(4,128)}, bf16[128,6144]{1,0:T(8,128)(2,1)}) %tuple.74, (s32[128]{0:T(128)}, s32[32,16]{0,1:T(8,128)}, ...), branch_computations={%region_0.0_spmd, %region_5.0_spmd} | conditional | flops 26172456960 | bytes 89402256 | solution.py:518
  2.3 2.9 %pack_other_core.7 = bf16[4,128,640]{2,1,0:T(8,128)(2,1)S(1)} custom-call(s32[128]{0:T(128)} %get-tuple-element.198.count_ref, s32[48]{0:T(128)} %get-tuple-element.202.ri_ref, s32[4,48]{1,0:T(4,128)} %get-tuple-element.203.mask_ref, bf16[128,6144]{1,0:T(8,128)(2,1)} %get-tuple-element.204.x_ref), custom_call_target="tpu_custom_call" | custom-call | flops 503316480 | bytes 1769472 | tf_op jit(solution)/shard_map/cond/branch_1_fun/pack_other_core/pallas_call | solution.py:173
  5.8 3.4 %pack_density.7 = (bf16[768,384]{1,0:T(8,128)(2,1)S(1)}, bf16[256,384]{1,0:T(8,128)(2,1)S(1)}, bf16[512,384]{1,0:T(8,128)(2,1)S(1)}) custom-call(s32[128]{0:T(128)S(1)} %copy-done.12, s32[32,16]{1,0:T(8,128)S(1)} %copy.10.mask_ref, bf16[1024,512]{1,0:T(8,128)(2,1)} %get-tuple-element.200.x_ref), custom_call_target="tpu_custom_call" | custom-call | flops 1006632960 | bytes 1048576 | tf_op jit(solution)/shard_map/cond/branch_1_fun/pack_density/pallas_call | solution.py:222
  9.5 2.6 %pack_own_core.7 = (bf16[224,640]{1,0:T(8,128)(2,1)S(1)}, bf16[224,640]{1,0:T(8,128)(2,1)S(1)}, bf16[224,640]{1,0:T(8,128)(2,1)S(1)}, bf16[224,640]{1,0:T(8,128)(2,1)S(1)}) custom-call(s32[128]{0:T(128)S(1)} %copy-done.12, s32[48]{0:T(128)S(1)} %copy-done.16, s32[4,48]{1,0:T(4,128)S(1)} %copy-done.8, bf16[128,6144]{1,0:T(8,128)(2,1)S(1)} %copy-done.3, ...), custom_call_target="tpu_custom_call" | custom-call | flops 503316480 | bytes 1769472 | tf_op jit(solution)/shard_map/cond/branch_1_fun/pack_own_core/pallas_call | solution.py:173
  12.0 3.0 %collective-permute-start.65 = (bf16[224,640]{1,0:T(8,128)(2,1)S(1)}, bf16[224,640]{1,0:T(8,128)(2,1)S(1)}, u32[]{:S(2)}, u32[]{:S(2)}) collective-permute-start(bf16[224,640]{1,0:T(8,128)(2,1)S(1)} %get-tuple-element.208), channel_id=1, source_target_pairs={{0,2},{1,3},{2,0},{3,1},{4,6},{5,7},{6,4},{7,5},{8,10},{9,11},{10,... | collective-permute-start | bytes 860168 | tf_op jit(solution)/shard_map/cond/branch_1_fun/ppermute | solution.py:269
  15.0 2.6 %collective-permute-start.68 = (bf16[224,640]{1,0:T(8,128)(2,1)S(1)}, bf16[224,640]{1,0:T(8,128)(2,1)S(1)}, u32[]{:S(2)}, u32[]{:S(2)}) collective-permute-start(bf16[224,640]{1,0:T(8,128)(2,1)S(1)} %get-tuple-element.211), channel_id=1, source_target_pairs={{0,4},{1,5},{2,6},{3,7},{4,0},{5,1},{6,2},{7,3},{8,12},{9,13},{10,... | collective-permute-start | bytes 860168 | tf_op jit(solution)/shard_map/cond/branch_1_fun/ppermute | solution.py:269
  17.6 1.9 %collective-permute-start.67 = (bf16[256,384]{1,0:T(8,128)(2,1)S(1)}, bf16[256,384]{1,0:T(8,128)(2,1)S(1)}, u32[]{:S(2)}, u32[]{:S(2)}) collective-permute-start(bf16[256,384]{1,0:T(8,128)(2,1)S(1)} %get-tuple-element.210), channel_id=1, source_target_pairs={{0,4},{1,5},{2,6},{3,7},{4,0},{5,1},{6,2},{7,3},{8,12},{9,13},{10,... | collective-permute-start | bytes 589832 | tf_op jit(solution)/shard_map/cond/branch_1_fun/ppermute | solution.py:269
  20.6 7.1 %collective-permute-done.65.refs_1_ = bf16[224,640]{1,0:T(8,128)(2,1)S(1)} collective-permute-done((bf16[224,640]{1,0:T(8,128)(2,1)S(1)}, bf16[224,640]{1,0:T(8,128)(2,1)S(1)}, u32[]{:S(2)}, u32[]{:S(2)}) %collective-permute-start.65) | collective-permute-done | bytes 286752 | tf_op jit(solution)/shard_map/cond/branch_1_fun/ppermute | solution.py:269
  28.8 1.7 %collective-permute-start.70 = (bf16[384,640]{1,0:T(8,128)(2,1)S(1)}, bf16[384,640]{1,0:T(8,128)(2,1)S(1)}, u32[]{:S(2)}, u32[]{:S(2)}) collective-permute-start(bf16[384,640]{1,0:T(8,128)(2,1)S(1)} %pack_part.14.refs_4_), channel_id=1, source_target_pairs={{0,8},{8,0},{16,24},{24,16},{1,9},{9,1},{17,25},{25,17},{2,10},{10... | collective-permute-start | bytes 1474568 | tf_op jit(solution)/shard_map/cond/branch_1_fun/ppermute | solution.py:269
  30.5 1.5 %collective-permute-start.71 = (bf16[384,640]{1,0:T(8,128)(2,1)S(1)}, bf16[384,640]{1,0:T(8,128)(2,1)S(1)}, u32[]{:S(2)}, u32[]{:S(2)}) collective-permute-start(bf16[384,640]{1,0:T(8,128)(2,1)S(1)} %pack_part.14.refs_4_), channel_id=1, source_target_pairs={{0,16},{8,24},{16,0},{24,8},{1,17},{9,25},{17,1},{25,9},{2,18},{10... | collective-permute-start | bytes 1474568 | tf_op jit(solution)/shard_map/cond/branch_1_fun/ppermute | solution.py:269
  32.0 10.1 %collective-permute-done.68.refs_0_ = bf16[224,640]{1,0:T(8,128)(2,1)S(1)} collective-permute-done((bf16[224,640]{1,0:T(8,128)(2,1)S(1)}, bf16[224,640]{1,0:T(8,128)(2,1)S(1)}, u32[]{:S(2)}, u32[]{:S(2)}) %collective-permute-start.68) | collective-permute-done | bytes 286752 | tf_op jit(solution)/shard_map/cond/branch_1_fun/ppermute | solution.py:269
  43.3 1.6 %collective-permute-start.74 = (bf16[384,640]{1,0:T(8,128)(2,1)S(1)}, bf16[384,640]{1,0:T(8,128)(2,1)S(1)}, u32[]{:S(2)}, u32[]{:S(2)}) collective-permute-start(bf16[384,640]{1,0:T(8,128)(2,1)S(1)} %pack_part.15.refs_5_), channel_id=1, source_target_pairs={{0,8},{8,0},{16,24},{24,16},{1,9},{9,1},{17,25},{25,17},{2,10},{10... | collective-permute-start | bytes 1474568 | tf_op jit(solution)/shard_map/cond/branch_1_fun/ppermute | solution.py:269
  44.9 1.5 %collective-permute-start.75 = (bf16[384,640]{1,0:T(8,128)(2,1)S(1)}, bf16[384,640]{1,0:T(8,128)(2,1)S(1)}, u32[]{:S(2)}, u32[]{:S(2)}) collective-permute-start(bf16[384,640]{1,0:T(8,128)(2,1)S(1)} %pack_part.15.refs_5_), channel_id=1, source_target_pairs={{0,16},{8,24},{16,0},{24,8},{1,17},{9,25},{17,1},{25,9},{2,18},{10... | collective-permute-start | bytes 1474568 | tf_op jit(solution)/shard_map/cond/branch_1_fun/ppermute | solution.py:269
  46.4 5.2 %collective-permute-done.67.refs_0_ = bf16[256,384]{1,0:T(8,128)(2,1)S(1)} collective-permute-done((bf16[256,384]{1,0:T(8,128)(2,1)S(1)}, bf16[256,384]{1,0:T(8,128)(2,1)S(1)}, u32[]{:S(2)}, u32[]{:S(2)}) %collective-permute-start.67) | collective-permute-done | bytes 196640 | tf_op jit(solution)/shard_map/cond/branch_1_fun/ppermute | solution.py:269
  51.6 2.5 %collective-permute-start.78 = (bf16[512,384]{1,0:T(8,128)(2,1)S(1)}, bf16[512,384]{1,0:T(8,128)(2,1)S(1)}, u32[]{:S(2)}, u32[]{:S(2)}) collective-permute-start(bf16[512,384]{1,0:T(8,128)(2,1)S(1)} %get-tuple-element.222), channel_id=1, source_target_pairs={{0,4},{1,5},{2,6},{3,7},{4,0},{5,1},{6,2},{7,3},{8,12},{9,13},{10,... | collective-permute-start | bytes 1179656 | tf_op jit(solution)/shard_map/cond/branch_1_fun/ppermute | solution.py:269
  54.1 3.3 %collective-permute-done.66.refs_2_ = bf16[768,384]{1,0:T(8,128)(2,1)S(1)} collective-permute-done((bf16[768,384]{1,0:T(8,128)(2,1)S(1)}, bf16[768,384]{1,0:T(8,128)(2,1)S(1)}, u32[]{:S(2)}, u32[]{:S(2)}) %collective-permute-start.66) | collective-permute-done | bytes 589856 | tf_op jit(solution)/shard_map/cond/branch_1_fun/ppermute | solution.py:269
  58.0 1.5 %collective-permute-start.77 = (bf16[384,640]{1,0:T(8,128)(2,1)S(1)}, bf16[384,640]{1,0:T(8,128)(2,1)S(1)}, u32[]{:S(2)}, u32[]{:S(2)}) collective-permute-start(bf16[384,640]{1,0:T(8,128)(2,1)S(1)} %collective-permute-done.75.refs_9_), channel_id=1, source_target_pairs={{0,8},{8,0},{16,24},{24,16},{1,9},{9,1},{17,25},{25,17},{2,10},{10... | collective-permute-start | bytes 1474568 | tf_op jit(solution)/shard_map/cond/branch_1_fun/ppermute | solution.py:269
  59.5 5.5 %collective-permute-start.79 = (bf16[256,384]{1,0:T(8,128)(2,1)S(1)}, bf16[256,384]{1,0:T(8,128)(2,1)S(1)}, u32[]{:S(2)}, u32[]{:S(2)}) collective-permute-start(bf16[256,384]{1,0:T(8,128)(2,1)S(1)} %collective-permute-done.67.refs_0_), channel_id=1, source_target_pairs={{0,2},{1,3},{2,0},{3,1},{4,6},{5,7},{6,4},{7,5},{8,10},{9,11},{10,... | collective-permute-start | bytes 589832 | tf_op jit(solution)/shard_map/cond/branch_1_fun/ppermute | solution.py:269
  65.0 7.5 %collective-permute-done.78.refs_1_ = bf16[512,384]{1,0:T(8,128)(2,1)S(1)} collective-permute-done((bf16[512,384]{1,0:T(8,128)(2,1)S(1)}, bf16[512,384]{1,0:T(8,128)(2,1)S(1)}, u32[]{:S(2)}, u32[]{:S(2)}) %collective-permute-start.78) | collective-permute-done | bytes 393248 | tf_op jit(solution)/shard_map/cond/branch_1_fun/ppermute | solution.py:269
  72.5 2.0 %collective-permute-done.79.refs_0_ = bf16[256,384]{1,0:T(8,128)(2,1)S(1)} collective-permute-done((bf16[256,384]{1,0:T(8,128)(2,1)S(1)}, bf16[256,384]{1,0:T(8,128)(2,1)S(1)}, u32[]{:S(2)}, u32[]{:S(2)}) %collective-permute-start.79) | collective-permute-done | bytes 196640 | tf_op jit(solution)/shard_map/cond/branch_1_fun/ppermute | solution.py:269
  74.6 6.7 %contract_near.7 = (f32[768,640]{1,0:T(8,128)S(1)}, bf16[4,384,640]{2,1,0:T(8,128)(2,1)S(1)}) custom-call(bf16[768,384]{1,0:T(8,128)(2,1)S(1)} %get-tuple-element.209.refs_0_, bf16[768,384]{1,0:T(8,128)(2,1)S(1)} %collective-permute-done.64.refs_1_, bf16[768,384]{1,0:T(8,128)(2,1)S(1)} %collective-permute-done.66.refs_2_, ...), custom_call_target="tpu_custom_call" | custom-call | flops 1509949440 | bytes 4325376 | tf_op jit(solution)/shard_map/cond/branch_1_fun/contract_near/pallas_call | solution.py:369
  82.6 3.5 %collective-permute-done.81.refs_1_ = bf16[512,384]{1,0:T(8,128)(2,1)S(1)} collective-permute-done((bf16[512,384]{1,0:T(8,128)(2,1)S(1)}, bf16[512,384]{1,0:T(8,128)(2,1)S(1)}, u32[]{:S(2)}, u32[]{:S(2)}) %collective-permute-start.81) | collective-permute-done | bytes 393248 | tf_op jit(solution)/shard_map/cond/branch_1_fun/ppermute | solution.py:269
  86.6 1.5 %collective-permute-done.82.refs_2_ = bf16[256,384]{1,0:T(8,128)(2,1)S(1)} collective-permute-done((bf16[256,384]{1,0:T(8,128)(2,1)S(1)}, bf16[256,384]{1,0:T(8,128)(2,1)S(1)}, u32[]{:S(2)}, u32[]{:S(2)}) %collective-permute-start.82) | collective-permute-done | bytes 196640 | tf_op jit(solution)/shard_map/cond/branch_1_fun/ppermute | solution.py:269
  88.1 3.4 %contract_last.7 = bf16[1024,768]{1,0:T(8,128)(2,1)S(1)} custom-call(f32[768,640]{1,0:T(8,128)S(1)} %contract_far.7.before, bf16[4,384,640]{2,1,0:T(8,128)(2,1)S(1)} %get-tuple-element.220.s_ref, bf16[1024,768]{1,0:T(8,128)(2,1)S(1)} %get-tuple-element.212.lam_hot, bf16[640,768]{1,0:T(8,128)(2,1)S(1)} %get-tuple-element.225.col_hot, ...), custom_call_target="tpu_custom_call" | custom-call | flops 754974720 | bytes 2162688 | tf_op jit(solution)/shard_map/cond/branch_1_fun/contract_last/pallas_call | solution.py:429
  (42 shorter events, 9.1 us)
Async XLA Ops:
  5.2 4.3 %copy-start.3 = (bf16[128,6144]{1,0:T(8,128)(2,1)S(1)}, bf16[128,6144]{1,0:T(8,128)(2,1)}, u32[]{:S(2)}) copy-start(bf16[128,6144]{1,0:T(8,128)(2,1)} %get-tuple-element.204.x_ref) | copy-start | bytes 4718596 | tf_op jit(solution)/shard_map/cond
  5.2 4.3 %copy-start.8 = (s32[4,48]{1,0:T(4,128)S(1)}, s32[4,48]{1,0:T(4,128)}, u32[]{:S(2)}) copy-start(s32[4,48]{1,0:T(4,128)} %get-tuple-element.203.mask_ref) | copy-start | bytes 2308 | tf_op jit(solution)/shard_map/cond
  5.2 4.3 %copy-start.16 = (s32[48]{0:T(128)S(1)}, s32[48]{0:T(128)}, u32[]{:S(2)}) copy-start(s32[48]{0:T(128)} %get-tuple-element.202.ri_ref) | copy-start | bytes 580 | tf_op jit(solution)/shard_map/cond
  5.2 4.2 %collective-permute-start.63 = (bf16[4,128,640]{2,1,0:T(8,128)(2,1)S(1)}, bf16[4,128,640]{2,1,0:T(8,128)(2,1)S(1)}, u32[]{:S(2)}, u32[]{:S(2)}) collective-permute-start(bf16[4,128,640]{2,1,0:T(8,128)(2,1)S(1)} %pack_other_core.7), channel_id=1, source_target_pairs={{0,1},{1,0},{2,3},{3,2},{4,5},{5,4},{6,7},{7,6},{8,9},{9,8},{10,11... | collective-permute-start | bytes 1966088 | tf_op jit(solution)/shard_map/cond/branch_1_fun/ppermute | solution.py:269
  9.2 11.4 %collective-permute-start.64 = (bf16[768,384]{1,0:T(8,128)(2,1)S(1)}, bf16[768,384]{1,0:T(8,128)(2,1)S(1)}, u32[]{:S(2)}, u32[]{:S(2)}) collective-permute-start(bf16[768,384]{1,0:T(8,128)(2,1)S(1)} %get-tuple-element.209.refs_0_), channel_id=1, source_target_pairs={{0,1},{1,0},{2,3},{3,2},{4,5},{5,4},{6,7},{7,6},{8,9},{9,8},{10,11... | collective-permute-start | bytes 1769480 | tf_op jit(solution)/shard_map/cond/branch_1_fun/ppermute | solution.py:269
  12.0 15.6 %collective-permute-start.65 = (bf16[224,640]{1,0:T(8,128)(2,1)S(1)}, bf16[224,640]{1,0:T(8,128)(2,1)S(1)}, u32[]{:S(2)}, u32[]{:S(2)}) collective-permute-start(bf16[224,640]{1,0:T(8,128)(2,1)S(1)} %get-tuple-element.208), channel_id=1, source_target_pairs={{0,2},{1,3},{2,0},{3,1},{4,6},{5,7},{6,4},{7,5},{8,10},{9,11},{10,... | collective-permute-start | bytes 860168 | tf_op jit(solution)/shard_map/cond/branch_1_fun/ppermute | solution.py:269
  15.0 27.2 %collective-permute-start.68 = (bf16[224,640]{1,0:T(8,128)(2,1)S(1)}, bf16[224,640]{1,0:T(8,128)(2,1)S(1)}, u32[]{:S(2)}, u32[]{:S(2)}) collective-permute-start(bf16[224,640]{1,0:T(8,128)(2,1)S(1)} %get-tuple-element.211), channel_id=1, source_target_pairs={{0,4},{1,5},{2,6},{3,7},{4,0},{5,1},{6,2},{7,3},{8,12},{9,13},{10,... | collective-permute-start | bytes 860168 | tf_op jit(solution)/shard_map/cond/branch_1_fun/ppermute | solution.py:269
  17.6 24.6 %collective-permute-start.69 = (bf16[224,640]{1,0:T(8,128)(2,1)S(1)}, bf16[224,640]{1,0:T(8,128)(2,1)S(1)}, u32[]{:S(2)}, u32[]{:S(2)}) collective-permute-start(bf16[224,640]{1,0:T(8,128)(2,1)S(1)} %get-tuple-element.214), channel_id=1, source_target_pairs={{0,6},{1,7},{2,4},{3,5},{4,2},{5,3},{6,0},{7,1},{8,14},{9,15},{10,... | collective-permute-start | bytes 860168 | tf_op jit(solution)/shard_map/cond/branch_1_fun/ppermute | solution.py:269
  17.6 33.9 %collective-permute-start.67 = (bf16[256,384]{1,0:T(8,128)(2,1)S(1)}, bf16[256,384]{1,0:T(8,128)(2,1)S(1)}, u32[]{:S(2)}, u32[]{:S(2)}) collective-permute-start(bf16[256,384]{1,0:T(8,128)(2,1)S(1)} %get-tuple-element.210), channel_id=1, source_target_pairs={{0,4},{1,5},{2,6},{3,7},{4,0},{5,1},{6,2},{7,3},{8,12},{9,13},{10,... | collective-permute-start | bytes 589832 | tf_op jit(solution)/shard_map/cond/branch_1_fun/ppermute | solution.py:269
  28.8 14.5 %collective-permute-start.70 = (bf16[384,640]{1,0:T(8,128)(2,1)S(1)}, bf16[384,640]{1,0:T(8,128)(2,1)S(1)}, u32[]{:S(2)}, u32[]{:S(2)}) collective-permute-start(bf16[384,640]{1,0:T(8,128)(2,1)S(1)} %pack_part.14.refs_4_), channel_id=1, source_target_pairs={{0,8},{8,0},{16,24},{24,16},{1,9},{9,1},{17,25},{25,17},{2,10},{10... | collective-permute-start | bytes 1474568 | tf_op jit(solution)/shard_map/cond/branch_1_fun/ppermute | solution.py:269
  30.5 12.8 %collective-permute-start.71 = (bf16[384,640]{1,0:T(8,128)(2,1)S(1)}, bf16[384,640]{1,0:T(8,128)(2,1)S(1)}, u32[]{:S(2)}, u32[]{:S(2)}) collective-permute-start(bf16[384,640]{1,0:T(8,128)(2,1)S(1)} %pack_part.14.refs_4_), channel_id=1, source_target_pairs={{0,16},{8,24},{16,0},{24,8},{1,17},{9,25},{17,1},{25,9},{2,18},{10... | collective-permute-start | bytes 1474568 | tf_op jit(solution)/shard_map/cond/branch_1_fun/ppermute | solution.py:269
  42.2 15.2 %collective-permute-start.66 = (bf16[768,384]{1,0:T(8,128)(2,1)S(1)}, bf16[768,384]{1,0:T(8,128)(2,1)S(1)}, u32[]{:S(2)}, u32[]{:S(2)}) collective-permute-start(bf16[768,384]{1,0:T(8,128)(2,1)S(1)} %get-tuple-element.209.refs_0_), channel_id=1, source_target_pairs={{0,2},{1,3},{2,0},{3,1},{4,6},{5,7},{6,4},{7,5},{8,10},{9,11},{10,... | collective-permute-start | bytes 1769480 | tf_op jit(solution)/shard_map/cond/branch_1_fun/ppermute | solution.py:269
  43.3 14.0 %collective-permute-start.74 = (bf16[384,640]{1,0:T(8,128)(2,1)S(1)}, bf16[384,640]{1,0:T(8,128)(2,1)S(1)}, u32[]{:S(2)}, u32[]{:S(2)}) collective-permute-start(bf16[384,640]{1,0:T(8,128)(2,1)S(1)} %pack_part.15.refs_5_), channel_id=1, source_target_pairs={{0,8},{8,0},{16,24},{24,16},{1,9},{9,1},{17,25},{25,17},{2,10},{10... | collective-permute-start | bytes 1474568 | tf_op jit(solution)/shard_map/cond/branch_1_fun/ppermute | solution.py:269
  44.9 12.5 %collective-permute-start.75 = (bf16[384,640]{1,0:T(8,128)(2,1)S(1)}, bf16[384,640]{1,0:T(8,128)(2,1)S(1)}, u32[]{:S(2)}, u32[]{:S(2)}) collective-permute-start(bf16[384,640]{1,0:T(8,128)(2,1)S(1)} %pack_part.15.refs_5_), channel_id=1, source_target_pairs={{0,16},{8,24},{16,0},{24,8},{1,17},{9,25},{17,1},{25,9},{2,18},{10... | collective-permute-start | bytes 1474568 | tf_op jit(solution)/shard_map/cond/branch_1_fun/ppermute | solution.py:269
  51.6 5.8 %collective-permute-start.72 = (bf16[256,384]{1,0:T(8,128)(2,1)S(1)}, bf16[256,384]{1,0:T(8,128)(2,1)S(1)}, u32[]{:S(2)}, u32[]{:S(2)}) collective-permute-start(bf16[256,384]{1,0:T(8,128)(2,1)S(1)} %collective-permute-done.67.refs_0_), channel_id=1, source_target_pairs={{0,1},{1,0},{2,3},{3,2},{4,5},{5,4},{6,7},{7,6},{8,9},{9,8},{10,11... | collective-permute-start | bytes 589832 | tf_op jit(solution)/shard_map/cond/branch_1_fun/ppermute | solution.py:269
  51.6 21.0 %collective-permute-start.78 = (bf16[512,384]{1,0:T(8,128)(2,1)S(1)}, bf16[512,384]{1,0:T(8,128)(2,1)S(1)}, u32[]{:S(2)}, u32[]{:S(2)}) collective-permute-start(bf16[512,384]{1,0:T(8,128)(2,1)S(1)} %get-tuple-element.222), channel_id=1, source_target_pairs={{0,4},{1,5},{2,6},{3,7},{4,0},{5,1},{6,2},{7,3},{8,12},{9,13},{10,... | collective-permute-start | bytes 1179656 | tf_op jit(solution)/shard_map/cond/branch_1_fun/ppermute | solution.py:269
  57.3 17.2 %collective-permute-start.73 = (bf16[768,384]{1,0:T(8,128)(2,1)S(1)}, bf16[768,384]{1,0:T(8,128)(2,1)S(1)}, u32[]{:S(2)}, u32[]{:S(2)}) collective-permute-start(bf16[768,384]{1,0:T(8,128)(2,1)S(1)} %collective-permute-done.66.refs_2_), channel_id=1, source_target_pairs={{0,1},{1,0},{2,3},{3,2},{4,5},{5,4},{6,7},{7,6},{8,9},{9,8},{10,11... | collective-permute-start | bytes 1769480 | tf_op jit(solution)/shard_map/cond/branch_1_fun/ppermute | solution.py:269
  57.4 17.2 %collective-permute-start.76 = (bf16[384,640]{1,0:T(8,128)(2,1)S(1)}, bf16[384,640]{1,0:T(8,128)(2,1)S(1)}, u32[]{:S(2)}, u32[]{:S(2)}) collective-permute-start(bf16[384,640]{1,0:T(8,128)(2,1)S(1)} %collective-permute-done.70.refs_6_), channel_id=1, source_target_pairs={{0,16},{8,24},{16,0},{24,8},{1,17},{9,25},{17,1},{25,9},{2,18},{10... | collective-permute-start | bytes 1474568 | tf_op jit(solution)/shard_map/cond/branch_1_fun/ppermute | solution.py:269
  58.0 16.6 %collective-permute-start.77 = (bf16[384,640]{1,0:T(8,128)(2,1)S(1)}, bf16[384,640]{1,0:T(8,128)(2,1)S(1)}, u32[]{:S(2)}, u32[]{:S(2)}) collective-permute-start(bf16[384,640]{1,0:T(8,128)(2,1)S(1)} %collective-permute-done.75.refs_9_), channel_id=1, source_target_pairs={{0,8},{8,0},{16,24},{24,16},{1,9},{9,1},{17,25},{25,17},{2,10},{10... | collective-permute-start | bytes 1474568 | tf_op jit(solution)/shard_map/cond/branch_1_fun/ppermute | solution.py:269
  59.5 15.1 %collective-permute-start.79 = (bf16[256,384]{1,0:T(8,128)(2,1)S(1)}, bf16[256,384]{1,0:T(8,128)(2,1)S(1)}, u32[]{:S(2)}, u32[]{:S(2)}) collective-permute-start(bf16[256,384]{1,0:T(8,128)(2,1)S(1)} %collective-permute-done.67.refs_0_), channel_id=1, source_target_pairs={{0,2},{1,3},{2,0},{3,1},{4,6},{5,7},{6,4},{7,5},{8,10},{9,11},{10,... | collective-permute-start | bytes 589832 | tf_op jit(solution)/shard_map/cond/branch_1_fun/ppermute | solution.py:269
  74.5 6.7 %collective-permute-start.80 = (bf16[512,384]{1,0:T(8,128)(2,1)S(1)}, bf16[512,384]{1,0:T(8,128)(2,1)S(1)}, u32[]{:S(2)}, u32[]{:S(2)}) collective-permute-start(bf16[512,384]{1,0:T(8,128)(2,1)S(1)} %collective-permute-done.78.refs_1_), channel_id=1, source_target_pairs={{0,1},{1,0},{2,3},{3,2},{4,5},{5,4},{6,7},{7,6},{8,9},{9,8},{10,11... | collective-permute-start | bytes 1179656 | tf_op jit(solution)/shard_map/cond/branch_1_fun/ppermute | solution.py:269
  74.5 11.5 %collective-permute-start.81 = (bf16[512,384]{1,0:T(8,128)(2,1)S(1)}, bf16[512,384]{1,0:T(8,128)(2,1)S(1)}, u32[]{:S(2)}, u32[]{:S(2)}) collective-permute-start(bf16[512,384]{1,0:T(8,128)(2,1)S(1)} %collective-permute-done.78.refs_1_), channel_id=1, source_target_pairs={{0,2},{1,3},{2,0},{3,1},{4,6},{5,7},{6,4},{7,5},{8,10},{9,11},{10,... | collective-permute-start | bytes 1179656 | tf_op jit(solution)/shard_map/cond/branch_1_fun/ppermute | solution.py:269
  86.1 2.0 %collective-permute-start.83 = (bf16[512,384]{1,0:T(8,128)(2,1)S(1)}, bf16[512,384]{1,0:T(8,128)(2,1)S(1)}, u32[]{:S(2)}, u32[]{:S(2)}) collective-permute-start(bf16[512,384]{1,0:T(8,128)(2,1)S(1)} %collective-permute-done.81.refs_1_), channel_id=1, source_target_pairs={{0,1},{1,0},{2,3},{3,2},{4,5},{5,4},{6,7},{7,6},{8,9},{9,8},{10,11... | collective-permute-start | bytes 1179656 | tf_op jit(solution)/shard_map/cond/branch_1_fun/ppermute | solution.py:269
  86.1 2.0 %collective-permute-start.82 = (bf16[256,384]{1,0:T(8,128)(2,1)S(1)}, bf16[256,384]{1,0:T(8,128)(2,1)S(1)}, u32[]{:S(2)}, u32[]{:S(2)}) collective-permute-start(bf16[256,384]{1,0:T(8,128)(2,1)S(1)} %collective-permute-done.79.refs_0_), channel_id=1, source_target_pairs={{0,1},{1,0},{2,3},{3,2},{4,5},{5,4},{6,7},{7,6},{8,9},{9,8},{10,11... | collective-permute-start | bytes 589832 | tf_op jit(solution)/shard_map/cond/branch_1_fun/ppermute | solution.py:269
  (3 other events, 8.1 us)

commit v4 on v3

--- a/solution.py
+++ b/solution.py
@@ -195,7 +195,9 @@
         first = iota((sum_atoms, cols), 0) * BW
         lane = iota((sum_atoms, cols), 1)
         of_atom = ones_where((lane >= first) & (lane < first + BW))
-        keep[...] = jnp.dot(ones_where(mask_ref[...] > 0), of_atom, preferred_element_type=F32).astype(BF16)
+        keep[...] = lax.dot_general(
+            ones_where(mask_ref[...] > 0), of_atom, (((0,), (0,)), ((), ())), preferred_element_type=F32
+        ).astype(BF16)
         pack_cols(count_ref, col * sum_atoms, sum_atoms, BW, sum_size, hot, unroll)
 
         @loop(steps, unroll)
@@ -232,7 +234,7 @@
         compiler_params=params(),
         cost_estimate=cost(2 * rows * sum_size * (cols + lam_size), 2 * rows * cols),
         name="pack_density",
-    )(basis_count, mask, dens)
+    )(basis_count, mask.T, dens)
 
 
 def pack_part(pieces, basis_count, first, ncols, chip_atoms, size, unroll):

time: 93.1 us -> 92.4 us (level)
  no operation moved by 1% of the time
where the time goes in v4:
time: 92.4 us; the launch traced here: 92.2 us
  waiting for transfers between devices  40.2 us (44%)
  starting transfers between devices  25.2 us (27%)
  Pallas kernels  24.2 us (26%)
  local copies, waits for them, and re-layouts  1.18 us (1%)
    ppermute x21, waiting for transfers between devices, exchange(): return lax.ppermute(x, axis, [(i, i ^ bit) for i in range(peers)])  40.2 us
    ppermute x21, starting transfers between devices, exchange(): return lax.ppermute(x, axis, [(i, i ^ bit) for i in range(peers)])  25.2 us
    pallas_call x1, Pallas kernels, contract_near(): pl.pallas_call(body, out_shape=[jax.ShapeDtypeStruct((lam, cols), F32), j...  6.69 us
    pallas_call x2, Pallas kernels, pack_integrals(): pl.pallas_call(body, out_shape=out_shape, in_specs=[SMEM_SPEC, SMEM_SPEC,...  5.52 us
    pallas_call x1, Pallas kernels, contract_last(): pl.pallas_call(body, out_shape=jax.ShapeDtypeStruct((rows, wide), BF16),...  3.42 us
    pallas_call x1, Pallas kernels, pack_density(): pl.pallas_call(body, out_shape=[jax.ShapeDtypeStruct((n, sum_size), BF16)...  2.69 us
    pallas_call x2, Pallas kernels, pack_part(): pl.pallas_call(body, out_shape=jax.ShapeDtypeStruct((size, cols), BF16),...  2.22 us
  transfers between devices with their start and end apart: 21, of which 8 were waited for; matrix products, arithmetic and copies ran while one was open for 0% of the time, Pallas kernels for 18%

profile of v4, /device:TPU:0, one launch (start us, length us, event | category | flops | bytes accessed | tf_op | source)
XLA Modules:
  0.0 92.2 jit_solution(12671685495591605273)
XLA Ops:
  2.0 89.0 %conditional.3 = (bf16[1024,768]{1,0:T(8,128)(2,1)S(1)}) conditional(s32[]{:T(128)} %convert_element_type.9, (s32[]{:T(128)}, s32[32,16]{0,1:T(8,128)}, s32[128]{0:T(128)}, bf16[1024,512]{1,0:T(8,128)(2,1)}, s32[48]{0:T(128)}, /*index=5*/s32[4,48]{1,0:T(4,128)}, bf16[128,6144]{1,0:T(8,128)(2,1)}) %tuple.74, (s32[32,16]{0,1:T(8,128)}, s32[128]{0:T(128)}, ...), branch_computations={%region_0.0_spmd, %region_5.0_spmd} | conditional | flops 26172456960 | bytes 89406328 | solution.py:520
  2.3 3.0 %pack_other_core.7 = bf16[4,128,640]{2,1,0:T(8,128)(2,1)S(1)} custom-call(s32[128]{0:T(128)} %get-tuple-element.198.count_ref, s32[48]{0:T(128)} %get-tuple-element.202.ri_ref, s32[4,48]{1,0:T(4,128)} %get-tuple-element.203.mask_ref, bf16[128,6144]{1,0:T(8,128)(2,1)} %get-tuple-element.204.x_ref), custom_call_target="tpu_custom_call" | custom-call | flops 503316480 | bytes 1769472 | tf_op jit(solution)/shard_map/cond/branch_1_fun/pack_other_core/pallas_call | solution.py:173
  5.8 2.7 %pack_density.7 = (bf16[768,384]{1,0:T(8,128)(2,1)S(1)}, bf16[256,384]{1,0:T(8,128)(2,1)S(1)}, bf16[512,384]{1,0:T(8,128)(2,1)S(1)}) custom-call(s32[128]{0:T(128)S(1)} %copy-done.12, s32[16,32]{1,0:T(8,128)S(1)} %bitcast.8, bf16[1024,512]{1,0:T(8,128)(2,1)S(1)} %copy-done.20), custom_call_target="tpu_custom_call" | custom-call | flops 1006632960 | bytes 1048576 | tf_op jit(solution)/shard_map/cond/branch_1_fun/pack_density/pallas_call | solution.py:224
  8.7 2.6 %pack_own_core.7 = (bf16[224,640]{1,0:T(8,128)(2,1)S(1)}, bf16[224,640]{1,0:T(8,128)(2,1)S(1)}, bf16[224,640]{1,0:T(8,128)(2,1)S(1)}, bf16[224,640]{1,0:T(8,128)(2,1)S(1)}) custom-call(s32[128]{0:T(128)S(1)} %copy-done.12, s32[48]{0:T(128)S(1)} %copy-done.16, s32[4,48]{1,0:T(4,128)S(1)} %copy-done.8, bf16[128,6144]{1,0:T(8,128)(2,1)S(1)} %copy-done.3, ...), custom_call_target="tpu_custom_call" | custom-call | flops 503316480 | bytes 1769472 | tf_op jit(solution)/shard_map/cond/branch_1_fun/pack_own_core/pallas_call | solution.py:173
  11.2 3.1 %collective-permute-start.65 = (bf16[224,640]{1,0:T(8,128)(2,1)S(1)}, bf16[224,640]{1,0:T(8,128)(2,1)S(1)}, u32[]{:S(2)}, u32[]{:S(2)}) collective-permute-start(bf16[224,640]{1,0:T(8,128)(2,1)S(1)} %get-tuple-element.208), channel_id=1, source_target_pairs={{0,2},{1,3},{2,0},{3,1},{4,6},{5,7},{6,4},{7,5},{8,10},{9,11},{10,... | collective-permute-start | bytes 860168 | tf_op jit(solution)/shard_map/cond/branch_1_fun/ppermute | solution.py:271
  14.3 2.6 %collective-permute-start.68 = (bf16[224,640]{1,0:T(8,128)(2,1)S(1)}, bf16[224,640]{1,0:T(8,128)(2,1)S(1)}, u32[]{:S(2)}, u32[]{:S(2)}) collective-permute-start(bf16[224,640]{1,0:T(8,128)(2,1)S(1)} %get-tuple-element.211), channel_id=1, source_target_pairs={{0,4},{1,5},{2,6},{3,7},{4,0},{5,1},{6,2},{7,3},{8,12},{9,13},{10,... | collective-permute-start | bytes 860168 | tf_op jit(solution)/shard_map/cond/branch_1_fun/ppermute | solution.py:271
  16.9 1.9 %collective-permute-start.67 = (bf16[256,384]{1,0:T(8,128)(2,1)S(1)}, bf16[256,384]{1,0:T(8,128)(2,1)S(1)}, u32[]{:S(2)}, u32[]{:S(2)}) collective-permute-start(bf16[256,384]{1,0:T(8,128)(2,1)S(1)} %get-tuple-element.210), channel_id=1, source_target_pairs={{0,4},{1,5},{2,6},{3,7},{4,0},{5,1},{6,2},{7,3},{8,12},{9,13},{10,... | collective-permute-start | bytes 589832 | tf_op jit(solution)/shard_map/cond/branch_1_fun/ppermute | solution.py:271
  19.9 7.0 %collective-permute-done.65.refs_1_ = bf16[224,640]{1,0:T(8,128)(2,1)S(1)} collective-permute-done((bf16[224,640]{1,0:T(8,128)(2,1)S(1)}, bf16[224,640]{1,0:T(8,128)(2,1)S(1)}, u32[]{:S(2)}, u32[]{:S(2)}) %collective-permute-start.65) | collective-permute-done | bytes 286752 | tf_op jit(solution)/shard_map/cond/branch_1_fun/ppermute | solution.py:271
  28.0 1.7 %collective-permute-start.70 = (bf16[384,640]{1,0:T(8,128)(2,1)S(1)}, bf16[384,640]{1,0:T(8,128)(2,1)S(1)}, u32[]{:S(2)}, u32[]{:S(2)}) collective-permute-start(bf16[384,640]{1,0:T(8,128)(2,1)S(1)} %pack_part.14.refs_4_), channel_id=1, source_target_pairs={{0,8},{8,0},{16,24},{24,16},{1,9},{9,1},{17,25},{25,17},{2,10},{10... | collective-permute-start | bytes 1474568 | tf_op jit(solution)/shard_map/cond/branch_1_fun/ppermute | solution.py:271
  29.7 1.5 %collective-permute-start.71 = (bf16[384,640]{1,0:T(8,128)(2,1)S(1)}, bf16[384,640]{1,0:T(8,128)(2,1)S(1)}, u32[]{:S(2)}, u32[]{:S(2)}) collective-permute-start(bf16[384,640]{1,0:T(8,128)(2,1)S(1)} %pack_part.14.refs_4_), channel_id=1, source_target_pairs={{0,16},{8,24},{16,0},{24,8},{1,17},{9,25},{17,1},{25,9},{2,18},{10... | collective-permute-start | bytes 1474568 | tf_op jit(solution)/shard_map/cond/branch_1_fun/ppermute | solution.py:271
  31.2 10.3 %collective-permute-done.68.refs_0_ = bf16[224,640]{1,0:T(8,128)(2,1)S(1)} collective-permute-done((bf16[224,640]{1,0:T(8,128)(2,1)S(1)}, bf16[224,640]{1,0:T(8,128)(2,1)S(1)}, u32[]{:S(2)}, u32[]{:S(2)}) %collective-permute-start.68) | collective-permute-done | bytes 286752 | tf_op jit(solution)/shard_map/cond/branch_1_fun/ppermute | solution.py:271
  42.7 1.5 %collective-permute-start.74 = (bf16[384,640]{1,0:T(8,128)(2,1)S(1)}, bf16[384,640]{1,0:T(8,128)(2,1)S(1)}, u32[]{:S(2)}, u32[]{:S(2)}) collective-permute-start(bf16[384,640]{1,0:T(8,128)(2,1)S(1)} %pack_part.15.refs_5_), channel_id=1, source_target_pairs={{0,8},{8,0},{16,24},{24,16},{1,9},{9,1},{17,25},{25,17},{2,10},{10... | collective-permute-start | bytes 1474568 | tf_op jit(solution)/shard_map/cond/branch_1_fun/ppermute | solution.py:271
  44.2 1.5 %collective-permute-start.75 = (bf16[384,640]{1,0:T(8,128)(2,1)S(1)}, bf16[384,640]{1,0:T(8,128)(2,1)S(1)}, u32[]{:S(2)}, u32[]{:S(2)}) collective-permute-start(bf16[384,640]{1,0:T(8,128)(2,1)S(1)} %pack_part.15.refs_5_), channel_id=1, source_target_pairs={{0,16},{8,24},{16,0},{24,8},{1,17},{9,25},{17,1},{25,9},{2,18},{10... | collective-permute-start | bytes 1474568 | tf_op jit(solution)/shard_map/cond/branch_1_fun/ppermute | solution.py:271
  45.7 5.1 %collective-permute-done.67.refs_0_ = bf16[256,384]{1,0:T(8,128)(2,1)S(1)} collective-permute-done((bf16[256,384]{1,0:T(8,128)(2,1)S(1)}, bf16[256,384]{1,0:T(8,128)(2,1)S(1)}, u32[]{:S(2)}, u32[]{:S(2)}) %collective-permute-start.67) | collective-permute-done | bytes 196640 | tf_op jit(solution)/shard_map/cond/branch_1_fun/ppermute | solution.py:271
  50.8 2.6 %collective-permute-start.78 = (bf16[512,384]{1,0:T(8,128)(2,1)S(1)}, bf16[512,384]{1,0:T(8,128)(2,1)S(1)}, u32[]{:S(2)}, u32[]{:S(2)}) collective-permute-start(bf16[512,384]{1,0:T(8,128)(2,1)S(1)} %get-tuple-element.222), channel_id=1, source_target_pairs={{0,4},{1,5},{2,6},{3,7},{4,0},{5,1},{6,2},{7,3},{8,12},{9,13},{10,... | collective-permute-start | bytes 1179656 | tf_op jit(solution)/shard_map/cond/branch_1_fun/ppermute | solution.py:271
  53.4 3.3 %collective-permute-done.66.refs_2_ = bf16[768,384]{1,0:T(8,128)(2,1)S(1)} collective-permute-done((bf16[768,384]{1,0:T(8,128)(2,1)S(1)}, bf16[768,384]{1,0:T(8,128)(2,1)S(1)}, u32[]{:S(2)}, u32[]{:S(2)}) %collective-permute-start.66) | collective-permute-done | bytes 589856 | tf_op jit(solution)/shard_map/cond/branch_1_fun/ppermute | solution.py:271
  57.4 1.4 %collective-permute-start.77 = (bf16[384,640]{1,0:T(8,128)(2,1)S(1)}, bf16[384,640]{1,0:T(8,128)(2,1)S(1)}, u32[]{:S(2)}, u32[]{:S(2)}) collective-permute-start(bf16[384,640]{1,0:T(8,128)(2,1)S(1)} %collective-permute-done.75.refs_9_), channel_id=1, source_target_pairs={{0,8},{8,0},{16,24},{24,16},{1,9},{9,1},{17,25},{25,17},{2,10},{10... | collective-permute-start | bytes 1474568 | tf_op jit(solution)/shard_map/cond/branch_1_fun/ppermute | solution.py:271
  58.8 5.5 %collective-permute-start.79 = (bf16[256,384]{1,0:T(8,128)(2,1)S(1)}, bf16[256,384]{1,0:T(8,128)(2,1)S(1)}, u32[]{:S(2)}, u32[]{:S(2)}) collective-permute-start(bf16[256,384]{1,0:T(8,128)(2,1)S(1)} %collective-permute-done.67.refs_0_), channel_id=1, source_target_pairs={{0,2},{1,3},{2,0},{3,1},{4,6},{5,7},{6,4},{7,5},{8,10},{9,11},{10,... | collective-permute-start | bytes 589832 | tf_op jit(solution)/shard_map/cond/branch_1_fun/ppermute | solution.py:271
  64.3 7.5 %collective-permute-done.78.refs_1_ = bf16[512,384]{1,0:T(8,128)(2,1)S(1)} collective-permute-done((bf16[512,384]{1,0:T(8,128)(2,1)S(1)}, bf16[512,384]{1,0:T(8,128)(2,1)S(1)}, u32[]{:S(2)}, u32[]{:S(2)}) %collective-permute-start.78) | collective-permute-done | bytes 393248 | tf_op jit(solution)/shard_map/cond/branch_1_fun/ppermute | solution.py:271
  71.8 2.0 %collective-permute-done.79.refs_0_ = bf16[256,384]{1,0:T(8,128)(2,1)S(1)} collective-permute-done((bf16[256,384]{1,0:T(8,128)(2,1)S(1)}, bf16[256,384]{1,0:T(8,128)(2,1)S(1)}, u32[]{:S(2)}, u32[]{:S(2)}) %collective-permute-start.79) | collective-permute-done | bytes 196640 | tf_op jit(solution)/shard_map/cond/branch_1_fun/ppermute | solution.py:271
  73.8 6.7 %contract_near.7 = (f32[768,640]{1,0:T(8,128)S(1)}, bf16[4,384,640]{2,1,0:T(8,128)(2,1)S(1)}) custom-call(bf16[768,384]{1,0:T(8,128)(2,1)S(1)} %get-tuple-element.209.refs_0_, bf16[768,384]{1,0:T(8,128)(2,1)S(1)} %collective-permute-done.64.refs_1_, bf16[768,384]{1,0:T(8,128)(2,1)S(1)} %collective-permute-done.66.refs_2_, ...), custom_call_target="tpu_custom_call" | custom-call | flops 1509949440 | bytes 4325376 | tf_op jit(solution)/shard_map/cond/branch_1_fun/contract_near/pallas_call | solution.py:371
  81.9 3.5 %collective-permute-done.81.refs_1_ = bf16[512,384]{1,0:T(8,128)(2,1)S(1)} collective-permute-done((bf16[512,384]{1,0:T(8,128)(2,1)S(1)}, bf16[512,384]{1,0:T(8,128)(2,1)S(1)}, u32[]{:S(2)}, u32[]{:S(2)}) %collective-permute-start.81) | collective-permute-done | bytes 393248 | tf_op jit(solution)/shard_map/cond/branch_1_fun/ppermute | solution.py:271
  85.9 1.5 %collective-permute-done.82.refs_2_ = bf16[256,384]{1,0:T(8,128)(2,1)S(1)} collective-permute-done((bf16[256,384]{1,0:T(8,128)(2,1)S(1)}, bf16[256,384]{1,0:T(8,128)(2,1)S(1)}, u32[]{:S(2)}, u32[]{:S(2)}) %collective-permute-start.82) | collective-permute-done | bytes 196640 | tf_op jit(solution)/shard_map/cond/branch_1_fun/ppermute | solution.py:271
  87.3 3.4 %contract_last.7 = bf16[1024,768]{1,0:T(8,128)(2,1)S(1)} custom-call(f32[768,640]{1,0:T(8,128)S(1)} %contract_far.7.before, bf16[4,384,640]{2,1,0:T(8,128)(2,1)S(1)} %get-tuple-element.220.s_ref, bf16[1024,768]{1,0:T(8,128)(2,1)S(1)} %get-tuple-element.212.lam_hot, bf16[640,768]{1,0:T(8,128)(2,1)S(1)} %get-tuple-element.225.col_hot, ...), custom_call_target="tpu_custom_call" | custom-call | flops 754974720 | bytes 2162688 | tf_op jit(solution)/shard_map/cond/branch_1_fun/contract_last/pallas_call | solution.py:431
  (43 shorter events, 8.9 us)
Async XLA Ops:
  2.3 3.6 %copy-start.12 = (s32[128]{0:T(128)S(1)}, s32[128]{0:T(128)}, u32[]{:S(2)}) copy-start(s32[128]{0:T(128)} %get-tuple-element.198.count_ref) | copy-start | bytes 1540 | tf_op jit(solution)/shard_map/cond
  2.3 3.5 %copy-start.20 = (bf16[1024,512]{1,0:T(8,128)(2,1)S(1)}, bf16[1024,512]{1,0:T(8,128)(2,1)}, u32[]{:S(2)}) copy-start(bf16[1024,512]{1,0:T(8,128)(2,1)} %get-tuple-element.200.x_ref) | copy-start | bytes 3145732 | tf_op jit(solution)/shard_map/cond
  2.3 3.5 %copy-start.24 = (s32[32,16]{0,1:T(8,128)S(1)}, s32[32,16]{0,1:T(8,128)}, u32[]{:S(2)}) copy-start(s32[32,16]{0,1:T(8,128)} %get-tuple-element.199) | copy-start | bytes 6148 | tf_op jit(solution)/shard_map/cond
  5.3 3.4 %collective-permute-start.63 = (bf16[4,128,640]{2,1,0:T(8,128)(2,1)S(1)}, bf16[4,128,640]{2,1,0:T(8,128)(2,1)S(1)}, u32[]{:S(2)}, u32[]{:S(2)}) collective-permute-start(bf16[4,128,640]{2,1,0:T(8,128)(2,1)S(1)} %pack_other_core.7), channel_id=1, source_target_pairs={{0,1},{1,0},{2,3},{3,2},{4,5},{5,4},{6,7},{7,6},{8,9},{9,8},{10,11... | collective-permute-start | bytes 1966088 | tf_op jit(solution)/shard_map/cond/branch_1_fun/ppermute | solution.py:271
  8.5 11.4 %collective-permute-start.64 = (bf16[768,384]{1,0:T(8,128)(2,1)S(1)}, bf16[768,384]{1,0:T(8,128)(2,1)S(1)}, u32[]{:S(2)}, u32[]{:S(2)}) collective-permute-start(bf16[768,384]{1,0:T(8,128)(2,1)S(1)} %get-tuple-element.209.refs_0_), channel_id=1, source_target_pairs={{0,1},{1,0},{2,3},{3,2},{4,5},{5,4},{6,7},{7,6},{8,9},{9,8},{10,11... | collective-permute-start | bytes 1769480 | tf_op jit(solution)/shard_map/cond/branch_1_fun/ppermute | solution.py:271
  11.2 15.6 %collective-permute-start.65 = (bf16[224,640]{1,0:T(8,128)(2,1)S(1)}, bf16[224,640]{1,0:T(8,128)(2,1)S(1)}, u32[]{:S(2)}, u32[]{:S(2)}) collective-permute-start(bf16[224,640]{1,0:T(8,128)(2,1)S(1)} %get-tuple-element.208), channel_id=1, source_target_pairs={{0,2},{1,3},{2,0},{3,1},{4,6},{5,7},{6,4},{7,5},{8,10},{9,11},{10,... | collective-permute-start | bytes 860168 | tf_op jit(solution)/shard_map/cond/branch_1_fun/ppermute | solution.py:271
  14.3 27.2 %collective-permute-start.68 = (bf16[224,640]{1,0:T(8,128)(2,1)S(1)}, bf16[224,640]{1,0:T(8,128)(2,1)S(1)}, u32[]{:S(2)}, u32[]{:S(2)}) collective-permute-start(bf16[224,640]{1,0:T(8,128)(2,1)S(1)} %get-tuple-element.211), channel_id=1, source_target_pairs={{0,4},{1,5},{2,6},{3,7},{4,0},{5,1},{6,2},{7,3},{8,12},{9,13},{10,... | collective-permute-start | bytes 860168 | tf_op jit(solution)/shard_map/cond/branch_1_fun/ppermute | solution.py:271
  16.9 24.6 %collective-permute-start.69 = (bf16[224,640]{1,0:T(8,128)(2,1)S(1)}, bf16[224,640]{1,0:T(8,128)(2,1)S(1)}, u32[]{:S(2)}, u32[]{:S(2)}) collective-permute-start(bf16[224,640]{1,0:T(8,128)(2,1)S(1)} %get-tuple-element.214), channel_id=1, source_target_pairs={{0,6},{1,7},{2,4},{3,5},{4,2},{5,3},{6,0},{7,1},{8,14},{9,15},{10,... | collective-permute-start | bytes 860168 | tf_op jit(solution)/shard_map/cond/branch_1_fun/ppermute | solution.py:271
  16.9 33.9 %collective-permute-start.67 = (bf16[256,384]{1,0:T(8,128)(2,1)S(1)}, bf16[256,384]{1,0:T(8,128)(2,1)S(1)}, u32[]{:S(2)}, u32[]{:S(2)}) collective-permute-start(bf16[256,384]{1,0:T(8,128)(2,1)S(1)} %get-tuple-element.210), channel_id=1, source_target_pairs={{0,4},{1,5},{2,6},{3,7},{4,0},{5,1},{6,2},{7,3},{8,12},{9,13},{10,... | collective-permute-start | bytes 589832 | tf_op jit(solution)/shard_map/cond/branch_1_fun/ppermute | solution.py:271
  28.0 14.7 %collective-permute-start.70 = (bf16[384,640]{1,0:T(8,128)(2,1)S(1)}, bf16[384,640]{1,0:T(8,128)(2,1)S(1)}, u32[]{:S(2)}, u32[]{:S(2)}) collective-permute-start(bf16[384,640]{1,0:T(8,128)(2,1)S(1)} %pack_part.14.refs_4_), channel_id=1, source_target_pairs={{0,8},{8,0},{16,24},{24,16},{1,9},{9,1},{17,25},{25,17},{2,10},{10... | collective-permute-start | bytes 1474568 | tf_op jit(solution)/shard_map/cond/branch_1_fun/ppermute | solution.py:271
  29.7 12.9 %collective-permute-start.71 = (bf16[384,640]{1,0:T(8,128)(2,1)S(1)}, bf16[384,640]{1,0:T(8,128)(2,1)S(1)}, u32[]{:S(2)}, u32[]{:S(2)}) collective-permute-start(bf16[384,640]{1,0:T(8,128)(2,1)S(1)} %pack_part.14.refs_4_), channel_id=1, source_target_pairs={{0,16},{8,24},{16,0},{24,8},{1,17},{9,25},{17,1},{25,9},{2,18},{10... | collective-permute-start | bytes 1474568 | tf_op jit(solution)/shard_map/cond/branch_1_fun/ppermute | solution.py:271
  41.5 15.2 %collective-permute-start.66 = (bf16[768,384]{1,0:T(8,128)(2,1)S(1)}, bf16[768,384]{1,0:T(8,128)(2,1)S(1)}, u32[]{:S(2)}, u32[]{:S(2)}) collective-permute-start(bf16[768,384]{1,0:T(8,128)(2,1)S(1)} %get-tuple-element.209.refs_0_), channel_id=1, source_target_pairs={{0,2},{1,3},{2,0},{3,1},{4,6},{5,7},{6,4},{7,5},{8,10},{9,11},{10,... | collective-permute-start | bytes 1769480 | tf_op jit(solution)/shard_map/cond/branch_1_fun/ppermute | solution.py:271
  42.7 14.1 %collective-permute-start.74 = (bf16[384,640]{1,0:T(8,128)(2,1)S(1)}, bf16[384,640]{1,0:T(8,128)(2,1)S(1)}, u32[]{:S(2)}, u32[]{:S(2)}) collective-permute-start(bf16[384,640]{1,0:T(8,128)(2,1)S(1)} %pack_part.15.refs_5_), channel_id=1, source_target_pairs={{0,8},{8,0},{16,24},{24,16},{1,9},{9,1},{17,25},{25,17},{2,10},{10... | collective-permute-start | bytes 1474568 | tf_op jit(solution)/shard_map/cond/branch_1_fun/ppermute | solution.py:271
  44.2 12.5 %collective-permute-start.75 = (bf16[384,640]{1,0:T(8,128)(2,1)S(1)}, bf16[384,640]{1,0:T(8,128)(2,1)S(1)}, u32[]{:S(2)}, u32[]{:S(2)}) collective-permute-start(bf16[384,640]{1,0:T(8,128)(2,1)S(1)} %pack_part.15.refs_5_), channel_id=1, source_target_pairs={{0,16},{8,24},{16,0},{24,8},{1,17},{9,25},{17,1},{25,9},{2,18},{10... | collective-permute-start | bytes 1474568 | tf_op jit(solution)/shard_map/cond/branch_1_fun/ppermute | solution.py:271
  50.8 5.9 %collective-permute-start.72 = (bf16[256,384]{1,0:T(8,128)(2,1)S(1)}, bf16[256,384]{1,0:T(8,128)(2,1)S(1)}, u32[]{:S(2)}, u32[]{:S(2)}) collective-permute-start(bf16[256,384]{1,0:T(8,128)(2,1)S(1)} %collective-permute-done.67.refs_0_), channel_id=1, source_target_pairs={{0,1},{1,0},{2,3},{3,2},{4,5},{5,4},{6,7},{7,6},{8,9},{9,8},{10,11... | collective-permute-start | bytes 589832 | tf_op jit(solution)/shard_map/cond/branch_1_fun/ppermute | solution.py:271
  50.8 21.0 %collective-permute-start.78 = (bf16[512,384]{1,0:T(8,128)(2,1)S(1)}, bf16[512,384]{1,0:T(8,128)(2,1)S(1)}, u32[]{:S(2)}, u32[]{:S(2)}) collective-permute-start(bf16[512,384]{1,0:T(8,128)(2,1)S(1)} %get-tuple-element.222), channel_id=1, source_target_pairs={{0,4},{1,5},{2,6},{3,7},{4,0},{5,1},{6,2},{7,3},{8,12},{9,13},{10,... | collective-permute-start | bytes 1179656 | tf_op jit(solution)/shard_map/cond/branch_1_fun/ppermute | solution.py:271
  56.7 17.1 %collective-permute-start.73 = (bf16[768,384]{1,0:T(8,128)(2,1)S(1)}, bf16[768,384]{1,0:T(8,128)(2,1)S(1)}, u32[]{:S(2)}, u32[]{:S(2)}) collective-permute-start(bf16[768,384]{1,0:T(8,128)(2,1)S(1)} %collective-permute-done.66.refs_2_), channel_id=1, source_target_pairs={{0,1},{1,0},{2,3},{3,2},{4,5},{5,4},{6,7},{7,6},{8,9},{9,8},{10,11... | collective-permute-start | bytes 1769480 | tf_op jit(solution)/shard_map/cond/branch_1_fun/ppermute | solution.py:271
  56.8 17.1 %collective-permute-start.76 = (bf16[384,640]{1,0:T(8,128)(2,1)S(1)}, bf16[384,640]{1,0:T(8,128)(2,1)S(1)}, u32[]{:S(2)}, u32[]{:S(2)}) collective-permute-start(bf16[384,640]{1,0:T(8,128)(2,1)S(1)} %collective-permute-done.70.refs_6_), channel_id=1, source_target_pairs={{0,16},{8,24},{16,0},{24,8},{1,17},{9,25},{17,1},{25,9},{2,18},{10... | collective-permute-start | bytes 1474568 | tf_op jit(solution)/shard_map/cond/branch_1_fun/ppermute | solution.py:271
  57.4 16.5 %collective-permute-start.77 = (bf16[384,640]{1,0:T(8,128)(2,1)S(1)}, bf16[384,640]{1,0:T(8,128)(2,1)S(1)}, u32[]{:S(2)}, u32[]{:S(2)}) collective-permute-start(bf16[384,640]{1,0:T(8,128)(2,1)S(1)} %collective-permute-done.75.refs_9_), channel_id=1, source_target_pairs={{0,8},{8,0},{16,24},{24,16},{1,9},{9,1},{17,25},{25,17},{2,10},{10... | collective-permute-start | bytes 1474568 | tf_op jit(solution)/shard_map/cond/branch_1_fun/ppermute | solution.py:271
  58.8 15.0 %collective-permute-start.79 = (bf16[256,384]{1,0:T(8,128)(2,1)S(1)}, bf16[256,384]{1,0:T(8,128)(2,1)S(1)}, u32[]{:S(2)}, u32[]{:S(2)}) collective-permute-start(bf16[256,384]{1,0:T(8,128)(2,1)S(1)} %collective-permute-done.67.refs_0_), channel_id=1, source_target_pairs={{0,2},{1,3},{2,0},{3,1},{4,6},{5,7},{6,4},{7,5},{8,10},{9,11},{10,... | collective-permute-start | bytes 589832 | tf_op jit(solution)/shard_map/cond/branch_1_fun/ppermute | solution.py:271
  73.8 6.7 %collective-permute-start.80 = (bf16[512,384]{1,0:T(8,128)(2,1)S(1)}, bf16[512,384]{1,0:T(8,128)(2,1)S(1)}, u32[]{:S(2)}, u32[]{:S(2)}) collective-permute-start(bf16[512,384]{1,0:T(8,128)(2,1)S(1)} %collective-permute-done.78.refs_1_), channel_id=1, source_target_pairs={{0,1},{1,0},{2,3},{3,2},{4,5},{5,4},{6,7},{7,6},{8,9},{9,8},{10,11... | collective-permute-start | bytes 1179656 | tf_op jit(solution)/shard_map/cond/branch_1_fun/ppermute | solution.py:271
  73.8 11.5 %collective-permute-start.81 = (bf16[512,384]{1,0:T(8,128)(2,1)S(1)}, bf16[512,384]{1,0:T(8,128)(2,1)S(1)}, u32[]{:S(2)}, u32[]{:S(2)}) collective-permute-start(bf16[512,384]{1,0:T(8,128)(2,1)S(1)} %collective-permute-done.78.refs_1_), channel_id=1, source_target_pairs={{0,2},{1,3},{2,0},{3,1},{4,6},{5,7},{6,4},{7,5},{8,10},{9,11},{10,... | collective-permute-start | bytes 1179656 | tf_op jit(solution)/shard_map/cond/branch_1_fun/ppermute | solution.py:271
  85.3 2.0 %collective-permute-start.83 = (bf16[512,384]{1,0:T(8,128)(2,1)S(1)}, bf16[512,384]{1,0:T(8,128)(2,1)S(1)}, u32[]{:S(2)}, u32[]{:S(2)}) collective-permute-start(bf16[512,384]{1,0:T(8,128)(2,1)S(1)} %collective-permute-done.81.refs_1_), channel_id=1, source_target_pairs={{0,1},{1,0},{2,3},{3,2},{4,5},{5,4},{6,7},{7,6},{8,9},{9,8},{10,11... | collective-permute-start | bytes 1179656 | tf_op jit(solution)/shard_map/cond/branch_1_fun/ppermute | solution.py:271
  85.3 2.0 %collective-permute-start.82 = (bf16[256,384]{1,0:T(8,128)(2,1)S(1)}, bf16[256,384]{1,0:T(8,128)(2,1)S(1)}, u32[]{:S(2)}, u32[]{:S(2)}) collective-permute-start(bf16[256,384]{1,0:T(8,128)(2,1)S(1)} %collective-permute-done.79.refs_0_), channel_id=1, source_target_pairs={{0,1},{1,0},{2,3},{3,2},{4,5},{5,4},{6,7},{7,6},{8,9},{9,8},{10,11... | collective-permute-start | bytes 589832 | tf_op jit(solution)/shard_map/cond/branch_1_fun/ppermute | solution.py:271
  (4 other events, 11.3 us)
